TPU v7x, 32 devices: a whole 2x2x4 slice. The times are simulated.
32 devices in a mesh: dp: 4 (over y, x), tensor: 8 (over z, core).
Axes of the slice: x: 2, y: 2, z: 4, core: 2. Of those that a mesh axis runs over, the one named last changes fastest.
Arguments:
- inputs: bfloat16 [8192, 2048], P(('dp', 'tensor')), may hold values from -6 to 6
- cotangent: bfloat16 [8192, 2048], P(('dp', 'tensor')), may hold values from -6 to 6
- lengths: int32 [4], P('dp'), may hold values from 1024 to 2048, as said below
- positions: int32 [8192], P('dp'), may hold values from 0 to 4094, as said below
- qkv_master: float32 [3, 2048, 2048], P(None, 'dp', 'tensor'), may hold values from -0.125 to 0.125
- gate_up_master: float32 [2, 2048, 5632], P(None, 'dp', 'tensor'), may hold values from -0.125 to 0.125
- out_master: float32 [2048, 2048], P('tensor', 'dp'), may hold values from -1 to 1
- down_master: float32 [5632, 2048], P('tensor', 'dp'), may hold values from -0.25 to 0.25
- bias_master: float32 [3, 32, 64], P(None, 'tensor', 'dp'), may hold values from -3 to 3
- norm_master: float32 [4, 2048], replicated
- qkv_first: float32 [3, 2048, 2048], P(None, 'dp', 'tensor'), may hold values from -48 to 48
- gate_up_first: float32 [2, 2048, 5632], P(None, 'dp', 'tensor'), may hold values from -64 to 64
- out_first: float32 [2048, 2048], P('tensor', 'dp'), may hold values from -20 to 20
- down_first: float32 [5632, 2048], P('tensor', 'dp'), may hold values from -20 to 20
- bias_first: float32 [3, 32, 64], P(None, 'tensor', 'dp'), may hold values from -96 to 96
- norm_first: float32 [4, 2048], replicated, may hold values from -48 to 48
- qkv_second: float32 [3, 2048, 2048], P(None, 'dp', 'tensor'), may hold values from 131.072 to 2048
- gate_up_second: float32 [2, 2048, 5632], P(None, 'dp', 'tensor'), may hold values from 221.184 to 3686.4
- out_second: float32 [2048, 2048], P('tensor', 'dp'), may hold values from 24.576 to 409.6
- down_second: float32 [5632, 2048], P('tensor', 'dp'), may hold values from 24.576 to 409.6
- bias_second: float32 [3, 32, 64], P(None, 'tensor', 'dp'), may hold values from 491.52 to 8192
- norm_second: float32 [4, 2048], replicated, may hold values from 131.072 to 2048
Outputs:
- block_output: bfloat16 [8192, 2048], P(('dp', 'tensor'))
- input_grad: float32 [8192, 2048], P(('dp', 'tensor'))
- qkv_new: float32 [3, 2048, 2048], P(None, 'dp', 'tensor')
- qkv_first_new: float32 [3, 2048, 2048], P(None, 'dp', 'tensor')
- qkv_second_new: float32 [3, 2048, 2048], P(None, 'dp', 'tensor')
- gate_up_new: float32 [2, 2048, 5632], P(None, 'dp', 'tensor')
- gate_up_first_new: float32 [2, 2048, 5632], P(None, 'dp', 'tensor')
- gate_up_second_new: float32 [2, 2048, 5632], P(None, 'dp', 'tensor')
- out_new: float32 [2048, 2048], P('tensor', 'dp')
- out_first_new: float32 [2048, 2048], P('tensor', 'dp')
- out_second_new: float32 [2048, 2048], P('tensor', 'dp')
- down_new: float32 [5632, 2048], P('tensor', 'dp')
- down_first_new: float32 [5632, 2048], P('tensor', 'dp')
- down_second_new: float32 [5632, 2048], P('tensor', 'dp')
- bias_new: float32 [3, 32, 64], P(None, 'tensor', 'dp')
- bias_first_new: float32 [3, 32, 64], P(None, 'tensor', 'dp')
- bias_second_new: float32 [3, 32, 64], P(None, 'tensor', 'dp')
- norm_new: float32 [4, 2048], replicated
- norm_first_new: float32 [4, 2048], replicated
- norm_second_new: float32 [4, 2048], replicated
Inputs may be any that keep to these rules, and one draw needn't show every extreme that they name: `lengths`: each row holds one sequence in its first slots and padding after it; some row has exactly 2048 tokens. `positions`: 0 at the first slot of every row and rising by 1 or 2 from slot to slot within a row; the first row rises by 2 at every slot.
All inputs are finite; a program needn't handle non-finite values.
Results may differ from a plain program's by a relative error of at most 0.012.
Values may be sent and summed in bfloat16 or wider, within the bound.
A program may use at most 256 MiB of HBM per device.

v0:
```python
import math

import jax
import jax.numpy as jnp
from jax import lax
from jax.sharding import PartitionSpec as P

D = 2048
HEADS = 32
HEAD_DIM = 64
ROTARY = 16
FF = 5632


norm_eps = 1e-05
beta_one = 0.9
beta_two = 0.95
adam_eps = 1e-08
adam_steps = 10
decay_rate = 0.1
rope_base = 10000.0
score_scale = 0.125
mask_fill = -1e30


def norm_forward(values, gain_row, shift_row):
    average = jnp.mean(values, axis=-1, keepdims=True)
    centred = values - average
    spread = jnp.mean(centred * centred, axis=-1, keepdims=True)
    return centred * lax.rsqrt(spread + norm_eps) * gain_row + shift_row


def norm_backward(values, gain_row, grad_rows):
    average = jnp.mean(values, axis=-1, keepdims=True)
    centred = values - average
    spread = jnp.mean(centred * centred, axis=-1, keepdims=True)
    inverse = lax.rsqrt(spread + norm_eps)
    normal = centred * inverse
    grad_normal = grad_rows * gain_row
    grad_values = inverse * (
        grad_normal
        - jnp.mean(grad_normal, axis=-1, keepdims=True)
        - normal * jnp.mean(grad_normal * normal, axis=-1, keepdims=True)
    )
    return (grad_values, jnp.sum(grad_rows * normal, axis=0), jnp.sum(grad_rows, axis=0))


def rotate(values, cosine, sine_part):
    half_rot = ROTARY // 2
    first_half = values[..., :half_rot]
    second_half = values[..., half_rot:ROTARY]
    cosine_wide = cosine[:, None, :]
    sine_wide = sine_part[:, None, :]
    return jnp.concatenate(
        [
            first_half * cosine_wide - second_half * sine_wide,
            second_half * cosine_wide + first_half * sine_wide,
            values[..., ROTARY:],
        ],
        axis=-1,
    )


def swiglu(gate_part, up_part):
    return jax.nn.silu(gate_part) * up_part


def adamw(weight_old, first_old, second_old, gradient, step_rate, decay_part):
    first_new = beta_one * first_old + (1.0 - beta_one) * gradient
    second_new = beta_two * second_old + (1.0 - beta_two) * gradient * gradient
    correct_one = 1.0 - beta_one**adam_steps
    correct_two = 1.0 - beta_two**adam_steps
    update = first_new / correct_one / (jnp.sqrt(second_new / correct_two) + adam_eps)
    return (weight_old - step_rate * (update + decay_part * weight_old), first_new, second_new)


def block_mask(first_slot, block_rows, row_length, row_size):
    query_slots = first_slot + jnp.arange(block_rows)
    key_slots = jnp.arange(row_length)
    return (key_slots[None, :] <= query_slots[:, None]) & (key_slots[None, :] < row_size)


def row_forward(queries, key_rows, value_rows, row_size, block_rows):
    row_length = key_rows.shape[0]
    block_count = row_length // block_rows
    heads_here = key_rows.shape[1]

    def one_block(block_pack):
        query_block, first_slot = block_pack
        allowed = block_mask(first_slot, block_rows, row_length, row_size)
        scores = (
            jnp.einsum("qhd,khd->hqk", query_block, key_rows, preferred_element_type=jnp.float32)
            * score_scale
        )
        masked = jnp.where(allowed[None], scores, mask_fill)
        highest = jnp.max(masked, axis=2, keepdims=True)
        weights = jnp.exp(masked - highest)
        row_total = jnp.sum(weights, axis=2, keepdims=True)
        weights_low = (weights / row_total).astype(jnp.bfloat16)
        mixed_block = jnp.einsum(
            "hqk,khd->qhd", weights_low, value_rows, preferred_element_type=jnp.float32
        )
        return (mixed_block.astype(jnp.bfloat16), (highest + jnp.log(row_total))[:, :, 0])

    starts = jnp.arange(block_count, dtype=jnp.int32) * block_rows
    return lax.map(
        one_block, (queries.reshape(block_count, block_rows, heads_here, HEAD_DIM), starts)
    )


def row_backward(queries, key_rows, value_rows, grad_mixed, log_totals, row_size, block_rows):
    row_length = key_rows.shape[0]
    block_count = row_length // block_rows
    heads_here = key_rows.shape[1]

    def one_block(carry, block_pack):
        grad_keys, grad_values = carry
        query_block, grad_block, log_block, first_slot = block_pack
        allowed = block_mask(first_slot, block_rows, row_length, row_size)
        scores = (
            jnp.einsum("qhd,khd->hqk", query_block, key_rows, preferred_element_type=jnp.float32)
            * score_scale
        )
        masked = jnp.where(allowed[None], scores, mask_fill)
        weights = jnp.exp(masked - log_block[:, :, None])
        weights_low = weights.astype(jnp.bfloat16)
        grad_values = grad_values + jnp.einsum(
            "hqk,qhd->khd", weights_low, grad_block, preferred_element_type=jnp.float32
        )
        grad_weights = jnp.einsum(
            "qhd,khd->hqk", grad_block, value_rows, preferred_element_type=jnp.float32
        )
        centre = jnp.sum(weights * grad_weights, axis=2, keepdims=True)
        grad_scores = (weights * (grad_weights - centre)).astype(jnp.bfloat16)
        grad_query = (
            jnp.einsum("hqk,khd->qhd", grad_scores, key_rows, preferred_element_type=jnp.float32)
            * score_scale
        )
        grad_keys = (
            grad_keys
            + jnp.einsum(
                "hqk,qhd->khd", grad_scores, query_block, preferred_element_type=jnp.float32
            )
            * score_scale
        )
        return ((grad_keys, grad_values), grad_query)

    starts = jnp.arange(block_count, dtype=jnp.int32) * block_rows
    zeros = jnp.zeros(key_rows.shape, jnp.float32)
    block_shape = (block_count, block_rows, heads_here, HEAD_DIM)
    (grad_keys, grad_values), grad_queries = lax.scan(
        one_block,
        (zeros, zeros),
        (queries.reshape(block_shape), grad_mixed.reshape(block_shape), log_totals, starts),
    )
    return (grad_queries.reshape(row_length, heads_here, HEAD_DIM), grad_keys, grad_values)


def local(
    inputs,
    cotangent,
    lengths,
    positions,
    qkv_master,
    gate_up_master,
    out_master,
    down_master,
    bias_master,
    norm_master,
    qkv_first,
    gate_up_first,
    out_first,
    down_first,
    bias_first,
    norm_first,
    qkv_second,
    gate_up_second,
    out_second,
    down_second,
    bias_second,
    norm_second,
):
    tensor_count = lax.axis_size("tensor")
    local_tokens = inputs.shape[0]
    group_tokens = local_tokens * tensor_count
    row_count = lengths.shape[0]
    row_length = group_tokens // row_count
    block_rows = min(512, row_length)
    heads_here = bias_master.shape[1]
    width_here = heads_here * HEAD_DIM
    own_start = lax.axis_index("tensor") * local_tokens
    qkv_copy, gate_up_copy, out_copy, down_copy, bias_copy = (
        lax.all_gather(qkv_master.astype(jnp.bfloat16), "dp", axis=1, tiled=True),
        lax.all_gather(gate_up_master.astype(jnp.bfloat16), "dp", axis=1, tiled=True),
        lax.all_gather(out_master.astype(jnp.bfloat16), "dp", axis=1, tiled=True),
        lax.all_gather(down_master.astype(jnp.bfloat16), "dp", axis=1, tiled=True),
        lax.all_gather(bias_master.astype(jnp.bfloat16), "dp", axis=2, tiled=True),
    )
    qkv_flat = jnp.transpose(qkv_copy, (1, 0, 2)).reshape(qkv_copy.shape[1], 3 * width_here)
    inputs_wide = inputs.astype(jnp.float32)
    normed_one = norm_forward(inputs_wide, norm_master[0], norm_master[1]).astype(jnp.bfloat16)
    gathered_one = lax.all_gather(normed_one, "tensor", axis=0, tiled=True)
    projected = jnp.dot(
        gathered_one, qkv_flat, preferred_element_type=jnp.float32
    ) + bias_copy.reshape(1, 3 * width_here).astype(jnp.float32)
    frequency = rope_base ** (-(2.0 * jnp.arange(ROTARY // 2, dtype=jnp.float32)) / ROTARY)
    angles = positions.astype(jnp.float32)[:, None] * frequency[None, :]
    cosine = jnp.cos(angles)
    sine_part = jnp.sin(angles)
    head_shape = (group_tokens, heads_here, HEAD_DIM)
    queries_low = rotate(projected[:, :width_here].reshape(head_shape), cosine, sine_part).astype(
        jnp.bfloat16
    )
    keys_low = rotate(
        projected[:, width_here : 2 * width_here].reshape(head_shape), cosine, sine_part
    ).astype(jnp.bfloat16)
    values_low = projected[:, 2 * width_here :].astype(jnp.bfloat16).reshape(head_shape)
    rows_shape = (row_count, row_length, heads_here, HEAD_DIM)

    def forward_row(row_pack):
        row_queries, row_keys, row_values, row_size = row_pack
        return row_forward(row_queries, row_keys, row_values, row_size, block_rows)

    attended, log_totals = lax.map(
        forward_row,
        (
            queries_low.reshape(rows_shape),
            keys_low.reshape(rows_shape),
            values_low.reshape(rows_shape),
            lengths,
        ),
    )
    mixed_low = attended.reshape(group_tokens, width_here)
    rows_part = mixed_low
    branch_one = lax.psum_scatter(
        jnp.dot(rows_part, out_copy, preferred_element_type=jnp.float32),
        "tensor",
        scatter_dimension=0,
        tiled=True,
    )
    middle = inputs_wide + branch_one
    normed_two = norm_forward(middle, norm_master[2], norm_master[3]).astype(jnp.bfloat16)
    gathered_two = lax.all_gather(normed_two, "tensor", axis=0, tiled=True)
    gate_up = jnp.einsum(
        "td,cdf->ctf", gathered_two, gate_up_copy, preferred_element_type=jnp.float32
    )
    hidden_wide, swiglu_pull = jax.vjp(swiglu, gate_up[0], gate_up[1])
    hidden = hidden_wide.astype(jnp.bfloat16)
    rows_part = hidden
    branch_two = lax.psum_scatter(
        jnp.dot(rows_part, down_copy, preferred_element_type=jnp.float32),
        "tensor",
        scatter_dimension=0,
        tiled=True,
    )
    block_output = (middle + branch_two).astype(jnp.bfloat16)
    group_index = own_start + jnp.arange(local_tokens, dtype=jnp.int32)
    row_of = group_index // row_length
    slot_of = group_index % row_length
    row_match = row_of[:, None] == jnp.arange(row_count, dtype=jnp.int32)[None, :]
    length_of = jnp.sum(jnp.where(row_match, lengths[None, :], 0), axis=1)
    valid = (slot_of < length_of).astype(jnp.float32)
    grad_result = cotangent.astype(jnp.float32) * valid[:, None]
    gathered_grad = lax.all_gather(grad_result.astype(jnp.bfloat16), "tensor", axis=0, tiled=True)
    grad_down = jnp.einsum("tf,td->fd", hidden, gathered_grad, preferred_element_type=jnp.float32)
    grad_hidden = jnp.einsum(
        "td,fd->tf", gathered_grad, down_copy, preferred_element_type=jnp.float32
    )
    grad_gate, grad_up = swiglu_pull(grad_hidden)
    grad_gate_up = jnp.stack([grad_gate, grad_up]).astype(jnp.bfloat16)
    grad_gate_up_w = jnp.einsum(
        "td,ctf->cdf", gathered_two, grad_gate_up, preferred_element_type=jnp.float32
    )
    rows_part = grad_gate_up
    grad_normed_two = lax.psum_scatter(
        jnp.einsum("ctf,cdf->td", rows_part, gate_up_copy, preferred_element_type=jnp.float32),
        "tensor",
        scatter_dimension=0,
        tiled=True,
    )
    grad_middle_norm, gain_two, shift_two = norm_backward(middle, norm_master[2], grad_normed_two)
    grad_middle = grad_result + grad_middle_norm
    gathered_mid = lax.all_gather(grad_middle.astype(jnp.bfloat16), "tensor", axis=0, tiled=True)
    grad_out_w = jnp.einsum(
        "tw,td->wd", mixed_low, gathered_mid, preferred_element_type=jnp.float32
    )
    grad_mixed = jnp.einsum(
        "td,wd->tw", gathered_mid, out_copy, preferred_element_type=jnp.float32
    ).astype(jnp.bfloat16)

    def backward_row(row_pack):
        row_queries, row_keys, row_values, row_grad, row_logs, row_size = row_pack
        return row_backward(
            row_queries, row_keys, row_values, row_grad, row_logs, row_size, block_rows
        )

    grad_queries, grad_keys, grad_values = lax.map(
        backward_row,
        (
            queries_low.reshape(rows_shape),
            keys_low.reshape(rows_shape),
            values_low.reshape(rows_shape),
            grad_mixed.reshape(rows_shape),
            log_totals,
            lengths,
        ),
    )
    grad_query_pre = rotate(grad_queries.reshape(head_shape), cosine, -sine_part)
    grad_key_pre = rotate(grad_keys.reshape(head_shape), cosine, -sine_part)
    grad_projected = jnp.concatenate(
        [
            grad_query_pre.reshape(group_tokens, width_here).astype(jnp.bfloat16),
            grad_key_pre.reshape(group_tokens, width_here).astype(jnp.bfloat16),
            grad_values.reshape(group_tokens, width_here).astype(jnp.bfloat16),
        ],
        axis=1,
    )
    grad_bias = jnp.sum(grad_projected, axis=0, dtype=jnp.float32).reshape(3, heads_here, HEAD_DIM)
    grad_qkv_w = jnp.einsum(
        "td,tcw->cdw",
        gathered_one,
        grad_projected.reshape(group_tokens, 3, width_here),
        preferred_element_type=jnp.float32,
    )
    rows_part = grad_projected
    grad_normed_one = lax.psum_scatter(
        jnp.einsum("tc,dc->td", rows_part, qkv_flat, preferred_element_type=jnp.float32),
        "tensor",
        scatter_dimension=0,
        tiled=True,
    )
    grad_input_norm, gain_one, shift_one = norm_backward(
        inputs_wide, norm_master[0], grad_normed_one
    )
    input_grad = grad_middle + grad_input_norm
    norm_grads = lax.psum(jnp.stack([gain_one, shift_one, gain_two, shift_two]), ("dp", "tensor"))
    qkv_grad, gate_up_grad, out_grad, down_grad, bias_grad = (
        lax.psum_scatter(grad_qkv_w, "dp", scatter_dimension=1, tiled=True),
        lax.psum_scatter(grad_gate_up_w, "dp", scatter_dimension=1, tiled=True),
        lax.psum_scatter(grad_out_w, "dp", scatter_dimension=1, tiled=True),
        lax.psum_scatter(grad_down, "dp", scatter_dimension=1, tiled=True),
        lax.psum_scatter(grad_bias, "dp", scatter_dimension=2, tiled=True),
    )
    qkv_new = adamw(qkv_master, qkv_first, qkv_second, qkv_grad, 2.0 / math.sqrt(D), decay_rate)
    gate_up_new = adamw(
        gate_up_master, gate_up_first, gate_up_second, gate_up_grad, 2.0 / math.sqrt(D), decay_rate
    )
    out_new = adamw(
        out_master, out_first, out_second, out_grad, 16.0 / math.sqrt(HEADS * HEAD_DIM), decay_rate
    )
    down_new = adamw(
        down_master, down_first, down_second, down_grad, 6.0 / math.sqrt(FF), decay_rate
    )
    bias_new = adamw(bias_master, bias_first, bias_second, bias_grad, 1.5, 0.0)
    norm_new = adamw(norm_master, norm_first, norm_second, norm_grads, 0.7, 0.0)
    return (
        block_output,
        input_grad,
        qkv_new[0],
        qkv_new[1],
        qkv_new[2],
        gate_up_new[0],
        gate_up_new[1],
        gate_up_new[2],
        out_new[0],
        out_new[1],
        out_new[2],
        down_new[0],
        down_new[1],
        down_new[2],
        bias_new[0],
        bias_new[1],
        bias_new[2],
        norm_new[0],
        norm_new[1],
        norm_new[2],
    )


def solution(mesh):
    return jax.shard_map(
        local,
        mesh=mesh,
        in_specs=(
            P(("dp", "tensor"), None),
            P(("dp", "tensor"), None),
            P("dp"),
            P("dp"),
            P(None, "dp", "tensor"),
            P(None, "dp", "tensor"),
            P("tensor", "dp"),
            P("tensor", "dp"),
            P(None, "tensor", "dp"),
            P(),
            P(None, "dp", "tensor"),
            P(None, "dp", "tensor"),
            P("tensor", "dp"),
            P("tensor", "dp"),
            P(None, "tensor", "dp"),
            P(),
            P(None, "dp", "tensor"),
            P(None, "dp", "tensor"),
            P("tensor", "dp"),
            P("tensor", "dp"),
            P(None, "tensor", "dp"),
            P(),
        ),
        out_specs=(
            P(("dp", "tensor"), None),
            P(("dp", "tensor"), None),
            P(None, "dp", "tensor"),
            P(None, "dp", "tensor"),
            P(None, "dp", "tensor"),
            P(None, "dp", "tensor"),
            P(None, "dp", "tensor"),
            P(None, "dp", "tensor"),
            P("tensor", "dp"),
            P("tensor", "dp"),
            P("tensor", "dp"),
            P("tensor", "dp"),
            P("tensor", "dp"),
            P("tensor", "dp"),
            P(None, "tensor", "dp"),
            P(None, "tensor", "dp"),
            P(None, "tensor", "dp"),
            P(),
            P(),
            P(),
        ),
        check_vma=False,
    )
```

profile of v0, /device:TPU:0, one launch (start us, length us, event | category | flops | bytes accessed | tf_op | source)
XLA Modules:
  0.0 1701.7 jit_solution(3761189605271463330)
XLA Ops:
  14.9 9.8 all_gather.29
  25.8 31.4 %all-gather.11.cloned.1.call-done = bf16[3,2048,256]{1,2,0:T(8,128)(2,1)} async-done(((bf16[3,512,256]{1,2,0:T(8,128)(2,1)}), bf16[3,2048,256]{1,2,0:T(8,128)(2,1)}) %all-gather.11.cloned.1.call-update) | async-done | bytes 3145744 | tf_op jit(solution)/shard_map/all_gather | solution.py:193
  57.2 84.3 %all-gather.9.cloned.1.call-done = bf16[2048,2048]{1,0:T(8,128)(2,1)} async-done(((bf16[256,2048]{1,0:T(8,128)(2,1)}), bf16[2048,2048]{1,0:T(8,128)(2,1)}) %all-gather.9.cloned.1.call-update) | async-done | bytes 8388624 | tf_op jit(solution)/shard_map/all_gather | solution.py:202
  141.5 10.1 broadcast_add_fusion
  152.6 67.3 %while.47 = (s32[]{:T(128)}, bf16[4,512,4,64]{1,3,2,0:T(8,128)(2,1)}, f32[4,4,512]{2,1,0:T(4,128)}, s32[4]{0:T(128)S(1)}, s32[]{:T(128)}, /*index=5*/bf16[4,512,...) while((s32[]{:T(128)}, ...), condition=%wide.region_5.6_spmd, body=%wide.region_2.5_spmd.sunk | while | flops 1126302208 | bytes 57221252 | solution.py:106
  158.5 4.3 fusion.158
  162.8 5.9 fusion.159
  175.2 4.3 fusion.158
  179.5 5.9 fusion.159
  191.9 4.3 fusion.158
  196.3 5.9 fusion.159
  208.7 4.3 fusion.158
  213.0 5.9 fusion.159
  224.0 9.7 fusion.106
  237.1 163.6 %reduce-scatter.10.cloned.1.call-done = f32[256,2048]{1,0:T(8,128)} async-done(((f32[2048,2048]{1,0:T(8,128)}), f32[256,2048]{1,0:T(8,128)}) %reduce-scatter.10.cloned.1.call-update) | async-done | bytes 2097168 | tf_op jit(solution)/shard_map/reduce_scatter | solution.py:235
  409.4 57.6 %all-gather.17.cloned.1.call-done = bf16[2,2048,704]{1,2,0:T(8,128)(2,1)} async-done(((bf16[2,512,704]{1,2,0:T(8,128)(2,1)}), bf16[2,2048,704]{1,2,0:T(8,128)(2,1)}) %all-gather.17.cloned.1.call-update) | async-done | bytes 5767184 | tf_op jit(solution)/shard_map/all_gather | solution.py:194
  467.0 84.1 %all-gather.15.cloned.1.call-done = bf16[2048,2048]{1,0:T(8,128)(2,1)} async-done(((bf16[256,2048]{1,0:T(8,128)(2,1)}), bf16[2048,2048]{1,0:T(8,128)(2,1)}) %all-gather.15.cloned.1.call-update) | async-done | bytes 8388624 | tf_op jit(solution)/shard_map/all_gather | solution.py:243
  551.1 18.7 %fusion.53 = f32[2,2048,704]{1,2,0:T(8,128)} fusion(bf16[2,2048,704]{1,2,0:T(8,128)(2,1)} %all-gather.17.cloned.1.call-done, bf16[2048,2048]{1,0:T(8,128)(2,1)} %all-gather.15.cloned.1.call-done), kind=kOutput, calls=%fused_computation.73 | convolution fusion | flops 11811160064 | bytes 25690112 | tf_op jit(solution)/shard_map/td,cdf->ctf/dot_general | solution.py:244
  569.8 23.9 %all-gather.19.cloned.1.call-done = bf16[704,2048]{1,0:T(8,128)(2,1)} async-done(((bf16[704,512]{1,0:T(8,128)(2,1)}), bf16[704,2048]{1,0:T(8,128)(2,1)}) %all-gather.19.cloned.1.call-update) | async-done | bytes 2883600 | tf_op jit(solution)/shard_map/all_gather | solution.py:196
  593.7 84.3 %all-gather.21.cloned.1.call-done = bf16[2048,2048]{1,0:T(8,128)(2,1)} async-done(((bf16[256,2048]{1,0:T(8,128)(2,1)}), bf16[2048,2048]{1,0:T(8,128)(2,1)}) %all-gather.21.cloned.1.call-update) | async-done | bytes 8388624 | tf_op jit(solution)/shard_map/all_gather | solution.py:264
  678.0 15.1 fusion.69
  695.7 16.4 convolution_bitcast_fusion
  712.3 12.4 fusion.107
  724.8 154.2 %reduce-scatter.14.cloned.1.call-done = f32[256,2048]{1,0:T(8,128)} async-done(((f32[2048,2048]{1,0:T(8,128)}), f32[256,2048]{1,0:T(8,128)}) %reduce-scatter.14.cloned.1.call-update) | async-done | bytes 2097168 | tf_op jit(solution)/shard_map/reduce_scatter | solution.py:275
  882.1 165.7 %reduce-scatter.12.cloned.1.call-done = f32[256,2048]{1,0:T(8,128)} async-done(((f32[2048,2048]{1,0:T(8,128)}), f32[256,2048]{1,0:T(8,128)}) %reduce-scatter.12.cloned.1.call-update) | async-done | bytes 2097168 | tf_op jit(solution)/shard_map/reduce_scatter | solution.py:250
  1047.8 5.2 fusion.102
  1053.1 11.0 fusion.109
  1065.9 17.9 %fusion.56 = f32[2,2048,704]{1,2,0:T(8,128)} fusion(bf16[2048,2048]{1,0:T(8,128)(2,1)} %all-gather.15.cloned.1.call-done, bf16[1,2048,704]{1,2,0:T(8,128)(2,1)} %copy-done.61, bf16[1,2048,704]{1,2,0:T(8,128)(2,1)S(1)} %copy-done.60), kind=kOutput, calls=%fused_computation.74 | convolution fusion | flops 11814043648 | bytes 25690112 | tf_op jit(solution)/shard_map/td,ctf->cdf/dot_general | solution.py:271
  1084.0 49.7 %all-gather.23.cloned.1.call-done = bf16[2048,2048]{1,0:T(8,128)(2,1)} async-done(((bf16[256,2048]{1,0:T(8,128)(2,1)}), bf16[2048,2048]{1,0:T(8,128)(2,1)}) %all-gather.23.cloned.1.call-update) | async-done | bytes 8388624 | tf_op jit(solution)/shard_map/all_gather | solution.py:283
  1133.7 5.8 convolution_convert_fusion
  1142.6 7.4 fusion.108
  1150.1 239.9 %while.48 = (s32[]{:T(128)}, f32[2048,4,64]{0,2,1:T(8,128)}, f32[2048,4,64]{0,2,1:T(8,128)}, f32[4,512,4,64]{1,0,3,2:T(4,128)}, bf16[4,512,4,64]{1,3,2,0:T(8,128...) while((s32[]{:T(128)}, f32[2048,4,64]{0,2,1:T(8,128)}, ...), condition=%wide.region_15.16_spmd.clone, body=%wide.region_13.15_spmd.clone.sunk | while | flops 2752119296 | bytes 183042288 | solution.py:151
  1157.5 7.2 fusion.172
  1164.7 11.6 multiply_reduce_fusion.7
  1176.3 11.3 multiply_convert_fusion.4
  1187.6 6.4 fusion.173
  1198.4 11.1 dynamic_update_slice.33
  1216.4 7.6 fusion.172
  1224.1 11.5 multiply_reduce_fusion.7
  1235.6 11.3 multiply_convert_fusion.4
  1246.9 6.6 fusion.173
  1253.5 4.6 fusion.171
  1258.7 11.2 dynamic_update_slice.33
  1276.7 7.6 fusion.172
  1284.4 11.5 multiply_reduce_fusion.7
  1295.9 11.5 multiply_convert_fusion.4
  1307.4 6.4 fusion.173
  1313.8 4.6 fusion.171
  1318.9 11.1 dynamic_update_slice.33
  1336.9 7.6 fusion.172
  1344.6 11.8 multiply_reduce_fusion.7
  1356.4 10.9 multiply_convert_fusion.4
  1367.3 6.2 fusion.173
  1373.6 4.6 fusion.171
  1378.8 11.1 dynamic_update_slice.33
  1400.0 8.7 fusion.59
  1408.8 12.1 fusion.87
  1426.8 6.0 multiply_subtract_fusion.2
  1432.9 6.9 multiply_subtract_fusion
  1440.5 11.2 all-reduce
  1455.5 23.8 %reduce-scatter.18.cloned.1.call-done = f32[3,512,256]{1,2,0:T(8,128)} async-done(((f32[3,2048,256]{1,2,0:T(8,128)}), f32[3,512,256]{1,2,0:T(8,128)}) %reduce-scatter.18.cloned.1.call-update) | async-done | bytes 1572880 | tf_op jit(solution)/shard_map/reduce_scatter | solution.py:338
  1479.3 5.0 multiply_subtract_fusion.1
  1492.3 157.7 %reduce-scatter.16.cloned.1.call-done = f32[256,2048]{1,0:T(8,128)} async-done(((f32[2048,2048]{1,0:T(8,128)}), f32[256,2048]{1,0:T(8,128)}) %reduce-scatter.16.cloned.1.call-update) | async-done | bytes 2097168 | tf_op jit(solution)/shard_map/reduce_scatter | solution.py:326
  1652.6 38.0 %psum.7 = f32[4,2048]{1,0:T(4,128)S(1)} all-reduce(f32[4,2048]{1,0:T(4,128)S(1)} %pad_maximum_fusion.6), channel_id=1, replica_groups=mesh['dp'=4,'tensor'=8] {'dp','tensor'}, use_global_device_ids=true, to_apply=%region_29.30 | all-reduce | flops 8192 | bytes 65536 | tf_op jit(solution)/shard_map/psum | solution.py:336
  (294 shorter events, 129.8 us)
Async XLA Ops:
  7.2 50.0 %all-gather.11.cloned.1.call-start = ((), (), s32[]{:S(2)}) async-start(), calls=%async_computation.9 | async-start | bytes 3932160 | tf_op jit(solution)/shard_map/all_gather | solution.py:193
  9.2 4.5 copy-start.10
  10.3 131.1 %all-gather.9.cloned.1.call-start = ((), (), s32[]{:S(2)}) async-start(), calls=%async_computation.8 | async-start | bytes 9437184 | tf_op jit(solution)/shard_map/all_gather | solution.py:202
  10.6 4.1 copy-start.45
  10.6 4.1 copy-start.51
  13.8 210.3 %all-gather.13.cloned.1.call-start = ((), (), s32[]{:S(2)}) async-start(), calls=%async_computation.10 | async-start | bytes 1310720 | tf_op jit(solution)/shard_map/all_gather | solution.py:195
  14.6 386.1 %reduce-scatter.10.cloned.1.call-start = ((), (), s32[]{:S(2)}) async-start(), calls=%async_computation.11 | async-start | bytes 18874368 | tf_op jit(solution)/shard_map/reduce_scatter | solution.py:235
  25.8 126.4 %copy-start.28 = (f32[2048,8]{0,1:T(8,128)}, f32[2048,8]{0,1:T(8,128)S(1)}, u32[]{:S(2)}) copy-start(f32[2048,8]{0,1:T(8,128)S(1)} %get-tuple-element.465) | copy-start | bytes 196612
  219.9 13.8 copy-start.1
  219.9 13.8 copy-start.5
  219.9 13.8 copy-start.9
  219.9 13.8 copy-start.57
  233.8 166.9 %copy-start.7 = (bf16[256,2048]{1,0:T(8,128)(2,1)S(1)}, bf16[256,2048]{1,0:T(8,128)(2,1)}, u32[]{:S(2)}) copy-start(bf16[256,2048]{1,0:T(8,128)(2,1)} %param.26) | copy-start | bytes 3145732
  233.8 233.2 %all-gather.17.cloned.1.call-start = ((), (), s32[]{:S(2)}) async-start(), calls=%async_computation.13 | async-start | bytes 7208960 | tf_op jit(solution)/shard_map/all_gather | solution.py:194
  237.1 166.5 %copy-start.31 = (f32[1,2048]{1,0:T(1,128)S(1)}, f32[1,2048]{1,0:T(1,128)}, u32[]{:S(2)}) copy-start(f32[1,2048]{1,0:T(1,128)} %get-tuple-element.459) | copy-start | bytes 24580
  237.1 166.5 %copy-start.38 = (f32[1,2048]{1,0:T(1,128)S(1)}, f32[1,2048]{1,0:T(1,128)}, u32[]{:S(2)}) copy-start(f32[1,2048]{1,0:T(1,128)} %get-tuple-element.462) | copy-start | bytes 24580
  237.1 314.0 %all-gather.15.cloned.1.call-start = ((), (), s32[]{:S(2)}) async-start(), calls=%async_computation.12 | async-start | bytes 9437184 | tf_op jit(solution)/shard_map/all_gather | solution.py:243
  405.0 188.7 %all-gather.19.cloned.1.call-start = ((), (), s32[]{:S(2)}) async-start(), calls=%async_computation.14 | async-start | bytes 3604480 | tf_op jit(solution)/shard_map/all_gather | solution.py:196
  406.1 272.0 %all-gather.21.cloned.1.call-start = ((), (), s32[]{:S(2)}) async-start(), calls=%async_computation.16 | async-start | bytes 9437184 | tf_op jit(solution)/shard_map/all_gather | solution.py:264
  409.4 469.7 %reduce-scatter.14.cloned.1.call-start = ((), (), s32[]{:S(2)}) async-start(), calls=%async_computation.17 | async-start | bytes 18874368 | tf_op jit(solution)/shard_map/reduce_scatter | solution.py:275
  678.0 17.7 %copy-start.55 = (bf16[2,2048,704]{1,2,0:T(8,128)(2,1)S(1)}, bf16[2,2048,704]{1,2,0:T(8,128)(2,1)}, u32[]{:S(2)}) copy-start(bf16[2,2048,704]{1,2,0:T(8,128)(2,1)} %all-gather.17.cloned.1.call-done) | copy-start | bytes 17301508
  712.1 335.7 %reduce-scatter.12.cloned.1.call-start = ((), (), s32[]{:S(2)}) async-start(), calls=%async_computation.15 | async-start | bytes 18874368 | tf_op jit(solution)/shard_map/reduce_scatter | solution.py:250
  724.7 154.3 %copy-start.42 = (f32[256]{0:T(256)S(1)}, f32[256]{0:T(256)}, u32[]{:S(2)}) copy-start(f32[256]{0:T(256)} %copy-done.41) | copy-start | bytes 3076
  724.7 154.3 %copy-start.48 = (f32[256]{0:T(256)S(1)}, f32[256]{0:T(256)}, u32[]{:S(2)}) copy-start(f32[256]{0:T(256)} %copy-done.47) | copy-start | bytes 3076
  724.8 323.1 %copy-start.19 = (bf16[256,2048]{1,0:T(8,128)(2,1)S(1)}, bf16[256,2048]{1,0:T(8,128)(2,1)}, u32[]{:S(2)}) copy-start(bf16[256,2048]{1,0:T(8,128)(2,1)} %param.27) | copy-start | bytes 3145732
  724.8 408.9 %all-gather.23.cloned.1.call-start = ((), (), s32[]{:S(2)}) async-start(), calls=%async_computation.18 | async-start | bytes 9437184 | tf_op jit(solution)/shard_map/all_gather | solution.py:283
  1053.1 373.7 %reduce-scatter.24.cloned.1.call-start = ((), (), s32[]{:S(2)}) async-start(), calls=%async_computation.23 | async-start | bytes 7208960 | tf_op jit(solution)/shard_map/reduce_scatter | solution.py:341
  1064.1 368.7 %reduce-scatter.20.cloned.1.call-start = ((), (), s32[]{:S(2)}) async-start(), calls=%async_computation.21 | async-start | bytes 14417920 | tf_op jit(solution)/shard_map/reduce_scatter | solution.py:339
  1083.8 49.8 %copy-start.27 = (bf16[256,2048]{1,0:T(8,128)(2,1)S(1)}, bf16[256,2048]{1,0:T(8,128)(2,1)}, u32[]{:S(2)}) copy-start(bf16[256,2048]{1,0:T(8,128)(2,1)} %all-gather.13.cloned.1.call-done) | copy-start | bytes 3145732
  1083.9 368.6 %reduce-scatter.22.cloned.1.call-start = ((), (), s32[]{:S(2)}) async-start(), calls=%async_computation.22 | async-start | bytes 2621440 | tf_op jit(solution)/shard_map/reduce_scatter | solution.py:340
  1142.6 7.5 copy-start.2
  1142.6 7.5 copy-start.58
  1150.1 329.2 %reduce-scatter.18.cloned.1.call-start = ((), (), s32[]{:S(2)}) async-start(), calls=%async_computation.20 | async-start | bytes 7864320 | tf_op jit(solution)/shard_map/reduce_scatter | solution.py:338
  1187.6 6.4 copy-start
  1246.9 6.6 copy-start
  1307.4 6.4 copy-start
  1367.3 6.2 copy-start
  1390.0 3.8 copy-start.4
  1393.8 3.5 copy-start.29
  1393.8 3.6 copy-start.30
  1395.5 4.5 copy-start.54
  1397.4 11.4 copy-start.17
  1399.4 9.4 copy-start.20
  1399.5 9.3 copy-start.22
  1408.7 241.2 %reduce-scatter.16.cloned.1.call-start = ((), (), s32[]{:S(2)}) async-start(), calls=%async_computation.19 | async-start | bytes 18874368 | tf_op jit(solution)/shard_map/reduce_scatter | solution.py:326
  1426.8 6.0 copy-start.12
  1432.8 6.9 copy-start.18
  1432.8 6.9 copy-start.21
  1432.8 6.9 copy-start.23
  1439.8 12.0 copy-start.46
  1439.8 12.0 copy-start.52
  1439.8 12.0 copy-start.53
  1439.8 39.5 %copy-start.11 = (f32[3,512,256]{1,2,0:T(8,128)S(1)}, f32[3,512,256]{1,2,0:T(8,128)}, u32[]{:S(2)}) copy-start(f32[3,512,256]{1,2,0:T(8,128)} %copy-done.10) | copy-start | bytes 4718596
  1439.8 39.5 %copy-start.14 = (f32[3,512,256]{1,2,0:T(8,128)S(1)}, f32[3,512,256]{1,2,0:T(8,128)}, u32[]{:S(2)}) copy-start(f32[3,512,256]{1,2,0:T(8,128)} %copy.111) | copy-start | bytes 4718596
  1487.4 162.5 %copy-start.8 = (bf16[256,2048]{1,0:T(8,128)(2,1)S(1)}, bf16[256,2048]{1,0:T(8,128)(2,1)}, u32[]{:S(2)}) copy-start(bf16[256,2048]{1,0:T(8,128)(2,1)} %param.26) | copy-start | bytes 3145732
  1487.4 162.5 %copy-start.35 = (f32[1,2048]{1,0:T(1,128)S(1)}, f32[1,2048]{1,0:T(1,128)}, u32[]{:S(2)}) copy-start(f32[1,2048]{1,0:T(1,128)} %copy-done.34) | copy-start | bytes 24580
  1487.4 162.5 %copy-start.44 = (f32[256]{0:T(256)S(1)}, f32[256]{0:T(256)}, u32[]{:S(2)}) copy-start(f32[256]{0:T(256)} %copy-done.43) | copy-start | bytes 3076
  1487.4 162.5 %copy-start.50 = (f32[256]{0:T(256)S(1)}, f32[256]{0:T(256)}, u32[]{:S(2)}) copy-start(f32[256]{0:T(256)} %copy-done.49) | copy-start | bytes 3076
  1489.1 163.4 %copy-start.36 = (f32[2048]{0:T(1024)S(1)}, f32[2048]{0:T(1024)}, u32[]{:S(2)}) copy-start(f32[2048]{0:T(1024)} %get-tuple-element.369) | copy-start | bytes 24580
  1489.1 163.4 %copy-start.37 = (f32[2048]{0:T(1024)S(1)}, f32[2048]{0:T(1024)}, u32[]{:S(2)}) copy-start(f32[2048]{0:T(1024)} %get-tuple-element.376) | copy-start | bytes 24580
  1489.1 201.5 %copy-start.33 = (f32[4,2048]{1,0:T(4,128)S(1)}, f32[4,2048]{1,0:T(4,128)}, u32[]{:S(2)}) copy-start(f32[4,2048]{1,0:T(4,128)} %param.35) | copy-start | bytes 98308
  1489.1 201.5 %copy-start.39 = (f32[4,2048]{1,0:T(4,128)S(1)}, f32[4,2048]{1,0:T(4,128)}, u32[]{:S(2)}) copy-start(f32[4,2048]{1,0:T(4,128)} %param.41) | copy-start | bytes 98308
  1489.1 201.5 %copy-start.40 = (f32[4,2048]{1,0:T(4,128)S(1)}, f32[4,2048]{1,0:T(4,128)}, u32[]{:S(2)}) copy-start(f32[4,2048]{1,0:T(4,128)} %param.47) | copy-start | bytes 98308
  1489.1 202.2 %copy-start.13 = (f32[256,2048]{1,0:T(8,128)S(1)}, f32[256,2048]{1,0:T(8,128)}, u32[]{:S(2)}) copy-start(f32[256,2048]{1,0:T(8,128)} %get-tuple-element.434) | copy-start | bytes 6291460
  (20 other events, 45.3 us)
Sparse Core Ops, SparseCore 0:
  10.5 46.6 all-gather.10
  59.4 82.0 all-gather.8
  143.9 25.0 all-gather.12
  233.9 166.7 reduce-scatter.9
  403.0 63.9 all-gather.16
  469.0 82.0 all-gather.14
  553.5 40.1 all-gather.18
  595.9 82.0 all-gather.20
  712.2 166.7 reduce-scatter.13
  881.2 166.5 reduce-scatter.11
  1053.2 80.4 all-gather.22
  1136.5 64.3 reduce-scatter.23
  1204.0 112.1 reduce-scatter.19
  1319.0 35.1 reduce-scatter.21
  1408.8 70.4 reduce-scatter.17
  1481.6 168.2 reduce-scatter.15
where the time goes:
time: 1710 us; the launch traced here: 1700 us
  waiting for transfers between devices  1080 us (63%)
  matrix products  316 us (18%)
  other arithmetic  138 us (8%)
  local copies, waits for them, and re-layouts  89.6 us (5%)
  blocking collectives  59 us (3%)
    reduce_scatter x1, waiting for transfers between devices, local(): lax.psum_scatter(jnp.dot(rows_part, down_copy, preferred_element_type=jnp...  166 us
    reduce_scatter x1, waiting for transfers between devices, local(): lax.psum_scatter(jnp.dot(rows_part, out_copy, preferred_element_type=jnp....  164 us
    reduce_scatter x1, waiting for transfers between devices, local(): lax.psum_scatter(jnp.einsum('tc,dc->td', rows_part, qkv_flat, preferred_e...  158 us
    reduce_scatter x1, waiting for transfers between devices, local(): lax.psum_scatter(jnp.einsum('ctf,cdf->td', rows_part, gate_up_copy, prefe...  154 us
    all_gather x1, waiting for transfers between devices, local(): lax.all_gather(grad_result.astype(jnp.bfloat16), 'tensor', axis=0, tiled=...  84.3 us
    all_gather x1, waiting for transfers between devices, local(): gathered_one = lax.all_gather(normed_one, 'tensor', axis=0, tiled=True)  84.3 us
    all_gather x1, waiting for transfers between devices, local(): gathered_two = lax.all_gather(normed_two, 'tensor', axis=0, tiled=True)  84.1 us
    all_gather x1, waiting for transfers between devices, local(): lax.all_gather(gate_up_master.astype(jnp.bfloat16), 'dp', axis=1, tiled=T...  57.6 us
  transfers between devices with their start and end apart: 16, of which 12 were waited for; matrix products, arithmetic and copies ran while one was open for 28% of the time, Pallas kernels for 0%

commit v1 on v0

v1 whole, which is shorter than its diff:
```python
import functools
import math

import jax
import jax.numpy as jnp
from jax import lax
from jax.experimental import pallas as pl
from jax.experimental.pallas import tpu as pltpu
from jax.sharding import PartitionSpec as P

D = 2048
HEADS = 32
HEAD_DIM = 64
ROTARY = 16
FF = 5632


norm_eps = 1e-05
beta_one = 0.9
beta_two = 0.95
adam_eps = 1e-08
adam_steps = 10
decay_rate = 0.1
rope_base = 10000.0
score_scale = 0.125
mask_fill = -1e30
log2_e = math.log2(math.e)
LANES = 128
VMEM_LIMIT = 58 * 1024 * 1024


def norm_forward(values, gain_row, shift_row):
    average = jnp.mean(values, axis=-1, keepdims=True)
    centred = values - average
    spread = jnp.mean(centred * centred, axis=-1, keepdims=True)
    return centred * lax.rsqrt(spread + norm_eps) * gain_row + shift_row


def norm_backward(values, gain_row, grad_rows):
    average = jnp.mean(values, axis=-1, keepdims=True)
    centred = values - average
    spread = jnp.mean(centred * centred, axis=-1, keepdims=True)
    inverse = lax.rsqrt(spread + norm_eps)
    normal = centred * inverse
    grad_normal = grad_rows * gain_row
    grad_values = inverse * (
        grad_normal
        - jnp.mean(grad_normal, axis=-1, keepdims=True)
        - normal * jnp.mean(grad_normal * normal, axis=-1, keepdims=True)
    )
    return (grad_values, jnp.sum(grad_rows * normal, axis=0), jnp.sum(grad_rows, axis=0))


def rotary_tables(positions):
    half_rot = ROTARY // 2
    frequency = rope_base ** (-(2.0 * jnp.arange(half_rot, dtype=jnp.float32)) / ROTARY)
    angles = positions.astype(jnp.float32)[:, None] * frequency[None, :]
    cosine = jnp.cos(angles)
    sine_part = jnp.sin(angles)
    count = positions.shape[0]
    still = HEAD_DIM - ROTARY
    none = jnp.zeros((count, half_rot), jnp.float32)
    rest = jnp.zeros((count, still), jnp.float32)
    keep = [cosine, cosine, jnp.ones((count, still), jnp.float32)]
    ahead = [-sine_part, none, rest]
    behind = [none, sine_part, rest]
    copies = LANES // HEAD_DIM
    return tuple(jnp.concatenate(part * copies, axis=1) for part in (keep, ahead, behind))


def sum_rows(partial):
    return lax.psum_scatter(
        partial.astype(jnp.bfloat16), "tensor", scatter_dimension=0, tiled=True
    ).astype(jnp.float32)


def sum_shard(gradient, dimension):
    return lax.psum_scatter(
        gradient.astype(jnp.bfloat16), "dp", scatter_dimension=dimension, tiled=True
    ).astype(jnp.float32)


def swiglu(gate_part, up_part):
    return jax.nn.silu(gate_part) * up_part


def adamw(weight_old, first_old, second_old, gradient, step_rate, decay_part):
    first_new = beta_one * first_old + (1.0 - beta_one) * gradient
    second_new = beta_two * second_old + (1.0 - beta_two) * gradient * gradient
    correct_one = 1.0 - beta_one**adam_steps
    correct_two = 1.0 - beta_two**adam_steps
    update = first_new / correct_one / (jnp.sqrt(second_new / correct_two) + adam_eps)
    return (weight_old - step_rate * (update + decay_part * weight_old), first_new, second_new)


def spin(x, keep, ahead, behind):
    return x * keep + pltpu.roll(x, LANES - ROTARY // 2, 1) * ahead + pltpu.roll(x, ROTARY // 2, 1) * behind


def dot_nt(a, b):
    return lax.dot_general(a, b, (((1,), (1,)), ((), ())), preferred_element_type=jnp.float32)


def dot_nn(a, b):
    return lax.dot_general(a, b, (((1,), (0,)), ((), ())), preferred_element_type=jnp.float32)


def masked_scores(s, key_start, query_start, length, causal):
    key_slots = key_start + lax.broadcasted_iota(jnp.int32, s.shape, 0)
    allowed = key_slots < length
    if causal:
        query_slots = query_start + lax.broadcasted_iota(jnp.int32, s.shape, 1)
        allowed = allowed & (key_slots <= query_slots)
    return jnp.where(allowed, s, mask_fill)


def forward_kernel(block, length_ref, pre_ref, keep_ref, ahead_ref, behind_ref,
                   q_ref, k_ref, v_ref, kt_ref, o_ref, lse_ref, vt_ref):
    heads, rows, _ = q_ref.shape
    width = heads * HEAD_DIM
    groups = width // LANES
    per_group = LANES // HEAD_DIM
    blocks = rows // block
    length = length_ref[0]

    def prepare(i, _):
        at = pl.ds(pl.multiple_of(i * block, block), block)
        keep, ahead, behind = keep_ref[at, :], ahead_ref[at, :], behind_ref[at, :]
        for g in range(groups):
            lanes = slice(g * LANES, (g + 1) * LANES)
            q = spin(pre_ref[at, g * LANES:(g + 1) * LANES], keep, ahead, behind)
            k = spin(pre_ref[at, width + g * LANES:width + (g + 1) * LANES], keep, ahead, behind)
            v = pre_ref[at, 2 * width + g * LANES:2 * width + (g + 1) * LANES]
            kt_ref[lanes, at] = k.T.astype(jnp.bfloat16)
            vt_ref[lanes, at] = v.T.astype(jnp.bfloat16)
            for p in range(per_group):
                cut = slice(p * HEAD_DIM, (p + 1) * HEAD_DIM)
                q_ref[g * per_group + p, at, :] = q[:, cut].astype(jnp.bfloat16)
                k_ref[g * per_group + p, at, :] = k[:, cut].astype(jnp.bfloat16)
                v_ref[g * per_group + p, at, :] = v[:, cut].astype(jnp.bfloat16)
        return 0

    lax.fori_loop(0, blocks, prepare, 0)
    full_blocks = length // block
    used_blocks = (length + block - 1) // block

    def query_block(i, _):
        at = pl.ds(pl.multiple_of(i * block, block), block)
        queries = [q_ref[h, at, :] for h in range(heads)]

        def key_block(j, carry, kind):
            key_start = pl.multiple_of(j * block, block)
            keys_at = pl.ds(key_start, block)
            out = []
            for h in range(heads):
                top, total, mixed = carry[h]
                s = dot_nt(k_ref[h, keys_at, :], queries[h]) * (score_scale * log2_e)
                if kind > 0:
                    s = masked_scores(s, key_start, i * block, length, kind == 2)
                new_top = jnp.maximum(top, jnp.max(s, axis=0, keepdims=True))
                shrink = jnp.exp2(top - new_top)
                p = jnp.exp2(s - new_top)
                total = total * shrink + jnp.sum(p, axis=0, keepdims=True)
                mixed = mixed * shrink + dot_nn(
                    vt_ref[h * HEAD_DIM:(h + 1) * HEAD_DIM, keys_at], p.astype(jnp.bfloat16))
                out.append((new_top, total, mixed))
            return tuple(out)

        start = tuple(
            (jnp.full((1, block), mask_fill, jnp.float32), jnp.zeros((1, block), jnp.float32),
             jnp.zeros((HEAD_DIM, block), jnp.float32)) for _ in range(heads))
        plain = jnp.minimum(i, full_blocks)
        carry = lax.fori_loop(0, plain, lambda j, c: key_block(j, c, 0), start)
        carry = lax.fori_loop(plain, jnp.minimum(i, used_blocks), lambda j, c: key_block(j, c, 1), carry)
        carry = key_block(i, carry, 2)
        for h in range(heads):
            top, total, mixed = carry[h]
            lse_ref[h:h + 1, at] = top + jnp.log2(total)
        for g in range(groups):
            pair = [carry[g * per_group + p][2] * (1.0 / carry[g * per_group + p][1]) for p in range(per_group)]
            o_ref[at, g * LANES:(g + 1) * LANES] = jnp.concatenate(pair, axis=0).T.astype(jnp.bfloat16)
        return 0

    lax.fori_loop(0, blocks, query_block, 0)


def attention_forward(lengths, projected, keep, ahead, behind, heads, block):
    rows = projected.shape[0]
    width = heads * HEAD_DIM
    vm = pl.BlockSpec(memory_space=pltpu.VMEM)
    split = jax.ShapeDtypeStruct((heads, rows, HEAD_DIM), jnp.bfloat16)
    return pl.pallas_call(
        functools.partial(forward_kernel, block),
        out_shape=(split, split, split,
                   jax.ShapeDtypeStruct((width, rows), jnp.bfloat16),
                   jax.ShapeDtypeStruct((rows, width), jnp.bfloat16),
                   jax.ShapeDtypeStruct((heads, rows), jnp.float32)),
        in_specs=[pl.BlockSpec(memory_space=pltpu.SMEM)] + [vm] * 4,
        out_specs=(vm,) * 6,
        scratch_shapes=[pltpu.VMEM((width, rows), jnp.bfloat16)],
        compiler_params=pltpu.CompilerParams(vmem_limit_bytes=VMEM_LIMIT),
        cost_estimate=pl.CostEstimate(flops=heads * rows * rows * HEAD_DIM * 8, bytes_accessed=rows * width * 30, transcendentals=heads * rows * rows),
        name="attention_forward",
    )(lengths, projected, keep, ahead, behind)


def backward_kernel(block, length_ref, q_ref, k_ref, v_ref, kt_ref, o_ref, lse_ref, do_ref,
                    keep_ref, ahead_ref, behind_ref, out_ref, bias_ref,
                    dos_ref, delta_ref, dqt_ref, dk_ref, dv_ref):
    heads, rows, _ = q_ref.shape
    width = heads * HEAD_DIM
    groups = width // LANES
    per_group = LANES // HEAD_DIM
    blocks = rows // block
    length = length_ref[0]

    def prepare(i, _):
        at = pl.ds(pl.multiple_of(i * block, block), block)
        for g in range(groups):
            lanes = slice(g * LANES, (g + 1) * LANES)
            grad = do_ref[at, lanes]
            for p in range(per_group):
                dos_ref[g * per_group + p, at, :] = grad[:, p * HEAD_DIM:(p + 1) * HEAD_DIM]
            both = (grad.astype(jnp.float32) * o_ref[at, lanes].astype(jnp.float32)).T
            for p in range(per_group):
                h = g * per_group + p
                delta_ref[h:h + 1, at] = jnp.sum(both[p * HEAD_DIM:(p + 1) * HEAD_DIM], axis=0, keepdims=True)
        dqt_ref[:, at] = jnp.zeros((width, block), jnp.float32)
        return 0

    lax.fori_loop(0, blocks, prepare, 0)

    def key_block(j, _):
        key_start = pl.multiple_of(j * block, block)
        keys_at = pl.ds(key_start, block)

        def query_block(i, carry, kind):
            at = pl.ds(pl.multiple_of(i * block, block), block)
            out = []
            for h in range(heads):
                dk, dv = carry[h]
                keys, queries, grad = k_ref[h, keys_at, :], q_ref[h, at, :], dos_ref[h, at, :]
                s = dot_nt(keys, queries) * (score_scale * log2_e)
                if kind > 0:
                    s = masked_scores(s, key_start, i * block, length, kind == 2)
                p = jnp.exp2(s - lse_ref[h:h + 1, at])
                dp = dot_nt(v_ref[h, keys_at, :], grad)
                ds = (p * (dp - delta_ref[h:h + 1, at])).astype(jnp.bfloat16)
                dv = dv + dot_nn(p.astype(jnp.bfloat16), grad)
                dk = dk + dot_nn(ds, queries)
                here = slice(h * HEAD_DIM, (h + 1) * HEAD_DIM)
                dqt_ref[here, at] += dot_nn(kt_ref[here, keys_at], ds)
                out.append((dk, dv))
            return tuple(out)

        zero = jnp.zeros((block, HEAD_DIM), jnp.float32)
        carry = query_block(j, tuple((zero, zero) for _ in range(heads)), 2)
        whole = key_start + block <= length
        carry = lax.fori_loop(j + 1, jnp.where(whole, blocks, j + 1), lambda i, c: query_block(i, c, 0), carry)
        carry = lax.fori_loop(j + 1, jnp.where(whole, j + 1, blocks), lambda i, c: query_block(i, c, 1), carry)
        for h in range(heads):
            dk_ref[h, keys_at, :] = carry[h][0]
            dv_ref[h, keys_at, :] = carry[h][1]
        return 0

    lax.fori_loop(0, blocks, key_block, 0)
    bias_ref[...] = jnp.zeros(bias_ref.shape, jnp.float32)

    def finish(i, _):
        at = pl.ds(pl.multiple_of(i * block, block), block)
        keep, ahead, behind = keep_ref[at, :], -ahead_ref[at, :], -behind_ref[at, :]
        for g in range(groups):
            lanes = slice(g * LANES, (g + 1) * LANES)
            dq = dqt_ref[lanes, at].T
            dk = jnp.concatenate([dk_ref[g * per_group + p, at, :] for p in range(per_group)], axis=1)
            dv = jnp.concatenate([dv_ref[g * per_group + p, at, :] for p in range(per_group)], axis=1)
            parts = (spin(dq * score_scale, keep, ahead, behind), spin(dk * score_scale, keep, ahead, behind), dv)
            for c in range(3):
                low = parts[c].astype(jnp.bfloat16)
                place = slice(c * width + g * LANES, c * width + (g + 1) * LANES)
                out_ref[at, place] = low
                bias_ref[:, place] += jnp.sum(low.astype(jnp.float32), axis=0, keepdims=True)
        return 0

    lax.fori_loop(0, blocks, finish, 0)


def attention_backward(lengths, q, k, v, kt, o, lse, grad, keep, ahead, behind, block):
    heads, rows, _ = q.shape
    width = heads * HEAD_DIM
    vm = pl.BlockSpec(memory_space=pltpu.VMEM)
    return pl.pallas_call(
        functools.partial(backward_kernel, block),
        out_shape=(jax.ShapeDtypeStruct((rows, 3 * width), jnp.bfloat16),
                   jax.ShapeDtypeStruct((1, 3 * width), jnp.float32)),
        in_specs=[pl.BlockSpec(memory_space=pltpu.SMEM)] + [vm] * 10,
        out_specs=(vm,) * 2,
        scratch_shapes=[
            pltpu.VMEM((heads, rows, HEAD_DIM), jnp.bfloat16),
            pltpu.VMEM((heads, rows), jnp.float32),
            pltpu.VMEM((width, rows), jnp.float32),
            pltpu.VMEM((heads, rows, HEAD_DIM), jnp.float32),
            pltpu.VMEM((heads, rows, HEAD_DIM), jnp.float32),
        ],
        compiler_params=pltpu.CompilerParams(vmem_limit_bytes=VMEM_LIMIT),
        cost_estimate=pl.CostEstimate(flops=heads * rows * rows * HEAD_DIM * 20, bytes_accessed=rows * width * 30, transcendentals=heads * rows * rows),
        name="attention_backward",
    )(lengths, q, k, v, kt, o, lse, grad, keep, ahead, behind)


def local(
    inputs,
    cotangent,
    lengths,
    positions,
    qkv_master,
    gate_up_master,
    out_master,
    down_master,
    bias_master,
    norm_master,
    qkv_first,
    gate_up_first,
    out_first,
    down_first,
    bias_first,
    norm_first,
    qkv_second,
    gate_up_second,
    out_second,
    down_second,
    bias_second,
    norm_second,
):
    tensor_count = lax.axis_size("tensor")
    local_tokens = inputs.shape[0]
    group_tokens = local_tokens * tensor_count
    row_count = lengths.shape[0]
    row_length = group_tokens // row_count
    block_rows = min(256, row_length)
    heads_here = bias_master.shape[1]
    width_here = heads_here * HEAD_DIM
    own_start = lax.axis_index("tensor") * local_tokens
    qkv_copy, gate_up_copy, out_copy, down_copy, bias_copy = (
        lax.all_gather(qkv_master.astype(jnp.bfloat16), "dp", axis=1, tiled=True),
        lax.all_gather(gate_up_master.astype(jnp.bfloat16), "dp", axis=1, tiled=True),
        lax.all_gather(out_master.astype(jnp.bfloat16), "dp", axis=1, tiled=True),
        lax.all_gather(down_master.astype(jnp.bfloat16), "dp", axis=1, tiled=True),
        lax.all_gather(bias_master.astype(jnp.bfloat16), "dp", axis=2, tiled=True),
    )
    qkv_flat = jnp.transpose(qkv_copy, (1, 0, 2)).reshape(qkv_copy.shape[1], 3 * width_here)
    inputs_wide = inputs.astype(jnp.float32)
    normed_one = norm_forward(inputs_wide, norm_master[0], norm_master[1]).astype(jnp.bfloat16)
    gathered_one = lax.all_gather(normed_one, "tensor", axis=0, tiled=True)
    projected = jnp.dot(
        gathered_one, qkv_flat, preferred_element_type=jnp.float32
    ) + bias_copy.reshape(1, 3 * width_here).astype(jnp.float32)
    keep, ahead, behind = rotary_tables(positions)
    queries, keys, values, keys_flipped, mixed_low, log_totals = attention_forward(
        lengths, projected, keep, ahead, behind, heads_here, block_rows
    )
    rows_part = mixed_low
    branch_one = sum_rows(jnp.dot(rows_part, out_copy, preferred_element_type=jnp.float32))
    middle = inputs_wide + branch_one
    normed_two = norm_forward(middle, norm_master[2], norm_master[3]).astype(jnp.bfloat16)
    gathered_two = lax.all_gather(normed_two, "tensor", axis=0, tiled=True)
    gate_up = jnp.einsum(
        "td,cdf->ctf", gathered_two, gate_up_copy, preferred_element_type=jnp.float32
    )
    hidden_wide, swiglu_pull = jax.vjp(swiglu, gate_up[0], gate_up[1])
    hidden = hidden_wide.astype(jnp.bfloat16)
    rows_part = hidden
    branch_two = sum_rows(jnp.dot(rows_part, down_copy, preferred_element_type=jnp.float32))
    block_output = (middle + branch_two).astype(jnp.bfloat16)
    group_index = own_start + jnp.arange(local_tokens, dtype=jnp.int32)
    row_of = group_index // row_length
    slot_of = group_index % row_length
    row_match = row_of[:, None] == jnp.arange(row_count, dtype=jnp.int32)[None, :]
    length_of = jnp.sum(jnp.where(row_match, lengths[None, :], 0), axis=1)
    valid = (slot_of < length_of).astype(jnp.float32)
    grad_result = cotangent.astype(jnp.float32) * valid[:, None]
    gathered_grad = lax.all_gather(grad_result.astype(jnp.bfloat16), "tensor", axis=0, tiled=True)
    grad_down = jnp.einsum("tf,td->fd", hidden, gathered_grad, preferred_element_type=jnp.float32)
    grad_hidden = jnp.einsum(
        "td,fd->tf", gathered_grad, down_copy, preferred_element_type=jnp.float32
    )
    grad_gate, grad_up = swiglu_pull(grad_hidden)
    grad_gate_up = jnp.stack([grad_gate, grad_up]).astype(jnp.bfloat16)
    grad_gate_up_w = jnp.einsum(
        "td,ctf->cdf", gathered_two, grad_gate_up, preferred_element_type=jnp.float32
    )
    rows_part = grad_gate_up
    grad_normed_two = sum_rows(jnp.einsum("ctf,cdf->td", rows_part, gate_up_copy, preferred_element_type=jnp.float32))
    grad_middle_norm, gain_two, shift_two = norm_backward(middle, norm_master[2], grad_normed_two)
    grad_middle = grad_result + grad_middle_norm
    gathered_mid = lax.all_gather(grad_middle.astype(jnp.bfloat16), "tensor", axis=0, tiled=True)
    grad_out_w = jnp.einsum(
        "tw,td->wd", mixed_low, gathered_mid, preferred_element_type=jnp.float32
    )
    grad_mixed = jnp.einsum(
        "td,wd->tw", gathered_mid, out_copy, preferred_element_type=jnp.float32
    ).astype(jnp.bfloat16)

    grad_projected, grad_bias = attention_backward(
        lengths, queries, keys, values, keys_flipped, mixed_low, log_totals, grad_mixed, keep, ahead, behind, block_rows
    )
    grad_bias = grad_bias.reshape(3, heads_here, HEAD_DIM)
    grad_qkv_w = jnp.einsum(
        "td,tcw->cdw",
        gathered_one,
        grad_projected.reshape(group_tokens, 3, width_here),
        preferred_element_type=jnp.float32,
    )
    rows_part = grad_projected
    grad_normed_one = sum_rows(jnp.einsum("tc,dc->td", rows_part, qkv_flat, preferred_element_type=jnp.float32))
    grad_input_norm, gain_one, shift_one = norm_backward(
        inputs_wide, norm_master[0], grad_normed_one
    )
    input_grad = grad_middle + grad_input_norm
    norm_grads = lax.psum(jnp.stack([gain_one, shift_one, gain_two, shift_two]), ("dp", "tensor"))
    qkv_grad, gate_up_grad, out_grad, down_grad, bias_grad = (
        sum_shard(grad_qkv_w, 1),
        sum_shard(grad_gate_up_w, 1),
        sum_shard(grad_out_w, 1),
        sum_shard(grad_down, 1),
        lax.psum_scatter(grad_bias, "dp", scatter_dimension=2, tiled=True),
    )
    qkv_new = adamw(qkv_master, qkv_first, qkv_second, qkv_grad, 2.0 / math.sqrt(D), decay_rate)
    gate_up_new = adamw(
        gate_up_master, gate_up_first, gate_up_second, gate_up_grad, 2.0 / math.sqrt(D), decay_rate
    )
    out_new = adamw(
        out_master, out_first, out_second, out_grad, 16.0 / math.sqrt(HEADS * HEAD_DIM), decay_rate
    )
    down_new = adamw(
        down_master, down_first, down_second, down_grad, 6.0 / math.sqrt(FF), decay_rate
    )
    bias_new = adamw(bias_master, bias_first, bias_second, bias_grad, 1.5, 0.0)
    norm_new = adamw(norm_master, norm_first, norm_second, norm_grads, 0.7, 0.0)
    return (
        block_output,
        input_grad,
        qkv_new[0],
        qkv_new[1],
        qkv_new[2],
        gate_up_new[0],
        gate_up_new[1],
        gate_up_new[2],
        out_new[0],
        out_new[1],
        out_new[2],
        down_new[0],
        down_new[1],
        down_new[2],
        bias_new[0],
        bias_new[1],
        bias_new[2],
        norm_new[0],
        norm_new[1],
        norm_new[2],
    )


def solution(mesh):
    return jax.shard_map(
        local,
        mesh=mesh,
        in_specs=(
            P(("dp", "tensor"), None),
            P(("dp", "tensor"), None),
            P("dp"),
            P("dp"),
            P(None, "dp", "tensor"),
            P(None, "dp", "tensor"),
            P("tensor", "dp"),
            P("tensor", "dp"),
            P(None, "tensor", "dp"),
            P(),
            P(None, "dp", "tensor"),
            P(None, "dp", "tensor"),
            P("tensor", "dp"),
            P("tensor", "dp"),
            P(None, "tensor", "dp"),
            P(),
            P(None, "dp", "tensor"),
            P(None, "dp", "tensor"),
            P("tensor", "dp"),
            P("tensor", "dp"),
            P(None, "tensor", "dp"),
            P(),
        ),
        out_specs=(
            P(("dp", "tensor"), None),
            P(("dp", "tensor"), None),
            P(None, "dp", "tensor"),
            P(None, "dp", "tensor"),
            P(None, "dp", "tensor"),
            P(None, "dp", "tensor"),
            P(None, "dp", "tensor"),
            P(None, "dp", "tensor"),
            P("tensor", "dp"),
            P("tensor", "dp"),
            P("tensor", "dp"),
            P("tensor", "dp"),
            P("tensor", "dp"),
            P("tensor", "dp"),
            P(None, "tensor", "dp"),
            P(None, "tensor", "dp"),
            P(None, "tensor", "dp"),
            P(),
            P(),
            P(),
        ),
        check_vma=False,
    )
```

time: 1710 us -> 1230 us (0.72)
  waiting for transfers between devices: 1080 us -> 777 us
  matrix products: 316 us -> 147 us
  Pallas kernels: 0 us -> 120 us
  other arithmetic: 138 us -> 55.7 us
  local copies, waits for them, and re-layouts: 89.6 us -> 40.6 us
    reduce_scatter x8, waiting for transfers between devices: 665 us -> 378 us  [the longest x4 327 us: sum_rows(): lax.psum_scatter(partial.astype(jnp.bfloat16), 'tensor', scatter_dimensio...]
    dot_general x28 -> x0, matrix products: 171 us -> none  [the longest x4 46.5 us: one_block(): jnp.einsum('qhd,khd->hqk', grad_block, value_rows, preferred_element_type...]
    pallas_call x0 -> x2, Pallas kernels: none -> 120 us  [the longest x1 60 us: attention_backward(): pl.pallas_call(functools.partial(backward_kernel, block), out_shape=(jax....]
    convert_element_type x8 -> x1, other arithmetic: 47.1 us -> 0.01 us  [rotary_tables(): angles = positions.astype(jnp.float32)[:, None] * frequency[None, :]]
    dynamic_update_slice x8 -> x0, local copies, waits for them, and re-layouts: 46.7 us -> none  [row_backward(): lax.scan(one_block, (zeros, zeros), (queries.reshape(block_shape), grad_m...]
    all_gather x1, waiting for transfers between devices: 31.4 us -> 11.9 us  [local(): lax.all_gather(qkv_master.astype(jnp.bfloat16), 'dp', axis=1, tiled=True)]
    reduce_sum x5 -> x0, other arithmetic: 17.9 us -> none  [the longest x4 17.3 us: one_block(): row_total = jnp.sum(weights, axis=2, keepdims=True)]
  transfers between devices with their start and end apart: 16 -> 16, of which waited for: 12 -> 13; matrix products, arithmetic and copies ran while one was open for 28% -> 15% of each run, Pallas kernels for 0% -> 10%
where the time goes in v1:
time: 1230 us; the launch traced here: 1210 us
  waiting for transfers between devices  777 us (63%)
  matrix products  147 us (12%)
  Pallas kernels  120 us (10%)
  blocking collectives  57.7 us (5%)
  other arithmetic  55.7 us (5%)
  local copies, waits for them, and re-layouts  40.6 us (3%)
  between operations  15.9 us (1%)
    reduce_scatter x4, waiting for transfers between devices, sum_rows(): lax.psum_scatter(partial.astype(jnp.bfloat16), 'tensor', scatter_dimensio...  327 us
    all_gather x1, waiting for transfers between devices, local(): gathered_one = lax.all_gather(normed_one, 'tensor', axis=0, tiled=True)  84.3 us
    all_gather x1, waiting for transfers between devices, local(): lax.all_gather(grad_result.astype(jnp.bfloat16), 'tensor', axis=0, tiled=...  84.3 us
    all_gather x1, waiting for transfers between devices, local(): gathered_two = lax.all_gather(normed_two, 'tensor', axis=0, tiled=True)  84.1 us
    pallas_call x1, Pallas kernels, attention_backward(): pl.pallas_call(functools.partial(backward_kernel, block), out_shape=(jax....  60 us
    pallas_call x1, Pallas kernels, attention_forward(): pl.pallas_call(functools.partial(forward_kernel, block), out_shape=(split...  59.6 us
    all_gather x1, waiting for transfers between devices, local(): lax.all_gather(gate_up_master.astype(jnp.bfloat16), 'dp', axis=1, tiled=T...  58.4 us
    all_gather x1, waiting for transfers between devices, local(): lax.all_gather(grad_middle.astype(jnp.bfloat16), 'tensor', axis=0, tiled=...  51.9 us
  transfers between devices with their start and end apart: 16, of which 13 were waited for; matrix products, arithmetic and copies ran while one was open for 15% of the time, Pallas kernels for 10%

profile of v1, /device:TPU:0, one launch (start us, length us, event | category | flops | bytes accessed | tf_op | source)
XLA Modules:
  0.0 1214.8 jit_solution(15226725089166970461)
XLA Ops:
  7.2 1.9 copy.80
  9.2 1.0 convert_element_type.120
  10.2 0.9 copy-done
  12.5 1.4 fusion.36
  14.0 0.7 convert_element_type.125
  15.0 9.7 all_gather.29
  24.9 5.5 multiply_sine_fusion
  30.5 1.0 broadcast_in_dim.20
  31.6 5.1 concatenate.10.ahead_ref
  36.7 4.9 concatenate.11.behind_ref
  42.3 3.0 concatenate.9.keep_ref
  45.2 11.9 all-gather.11.cloned.1.call-done
  57.2 84.3 %all-gather.9.cloned.1.call-done = bf16[2048,2048]{1,0:T(8,128)(2,1)} async-done(((bf16[256,2048]{1,0:T(8,128)(2,1)}), bf16[2048,2048]{1,0:T(8,128)(2,1)}) %all-gather.9.cloned.1.call-update) | async-done | bytes 8388624 | tf_op jit(solution)/shard_map/all_gather | solution.py:354
  141.4 11.8 broadcast_add_fusion.pre_ref
  153.2 59.6 %attention_forward.1 = (bf16[4,2048,64]{2,1,0:T(8,128)(2,1)}, bf16[4,2048,64]{2,1,0:T(8,128)(2,1)}, bf16[4,2048,64]{2,1,0:T(8,128)(2,1)}, bf16[256,2048]{1,0:T(8...) custom-call(s32[1]{0:T(128)} %copy.94.length_ref, f32[2048,768]{1,0:T(8,128)} %broadcast_add_fusion.pre_ref, ...), custom_call_target="tpu_custom_call" | custom-call | flops 8589934592 | bytes 15728640 | tf_op jit(solution)/shard_map/attention_forward/pallas_call | solution.py:192
  212.8 7.2 convolution_convert_fusion.2
  220.0 3.1 convert_element_type.129
  223.2 84.2 %reduce-scatter.10.cloned.1.call-done = bf16[256,2048]{1,0:T(8,128)(2,1)} async-done(((bf16[2048,2048]{1,0:T(8,128)(2,1)}), bf16[256,2048]{1,0:T(8,128)(2,1)}) %reduce-scatter.10.cloned.1.call-update) | async-done | bytes 1048592 | tf_op jit(solution)/shard_map/reduce_scatter | solution.py:72
  307.3 1.7 fusion.49
  310.1 1.5 add_convert_fusion.1
  311.7 0.9 convert_element_type.131
  312.8 2.4 fusion.48
  315.3 58.4 %all-gather.17.cloned.1.call-done = bf16[2,2048,704]{1,2,0:T(8,128)(2,1)} async-done(((bf16[2,512,704]{1,2,0:T(8,128)(2,1)}), bf16[2,2048,704]{1,2,0:T(8,128)(2,1)}) %all-gather.17.cloned.1.call-update) | async-done | bytes 5767184 | tf_op jit(solution)/shard_map/all_gather | solution.py:346
  373.6 84.1 %all-gather.15.cloned.1.call-done = bf16[2048,2048]{1,0:T(8,128)(2,1)} async-done(((bf16[256,2048]{1,0:T(8,128)(2,1)}), bf16[2048,2048]{1,0:T(8,128)(2,1)}) %all-gather.15.cloned.1.call-update) | async-done | bytes 8388624 | tf_op jit(solution)/shard_map/all_gather | solution.py:366
  457.7 19.2 %fusion.10 = f32[2,2048,704]{1,2,0:T(8,128)} fusion(bf16[2,2048,704]{1,2,0:T(8,128)(2,1)} %all-gather.17.cloned.1.call-done, bf16[2048,2048]{1,0:T(8,128)(2,1)} %all-gather.15.cloned.1.call-done), kind=kOutput, calls=%fused_computation.22 | convolution fusion | flops 11811160064 | bytes 25690112 | tf_op jit(solution)/shard_map/td,cdf->ctf/dot_general | solution.py:367
  477.0 23.4 %all-gather.19.cloned.1.call-done = bf16[704,2048]{1,0:T(8,128)(2,1)} async-done(((bf16[704,512]{1,0:T(8,128)(2,1)}), bf16[704,2048]{1,0:T(8,128)(2,1)}) %all-gather.19.cloned.1.call-update) | async-done | bytes 2883600 | tf_op jit(solution)/shard_map/all_gather | solution.py:348
  500.4 84.3 %all-gather.21.cloned.1.call-done = bf16[2048,2048]{1,0:T(8,128)(2,1)} async-done(((bf16[256,2048]{1,0:T(8,128)(2,1)}), bf16[2048,2048]{1,0:T(8,128)(2,1)}) %all-gather.21.cloned.1.call-update) | async-done | bytes 8388624 | tf_op jit(solution)/shard_map/all_gather | solution.py:382
  584.6 15.1 %fusion.30 = (bf16[1,2048,704]{1,2,0:T(8,128)(2,1)S(1)}, bf16[1,2048,704]{1,2,0:T(8,128)(2,1)S(1)}, bf16[2048,704]{0,1:T(8,128)(2,1)}) fusion(f32[2,2048,704]{1,2,0:T(8,128)} %fusion.10, bf16[2048,2048]{1,0:T(8,128)(2,1)} %all-gather.21.cloned.1.call-done, bf16[704,2048]{1,0:T(8,128)(2,1)} %all-gather.19.cloned.1.call-done), kind=kOutput, calls=%fused_computation.48 | convolution fusion | flops 5928648704 | bytes 31457280 | tf_op jit(solution)/shard_map/td,fd->tf/dot_general | solution.py:384
  599.8 1.6 copy-done.36
  601.4 0.9 copy-done.37
  602.3 15.9 %bitcast_convert_fusion = bf16[2048,2048]{1,0:T(8,128)(2,1)} fusion(bf16[2,2048,704]{1,2,0:T(8,128)(2,1)S(1)} %copy-done.34, bf16[1,2048,704]{1,2,0:T(8,128)(2,1)S(1)} %get-tuple-element.165, bf16[1,2048,704]{1,2,0:T(8,128)(2,1)S(1)} %get-tuple-element.164), kind=kOutput, calls=%fused_computation | convolution fusion | flops 11818237952 | bytes 19922944 | tf_op jit(solution)/shard_map/ctf,cdf->td/dot_general | solution.py:393
  618.4 11.2 convolution_convert_fusion.1
  629.8 76.8 %reduce-scatter.14.cloned.1.call-done = bf16[256,2048]{1,0:T(8,128)(2,1)} async-done(((bf16[2048,2048]{1,0:T(8,128)(2,1)}), bf16[256,2048]{1,0:T(8,128)(2,1)}) %reduce-scatter.14.cloned.1.call-update) | async-done | bytes 1048592 | tf_op jit(solution)/shard_map/reduce_scatter | solution.py:72
  706.5 2.4 fusion.46
  709.0 87.7 %reduce-scatter.12.cloned.1.call-done = bf16[256,2048]{1,0:T(8,128)(2,1)} async-done(((bf16[2048,2048]{1,0:T(8,128)(2,1)}), bf16[256,2048]{1,0:T(8,128)(2,1)}) %reduce-scatter.12.cloned.1.call-update) | async-done | bytes 1048592 | tf_op jit(solution)/shard_map/reduce_scatter | solution.py:72
  796.7 4.8 fusion.71
  801.5 10.5 convolution_convert_fusion.3
  812.2 17.9 %convert_bitcast_fusion = bf16[2,2048,704]{1,2,0:T(8,128)(2,1)} fusion(bf16[2048,2048]{1,0:T(8,128)(2,1)} %all-gather.15.cloned.1.call-done, bf16[1,2048,704]{1,2,0:T(8,128)(2,1)} %copy-done.37, bf16[1,2048,704]{1,2,0:T(8,128)(2,1)} %copy-done.36), kind=kOutput, calls=%fused_computation.17 | convolution fusion | flops 11816927232 | bytes 19922944 | tf_op jit(solution)/shard_map/td,ctf->cdf/dot_general | solution.py:389
  830.2 51.9 %all-gather.23.cloned.1.call-done = bf16[2048,2048]{1,0:T(8,128)(2,1)} async-done(((bf16[256,2048]{1,0:T(8,128)(2,1)}), bf16[2048,2048]{1,0:T(8,128)(2,1)}) %all-gather.23.cloned.1.call-update) | async-done | bytes 8388624 | tf_op jit(solution)/shard_map/all_gather | solution.py:396
  882.1 6.7 convolution_convert_fusion.4
  889.1 7.2 convolution_convert_fusion.5.do_ref
  896.3 60.0 %attention_backward.1 = (bf16[2048,768]{1,0:T(8,128)(2,1)}, f32[1,768]{1,0:T(1,128)}) custom-call(s32[1]{0:T(128)} %copy.94.length_ref, bf16[4,2048,64]{2,1,0:T(8,128)(2,1)} %get-tuple-element.29.q_ref, bf16[4,2048,64]{2,1,0:T(8,128)(2,1)} %get-tuple-element.30.k_ref, bf16[4,2048,64]{2,1,0:T(8,128)(2,1)} %get-tuple-element.31.v_ref, ...), custom_call_target="tpu_custom_call" | custom-call | flops 21474836480 | bytes 15728640 | tf_op jit(solution)/shard_map/attention_backward/pallas_call | solution.py:292
  956.3 4.7 copy.85
  961.0 12.0 fusion.18
  973.4 12.3 %convolution_convert_fusion = bf16[2048,2048]{1,0:T(8,128)(2,1)} fusion(bf16[2048,768]{1,0:T(8,128)(2,1)} %get-tuple-element.34, bf16[2048,768]{0,1:T(8,128)(2,1)} %bitcast.98), kind=kOutput, calls=%fused_computation.8 | convolution fusion | flops 6446645248 | bytes 14680064 | tf_op jit(solution)/shard_map/tc,dc->td/dot_general | solution.py:415
  985.7 1.5 copy-done.12
  987.2 1.6 copy.84
  988.8 3.1 copy.86
  993.2 4.9 multiply_subtract_fusion.2
  998.2 9.1 multiply_subtract_fusion
  1007.4 10.1 all-reduce
  1017.5 0.7 multiply_subtract_fusion.5
  1018.2 6.7 reduce-scatter.22.cloned.1.call-done
  1024.8 2.7 multiply_subtract_fusion.3
  1027.5 44.4 %reduce-scatter.18.cloned.1.call-done = bf16[3,512,256]{1,2,0:T(8,128)(2,1)} async-done(((bf16[3,2048,256]{1,2,0:T(8,128)(2,1)}), bf16[3,512,256]{1,2,0:T(8,128)(2,1)}) %reduce-scatter.18.cloned.1.call-update) | async-done | bytes 786448 | tf_op jit(solution)/shard_map/reduce_scatter | solution.py:78
  1071.9 5.2 multiply_subtract_fusion.1
  1077.1 3.1 copy.89
  1080.2 1.6 copy.90
  1081.9 3.2 copy.91
  1085.0 78.8 %reduce-scatter.16.cloned.1.call-done = bf16[256,2048]{1,0:T(8,128)(2,1)} async-done(((bf16[2048,2048]{1,0:T(8,128)(2,1)}), bf16[256,2048]{1,0:T(8,128)(2,1)}) %reduce-scatter.16.cloned.1.call-update) | async-done | bytes 1048592 | tf_op jit(solution)/shard_map/reduce_scatter | solution.py:72
  1163.8 2.3 fusion.47
  1166.1 37.9 %psum.7 = f32[4,2048]{1,0:T(4,128)S(1)} all-reduce(f32[4,2048]{1,0:T(4,128)S(1)} %pad_maximum_fusion.3), channel_id=1, replica_groups=mesh['dp'=4,'tensor'=8] {'dp','tensor'}, use_global_device_ids=true, to_apply=%region_21.22 | all-reduce | flops 8192 | bytes 65536 | tf_op jit(solution)/shard_map/psum | solution.py:420
  1204.1 0.7 multiply_subtract_fusion.4
  1204.8 3.3 fusion.39
  (131 shorter events, 5.5 us)
Async XLA Ops:
  7.2 50.0 %all-gather.11.cloned.1.call-start = ((), (), s32[]{:S(2)}) async-start(), calls=%async_computation.9 | async-start | bytes 3932160 | tf_op jit(solution)/shard_map/all_gather | solution.py:345
  9.1 2.2 copy-start.2
  9.1 2.0 copy-start
  9.1 2.7 copy-start.16
  10.2 131.3 %all-gather.9.cloned.1.call-start = ((), (), s32[]{:S(2)}) async-start(), calls=%async_computation.8 | async-start | bytes 9437184 | tf_op jit(solution)/shard_map/all_gather | solution.py:354
  11.4 2.6 copy-start.20
  11.4 2.6 copy-start.10
  11.8 2.9 copy-start.26
  11.9 0.6 copy-start.14
  12.5 2.4 copy-start.24
  12.5 12.4 %copy-start.30 = (s32[2048]{0:T(1024)S(1)}, s32[2048]{0:T(1024)}, u32[]{:S(2)}) copy-start(s32[2048]{0:T(1024)} %param.25) | copy-start | bytes 24580
  14.0 198.8 %all-gather.13.cloned.1.call-start = ((), (), s32[]{:S(2)}) async-start(), calls=%async_computation.10 | async-start | bytes 1310720 | tf_op jit(solution)/shard_map/all_gather | solution.py:347
  14.8 292.5 %reduce-scatter.10.cloned.1.call-start = ((), (), s32[]{:S(2)}) async-start(), calls=%async_computation.11 | async-start | bytes 9437184 | tf_op jit(solution)/shard_map/reduce_scatter | solution.py:72
  219.9 153.7 %all-gather.17.cloned.1.call-start = ((), (), s32[]{:S(2)}) async-start(), calls=%async_computation.13 | async-start | bytes 7208960 | tf_op jit(solution)/shard_map/all_gather | solution.py:346
  223.1 234.6 %all-gather.15.cloned.1.call-start = ((), (), s32[]{:S(2)}) async-start(), calls=%async_computation.12 | async-start | bytes 9437184 | tf_op jit(solution)/shard_map/all_gather | solution.py:366
  307.3 1.7 copy-start.1
  309.0 0.6 copy-start.22
  309.5 0.6 copy-start.28
  310.1 1.6 copy-start.7
  311.6 188.7 %all-gather.19.cloned.1.call-start = ((), (), s32[]{:S(2)}) async-start(), calls=%async_computation.14 | async-start | bytes 3604480 | tf_op jit(solution)/shard_map/all_gather | solution.py:348
  312.7 272.0 %all-gather.21.cloned.1.call-start = ((), (), s32[]{:S(2)}) async-start(), calls=%async_computation.16 | async-start | bytes 9437184 | tf_op jit(solution)/shard_map/all_gather | solution.py:382
  315.2 391.3 %reduce-scatter.14.cloned.1.call-start = ((), (), s32[]{:S(2)}) async-start(), calls=%async_computation.17 | async-start | bytes 9437184 | tf_op jit(solution)/shard_map/reduce_scatter | solution.py:72
  584.6 17.7 %copy-start.34 = (bf16[2,2048,704]{1,2,0:T(8,128)(2,1)S(1)}, bf16[2,2048,704]{1,2,0:T(8,128)(2,1)}, u32[]{:S(2)}) copy-start(bf16[2,2048,704]{1,2,0:T(8,128)(2,1)} %all-gather.17.cloned.1.call-done) | copy-start | bytes 17301508
  599.8 1.6 copy-start.36
  599.8 2.5 copy-start.37
  618.2 178.4 %reduce-scatter.12.cloned.1.call-start = ((), (), s32[]{:S(2)}) async-start(), calls=%async_computation.15 | async-start | bytes 9437184 | tf_op jit(solution)/shard_map/reduce_scatter | solution.py:72
  629.7 76.8 %copy-start.23 = (f32[256]{0:T(256)S(1)}, f32[256]{0:T(256)}, u32[]{:S(2)}) copy-start(f32[256]{0:T(256)} %copy-done.22) | copy-start | bytes 3076
  629.7 76.8 %copy-start.29 = (f32[256]{0:T(256)S(1)}, f32[256]{0:T(256)}, u32[]{:S(2)}) copy-start(f32[256]{0:T(256)} %copy-done.28) | copy-start | bytes 3076
  629.7 252.3 %all-gather.23.cloned.1.call-start = ((), (), s32[]{:S(2)}) async-start(), calls=%async_computation.18 | async-start | bytes 9437184 | tf_op jit(solution)/shard_map/all_gather | solution.py:396
  706.5 90.1 %copy-start.9 = (bf16[256,2048]{1,0:T(8,128)(2,1)S(1)}, bf16[256,2048]{1,0:T(8,128)(2,1)}, u32[]{:S(2)}) copy-start(bf16[256,2048]{1,0:T(8,128)(2,1)} %reduce-scatter.14.cloned.1.call-done) | copy-start | bytes 3145732
  801.5 191.7 %reduce-scatter.24.cloned.1.call-start = ((), (), s32[]{:S(2)}) async-start(), calls=%async_computation.23 | async-start | bytes 3604480 | tf_op jit(solution)/shard_map/reduce_scatter | solution.py:78
  812.1 186.1 %reduce-scatter.20.cloned.1.call-start = ((), (), s32[]{:S(2)}) async-start(), calls=%async_computation.21 | async-start | bytes 7208960 | tf_op jit(solution)/shard_map/reduce_scatter | solution.py:78
  830.1 52.0 %copy-start.4 = (bf16[2048,256]{1,0:T(8,128)(2,1)S(1)}, bf16[2048,256]{1,0:T(8,128)(2,1)}, u32[]{:S(2)}) copy-start(bf16[2048,256]{1,0:T(8,128)(2,1)} %get-tuple-element.28.o_ref) | copy-start | bytes 3145732
  830.1 59.0 %copy-start.13 = (bf16[256,2048]{1,0:T(8,128)(2,1)S(1)}, bf16[256,2048]{1,0:T(8,128)(2,1)}, u32[]{:S(2)}) copy-start(bf16[256,2048]{1,0:T(8,128)(2,1)} %all-gather.13.cloned.1.call-done) | copy-start | bytes 3145732
  830.1 194.7 %reduce-scatter.22.cloned.1.call-start = ((), (), s32[]{:S(2)}) async-start(), calls=%async_computation.22 | async-start | bytes 1310720 | tf_op jit(solution)/shard_map/reduce_scatter | solution.py:78
  888.8 183.1 %reduce-scatter.18.cloned.1.call-start = ((), (), s32[]{:S(2)}) async-start(), calls=%async_computation.20 | async-start | bytes 3932160 | tf_op jit(solution)/shard_map/reduce_scatter | solution.py:78
  973.0 190.8 %reduce-scatter.16.cloned.1.call-start = ((), (), s32[]{:S(2)}) async-start(), calls=%async_computation.19 | async-start | bytes 9437184 | tf_op jit(solution)/shard_map/reduce_scatter | solution.py:72
  985.7 1.5 copy-start.12
  988.8 3.1 copy-start.35
  988.8 4.4 copy-start.8
  998.1 9.1 copy-start.33
  998.2 19.3 %copy-start.25 = (f32[3,4,16]{2,1,0:T(4,128)S(1)}, f32[3,4,16]{2,1,0:T(4,128)}, u32[]{:S(2)}) copy-start(f32[3,4,16]{2,1,0:T(4,128)} %param.30) | copy-start | bytes 2308
  998.2 19.3 %copy-start.31 = (f32[3,4,16]{2,1,0:T(4,128)S(1)}, f32[3,4,16]{2,1,0:T(4,128)}, u32[]{:S(2)}) copy-start(f32[3,4,16]{2,1,0:T(4,128)} %param.36) | copy-start | bytes 2308
  998.2 19.3 %copy-start.32 = (f32[3,4,16]{2,1,0:T(4,128)S(1)}, f32[3,4,16]{2,1,0:T(4,128)}, u32[]{:S(2)}) copy-start(f32[3,4,16]{2,1,0:T(4,128)} %param.42) | copy-start | bytes 2308
  998.2 26.7 %copy-start.11 = (f32[256,512]{1,0:T(8,128)S(1)}, f32[256,512]{1,0:T(8,128)}, u32[]{:S(2)}) copy-start(f32[256,512]{1,0:T(8,128)} %param.28) | copy-start | bytes 1572868
  1007.3 64.6 %copy-start.3 = (f32[3,512,256]{1,2,0:T(8,128)S(1)}, f32[3,512,256]{1,2,0:T(8,128)}, u32[]{:S(2)}) copy-start(f32[3,512,256]{1,2,0:T(8,128)} %copy-done.2) | copy-start | bytes 4718596
  1077.1 3.1 copy-start.6
  1081.8 82.0 %copy-start.15 = (f32[1,2048]{1,0:T(1,128)S(1)}, f32[1,2048]{1,0:T(1,128)}, u32[]{:S(2)}) copy-start(f32[1,2048]{1,0:T(1,128)} %copy-done.14) | copy-start | bytes 24580
  1081.8 82.0 %copy-start.21 = (f32[256]{0:T(256)S(1)}, f32[256]{0:T(256)}, u32[]{:S(2)}) copy-start(f32[256]{0:T(256)} %copy-done.20) | copy-start | bytes 3076
  1081.8 82.0 %copy-start.27 = (f32[256]{0:T(256)S(1)}, f32[256]{0:T(256)}, u32[]{:S(2)}) copy-start(f32[256]{0:T(256)} %copy-done.26) | copy-start | bytes 3076
  1081.8 122.2 %copy-start.17 = (f32[4,2048]{1,0:T(4,128)S(1)}, f32[4,2048]{1,0:T(4,128)}, u32[]{:S(2)}) copy-start(f32[4,2048]{1,0:T(4,128)} %param.31) | copy-start | bytes 98308
  1081.8 122.3 %copy-start.18 = (f32[4,2048]{1,0:T(4,128)S(1)}, f32[4,2048]{1,0:T(4,128)}, u32[]{:S(2)}) copy-start(f32[4,2048]{1,0:T(4,128)} %param.37) | copy-start | bytes 98308
  1081.8 122.3 %copy-start.19 = (f32[4,2048]{1,0:T(4,128)S(1)}, f32[4,2048]{1,0:T(4,128)}, u32[]{:S(2)}) copy-start(f32[4,2048]{1,0:T(4,128)} %param.43) | copy-start | bytes 98308
  1081.9 122.9 %copy-start.5 = (f32[256,2048]{1,0:T(8,128)S(1)}, f32[256,2048]{1,0:T(8,128)}, u32[]{:S(2)}) copy-start(f32[256,2048]{1,0:T(8,128)} %get-tuple-element.163) | copy-start | bytes 6291460
Sparse Core Ops, SparseCore 0:
  10.4 46.6 all-gather.10
  59.3 82.0 all-gather.8
  143.8 25.0 all-gather.12
  220.1 87.2 reduce-scatter.9
  309.6 64.0 all-gather.16
  375.6 82.0 all-gather.14
  460.1 40.1 all-gather.18
  502.5 82.0 all-gather.20
  618.3 88.1 reduce-scatter.13
  708.7 87.9 reduce-scatter.11
  801.6 80.3 all-gather.22
  884.9 40.2 reduce-scatter.23
  928.3 65.8 reduce-scatter.19
  996.9 27.9 reduce-scatter.21
  1027.9 43.9 reduce-scatter.17
  1074.2 89.5 reduce-scatter.15

commit v2 on v1

--- a/solution.py
+++ b/solution.py
@@ -26,7 +26,7 @@
 mask_fill = -1e30
 log2_e = math.log2(math.e)
 LANES = 128
-VMEM_LIMIT = 58 * 1024 * 1024
+VMEM_LIMIT = 60 * 1024 * 1024
 
 
 def norm_forward(values, gain_row, shift_row):
@@ -48,7 +48,11 @@
         - jnp.mean(grad_normal, axis=-1, keepdims=True)
         - normal * jnp.mean(grad_normal * normal, axis=-1, keepdims=True)
     )
-    return (grad_values, jnp.sum(grad_rows * normal, axis=0), jnp.sum(grad_rows, axis=0))
+    return (
+        grad_values,
+        jnp.sum(grad_rows * normal, axis=0, keepdims=True),
+        jnp.sum(grad_rows, axis=0, keepdims=True),
+    )
 
 
 def rotary_tables(positions):
@@ -68,20 +72,10 @@
     return tuple(jnp.concatenate(part * copies, axis=1) for part in (keep, ahead, behind))
 
 
-def sum_rows(partial):
-    return lax.psum_scatter(
-        partial.astype(jnp.bfloat16), "tensor", scatter_dimension=0, tiled=True
-    ).astype(jnp.float32)
-
-
 def sum_shard(gradient, dimension):
     return lax.psum_scatter(
         gradient.astype(jnp.bfloat16), "dp", scatter_dimension=dimension, tiled=True
     ).astype(jnp.float32)
-
-
-def swiglu(gate_part, up_part):
-    return jax.nn.silu(gate_part) * up_part
 
 
 def adamw(weight_old, first_old, second_old, gradient, step_rate, decay_part):
@@ -306,6 +300,522 @@
         cost_estimate=pl.CostEstimate(flops=heads * rows * rows * HEAD_DIM * 20, bytes_accessed=rows * width * 30, transcendentals=heads * rows * rows),
         name="attention_backward",
     )(lengths, q, k, v, kt, o, lse, grad, keep, ahead, behind)
+
+
+VM = pl.BlockSpec(memory_space=pltpu.VMEM)
+MESH = pl.DeviceIdType.MESH
+
+
+def params(number):
+    return pltpu.CompilerParams(collective_id=number, has_side_effects=True, vmem_limit_bytes=VMEM_LIMIT)
+
+
+def lasting(us):
+    return pl.CostEstimate(flops=int(us * 1.1e9), bytes_accessed=0, transcendentals=0)
+
+
+def place():
+    t = lax.axis_index("tensor")
+    return t, lax.rem(t, 2), lax.div(t, 2)
+
+
+def greet(n):
+    t, core, chip = place()
+    barrier = pltpu.get_barrier_semaphore()
+
+    def hail(index):
+        pl.semaphore_signal(barrier, inc=1, device_id={"tensor": index}, device_id_type=MESH)
+
+    hail(t + 1 - 2 * core)
+    pl.when(chip > 0)(lambda: hail(t - 2))
+    pl.when(chip < n - 1)(lambda: hail(t + 2))
+    pl.semaphore_wait(barrier, 1 + jnp.minimum(chip, 1) + jnp.minimum(n - 1 - chip, 1))
+
+
+def near(j, m, n):
+    below, above = m, n - 1 - m
+    both = jnp.minimum(below, above)
+    half = lax.div(j + 1, 2)
+    inside = m + jnp.where(lax.rem(j, 2) == 1, -half, half)
+    outside = m + jnp.where(above > below, j - both, both - j)
+    return jnp.where(j <= 2 * both, inside, outside)
+
+
+class Gather:
+    def __init__(self, n, own, buf, sems, pieces):
+        self.n, self.own, self.buf, self.pieces = n, own, buf, pieces
+        self.up, self.down, self.side, self.line_in, self.side_in = [sems.at[i] for i in range(5)]
+        self.t, self.core, self.m = place()
+        self.sibling = self.t + 1 - 2 * self.core
+        self.rows = own.shape[0] // pieces
+
+    def copy(self, src, k, p, core, send, recv, target):
+        at = pl.ds(pl.multiple_of(p * self.rows, self.rows), self.rows)
+        index = k * self.pieces + p
+        return pltpu.make_async_remote_copy(
+            src_ref=src.at[at], dst_ref=self.buf.at[2 * k + core, at], send_sem=send.at[index],
+            recv_sem=recv.at[index], device_id={"tensor": target}, device_id_type=MESH)
+
+    def to_up(self, k, p, src):
+        return self.copy(src, k, p, self.core, self.up, self.line_in, self.t + 2)
+
+    def to_down(self, k, p, src):
+        return self.copy(src, k, p, self.core, self.down, self.line_in, self.t - 2)
+
+    def to_side(self, k, p, src):
+        return self.copy(src, k, p, self.core, self.side, self.side_in, self.sibling)
+
+    def start(self):
+        m = self.m
+        for p in range(self.pieces):
+            pl.when(m < self.n - 1)(lambda: self.to_up(m, p, self.own).start())
+            pl.when(m > 0)(lambda: self.to_down(m, p, self.own).start())
+            self.to_side(m, p, self.own).start()
+
+    def arrive(self, d, only=None):
+        m = self.m
+        lo, hi = m - d, m + d
+        for p in range(self.pieces) if only is None else (only,):
+            @pl.when(lo >= 0)
+            def _():
+                src = self.buf.at[2 * lo + self.core]
+                self.to_up(lo, p, src).wait_recv()
+                pl.when(m < self.n - 1)(lambda: self.to_up(lo, p, src).start())
+                self.to_side(lo, p, src).start()
+
+            @pl.when(hi < self.n)
+            def _():
+                src = self.buf.at[2 * hi + self.core]
+                self.to_down(hi, p, src).wait_recv()
+                pl.when(m > 0)(lambda: self.to_down(hi, p, src).start())
+                self.to_side(hi, p, src).start()
+
+    def side_wait(self, k):
+        for p in range(self.pieces):
+            self.copy(self.own, k, p, 1 - self.core, self.side, self.side_in, self.sibling).wait_recv()
+
+    def finish(self):
+        m = self.m
+
+        def one(k, _):
+            for p in range(self.pieces):
+                pl.when((k <= m) & (m < self.n - 1))(lambda: self.to_up(k, p, self.own).wait_send())
+                pl.when((k >= m) & (m > 0))(lambda: self.to_down(k, p, self.own).wait_send())
+                self.to_side(k, p, self.own).wait_send()
+            return 0
+
+        lax.fori_loop(0, self.n, one, 0)
+
+
+class Scatter:
+    def __init__(self, n, pieces, side_out, side_in, line_in, side_sems, line_send, line_recv):
+        self.n, self.pieces = n, pieces
+        self.side_out, self.side_in, self.line_in = side_out, side_in, line_in
+        self.side_send, self.side_recv = side_sems.at[0], side_sems.at[1]
+        self.line_send, self.line_recv = line_send, line_recv
+        self.t, self.core, self.m = place()
+        self.sibling = self.t + 1 - 2 * self.core
+        self.rows = side_out.shape[1] // pieces
+        self.step = min(32, self.rows)
+
+    def side(self, k):
+        return pltpu.make_async_remote_copy(
+            src_ref=self.side_out.at[k], dst_ref=self.side_in.at[k], send_sem=self.side_send.at[k],
+            recv_sem=self.side_recv.at[k], device_id={"tensor": self.sibling}, device_id_type=MESH)
+
+    def line(self, k, p, slot, target):
+        at = pl.ds(pl.multiple_of(p * self.rows, self.rows), self.rows)
+        return pltpu.make_async_remote_copy(
+            src_ref=self.side_in.at[k, at], dst_ref=self.line_in.at[slot, at],
+            send_sem=self.line_send.at[k * self.pieces + p], recv_sem=self.line_recv.at[slot * self.pieces + p],
+            device_id={"tensor": target}, device_id_type=MESH)
+
+    def each(self, p, body):
+        def one(i, _):
+            body(pl.ds(pl.multiple_of(p * self.rows + i * self.step, self.step), self.step))
+            return 0
+
+        lax.fori_loop(0, self.rows // self.step, one, 0)
+
+    def pass_on(self, k, own, between=None):
+        m, n = self.m, self.n
+        self.side(k).wait_recv()
+        inner = ((k > m) & (m > 0)) | ((k < m) & (m < n - 1))
+
+        def one(p, _):
+            @pl.when(inner)
+            def _():
+                self.line(k, p, k, self.t).wait_recv()
+
+                def add(at):
+                    total = own[at, :] + self.side_in[k, at, :].astype(jnp.float32) + self.line_in[k, at, :].astype(jnp.float32)
+                    self.side_in[k, at, :] = total.astype(jnp.bfloat16)
+
+                self.each(p, add)
+
+            @pl.when(jnp.logical_not(inner))
+            def _():
+                def add(at):
+                    self.side_in[k, at, :] = (own[at, :] + self.side_in[k, at, :].astype(jnp.float32)).astype(jnp.bfloat16)
+
+                self.each(p, add)
+
+            pl.when(k > m)(lambda: self.line(k, p, k, self.t + 2).start())
+            pl.when(k < m)(lambda: self.line(k, p, jnp.where(k == m - 1, n, k), self.t - 2).start())
+            if between is not None:
+                between(p)
+            return 0
+
+        lax.fori_loop(0, self.pieces, one, 0)
+
+    def settle(self, own, consume):
+        m, n = self.m, self.n
+        self.side(m).wait_recv()
+
+        def one(p, _):
+            def first(at):
+                own[at, :] += self.side_in[m, at, :].astype(jnp.float32)
+
+            self.each(p, first)
+
+            def more(slot):
+                self.line(m, p, slot, self.t).wait_recv()
+
+                def add(at):
+                    own[at, :] += self.line_in[slot, at, :].astype(jnp.float32)
+
+                self.each(p, add)
+
+            pl.when(m > 0)(lambda: more(m))
+            pl.when(m < n - 1)(lambda: more(n))
+            self.each(p, lambda at: consume(at, own[at, :]))
+            return 0
+
+        lax.fori_loop(0, self.pieces, one, 0)
+
+    def finish(self):
+        def one(k, _):
+            self.side(k).wait_send()
+
+            @pl.when(k != self.m)
+            def _():
+                for p in range(self.pieces):
+                    self.line(k, p, k, self.t).wait_send()
+
+            return 0
+
+        lax.fori_loop(0, self.n, one, 0)
+
+
+def scatter_scratch(n, pieces, rows, width):
+    return [
+        pltpu.VMEM((n, rows, width), jnp.bfloat16), pltpu.VMEM((n, rows, width), jnp.bfloat16),
+        pltpu.VMEM((n + 1, rows, width), jnp.bfloat16),
+        pltpu.SemaphoreType.DMA((2, n)), pltpu.SemaphoreType.DMA((n * pieces,)), pltpu.SemaphoreType.DMA(((n + 1) * pieces,)),
+    ]
+
+
+def gather_kernel(n, pieces, x_ref, g_ref, sems):
+    greet(n)
+    g = Gather(n, x_ref, g_ref, sems, pieces)
+    g.start()
+    g_ref[g.t] = x_ref[...]
+    for d in range(1, n):
+        g.arrive(d)
+    for k in range(n):
+        g.side_wait(k)
+    g.finish()
+
+
+def gather(x, n, number, pieces=4):
+    rows, d = x.shape
+    return pl.pallas_call(functools.partial(gather_kernel, n, pieces),
+        out_shape=jax.ShapeDtypeStruct((2 * n, rows, d), x.dtype),
+        in_specs=[VM], out_specs=VM,
+        scratch_shapes=[pltpu.SemaphoreType.DMA((5, n * pieces))],
+        compiler_params=params(number),
+        cost_estimate=lasting(78), name="gather_rows")(x)
+
+
+def out_kernel(n, pieces, mixed_ref, w_ref, x_ref, norm_ref, cot_ref, middle_ref, normed_ref, cots_ref,
+               acc_ref, side_out, side_in, line_in, side_sems, line_send, line_recv, gather_sems):
+    greet(n)
+    g = Gather(n, cot_ref, cots_ref, gather_sems, pieces)
+    s = Scatter(n, pieces, side_out, side_in, line_in, side_sems, line_send, line_recv)
+    g.start()
+    cots_ref[g.t] = cot_ref[...]
+    m, core = s.m, s.core
+    width = w_ref.shape[1]
+    cut = min(512, width)
+
+    def one(j, _):
+        k = near(n - 1 - j, m, n)
+        for a in range(0, width, cut):
+            s.side_out[k, :, a:a + cut] = dot_nn(mixed_ref[2 * k + 1 - core], w_ref[:, a:a + cut]).astype(jnp.bfloat16)
+        s.side(k).start()
+        for a in range(0, width, cut):
+            acc_ref[:, a:a + cut] = dot_nn(mixed_ref[2 * k + core], w_ref[:, a:a + cut])
+        pl.when(j < n - 1)(lambda: s.pass_on(k, acc_ref, lambda p: g.arrive(j + 1, p)))
+        return 0
+
+    lax.fori_loop(0, n, one, 0)
+
+    def consume(at, total):
+        middle = x_ref[at, :].astype(jnp.float32) + total
+        middle_ref[at, :] = middle
+        normed_ref[at, :] = norm_forward(middle, norm_ref[2:3, :], norm_ref[3:4, :]).astype(jnp.bfloat16)
+
+    s.settle(acc_ref, consume)
+    for k in range(n):
+        g.side_wait(k)
+    g.finish()
+    s.finish()
+
+
+def out_branch(mixed, w, x, norms, cot, n, number, pieces=4):
+    rows, width = x.shape
+    return pl.pallas_call(functools.partial(out_kernel, n, pieces),
+        out_shape=(jax.ShapeDtypeStruct((rows, width), jnp.float32), jax.ShapeDtypeStruct((rows, width), jnp.bfloat16),
+                   jax.ShapeDtypeStruct((2 * n, rows, width), jnp.bfloat16)),
+        in_specs=[VM] * 5, out_specs=(VM,) * 3,
+        scratch_shapes=[pltpu.VMEM((rows, width), jnp.float32)] + scatter_scratch(n, pieces, rows, width) + [pltpu.SemaphoreType.DMA((5, n * pieces))],
+        compiler_params=params(number),
+        cost_estimate=lasting(115), name="out_branch")(mixed.reshape(2 * n, rows, mixed.shape[1]), w, x, norms, cot)
+
+
+def mlp_kernel(n, pieces, x_ref, cots_ref, gate_up_ref, down_ref, middle_ref, norm_ref,
+               xs_ref, hidden_ref, grads_ref, grad_middle_ref, low_ref, sums_ref,
+               acc_ref, side_out, side_in, line_in, side_sems, line_send, line_recv, gather_sems):
+    greet(n)
+    g = Gather(n, x_ref, xs_ref, gather_sems, pieces)
+    s = Scatter(n, pieces, side_out, side_in, line_in, side_sems, line_send, line_recv)
+    g.start()
+    xs_ref[g.t] = x_ref[...]
+    m, core = s.m, s.core
+
+    def work(slot):
+        x = xs_ref[slot]
+        gate = dot_nn(x, gate_up_ref[0])
+        up = dot_nn(x, gate_up_ref[1])
+        grad_hidden = dot_nt(cots_ref[slot], down_ref[...])
+        sig = 1.0 / (1.0 + jnp.exp(-gate))
+        silu = gate * sig
+        hidden_ref[slot] = (silu * up).astype(jnp.bfloat16)
+        grads_ref[0, slot] = (grad_hidden * up * (sig * (1.0 + gate * (1.0 - sig)))).astype(jnp.bfloat16)
+        grads_ref[1, slot] = (grad_hidden * silu).astype(jnp.bfloat16)
+
+    def ring(d, _):
+        pl.when(d > 0)(lambda: g.arrive(d))
+
+        def one(q, _):
+            other, above = lax.div(q, 2), lax.rem(q, 2)
+            k = jnp.where(above == 1, m + d, m - d)
+
+            @pl.when((k >= 0) & (k < n) & ((d > 0) | (above == 0)))
+            def _():
+                pl.when(other == 1)(lambda: g.side_wait(k))
+                work(2 * k + jnp.where(other == 1, 1 - core, core))
+
+            return 0
+
+        lax.fori_loop(0, 4, one, 0)
+        return 0
+
+    lax.fori_loop(0, n, ring, 0)
+    width = x_ref.shape[1]
+    cut = min(512, width)
+
+    def one(j, _):
+        k = near(n - 1 - j, m, n)
+
+        def partial(slot, a):
+            return dot_nt(grads_ref[0, slot], gate_up_ref[0, a:a + cut, :]) + dot_nt(grads_ref[1, slot], gate_up_ref[1, a:a + cut, :])
+
+        for a in range(0, width, cut):
+            s.side_out[k, :, a:a + cut] = partial(2 * k + 1 - core, a).astype(jnp.bfloat16)
+        s.side(k).start()
+        for a in range(0, width, cut):
+            acc_ref[:, a:a + cut] = partial(2 * k + core, a)
+        pl.when(j < n - 1)(lambda: s.pass_on(k, acc_ref))
+        return 0
+
+    lax.fori_loop(0, n, one, 0)
+    sums_ref[...] = jnp.zeros(sums_ref.shape, jnp.float32)
+
+    def consume(at, total):
+        back, gain, shift = norm_backward(middle_ref[at, :], norm_ref[2:3, :], total)
+        result = cots_ref[s.t, at, :].astype(jnp.float32) + back
+        grad_middle_ref[at, :] = result
+        low_ref[at, :] = result.astype(jnp.bfloat16)
+        sums_ref[0:1, :] += gain
+        sums_ref[1:2, :] += shift
+
+    s.settle(acc_ref, consume)
+    g.finish()
+    s.finish()
+
+
+def mlp(x, cots, gate_up, down, middle, norms, n, number, pieces=4):
+    rows, width = x.shape
+    hidden = down.shape[0]
+    f32, low = jnp.float32, jnp.bfloat16
+    return pl.pallas_call(functools.partial(mlp_kernel, n, pieces),
+        out_shape=(jax.ShapeDtypeStruct((2 * n, rows, width), low), jax.ShapeDtypeStruct((2 * n, rows, hidden), low),
+                   jax.ShapeDtypeStruct((2, 2 * n, rows, hidden), low), jax.ShapeDtypeStruct((rows, width), f32),
+                   jax.ShapeDtypeStruct((rows, width), low), jax.ShapeDtypeStruct((2, width), f32)),
+        in_specs=[VM] * 6, out_specs=(VM,) * 6,
+        scratch_shapes=[pltpu.VMEM((rows, width), f32)] + scatter_scratch(n, pieces, rows, width) + [pltpu.SemaphoreType.DMA((5, n * pieces))],
+        compiler_params=params(number), cost_estimate=lasting(165), name="mlp")(x, cots, gate_up, down, middle, norms)
+
+
+def down_kernel(n, pieces, hidden_ref, down_ref, middle_ref, x_ref, out_ref, block_ref, xs_ref, back_ref,
+                acc_ref, side_out, side_in, line_in, side_sems, line_send, line_recv, gather_sems):
+    greet(n)
+    g = Gather(n, x_ref, xs_ref, gather_sems, pieces)
+    s = Scatter(n, pieces, side_out, side_in, line_in, side_sems, line_send, line_recv)
+    g.start()
+    xs_ref[g.t] = x_ref[...]
+    m, core = s.m, s.core
+    width = down_ref.shape[1]
+    cut = min(512, width)
+
+    def one(j, _):
+        k = near(n - 1 - j, m, n)
+        for a in range(0, width, cut):
+            s.side_out[k, :, a:a + cut] = dot_nn(hidden_ref[2 * k + 1 - core], down_ref[:, a:a + cut]).astype(jnp.bfloat16)
+        s.side(k).start()
+        for a in range(0, width, cut):
+            acc_ref[:, a:a + cut] = dot_nn(hidden_ref[2 * k + core], down_ref[:, a:a + cut])
+        pl.when(j < n - 1)(lambda: s.pass_on(k, acc_ref, lambda p: g.arrive(j + 1, p)))
+        return 0
+
+    lax.fori_loop(0, n, one, 0)
+
+    def consume(at, total):
+        block_ref[at, :] = (middle_ref[at, :] + total).astype(jnp.bfloat16)
+
+    s.settle(acc_ref, consume)
+
+    def last(k, _):
+        g.side_wait(k)
+        for c in range(2):
+            back_ref[2 * k + c] = dot_nt(xs_ref[2 * k + c], out_ref[...]).astype(jnp.bfloat16)
+        return 0
+
+    lax.fori_loop(0, n, last, 0)
+    g.finish()
+    s.finish()
+
+
+def down_branch(hidden, down, middle, x, out, n, number, pieces=4):
+    rows, width = x.shape
+    f32, low = jnp.float32, jnp.bfloat16
+    return pl.pallas_call(functools.partial(down_kernel, n, pieces),
+        out_shape=(jax.ShapeDtypeStruct((rows, width), low), jax.ShapeDtypeStruct((2 * n, rows, width), low),
+                   jax.ShapeDtypeStruct((2 * n, rows, out.shape[0]), low)),
+        in_specs=[VM] * 5, out_specs=(VM,) * 3,
+        scratch_shapes=[pltpu.VMEM((rows, width), f32)] + scatter_scratch(n, pieces, rows, width) + [pltpu.SemaphoreType.DMA((5, n * pieces))],
+        compiler_params=params(number), cost_estimate=lasting(115), name="down_branch")(hidden, down, middle, x, out)
+
+
+def first_kernel(n, pieces, grad_ref, w_ref, x_ref, middle_ref, norm_ref, result_ref, sums_ref,
+                 acc_ref, side_out, side_in, line_in, side_sems, line_send, line_recv):
+    greet(n)
+    s = Scatter(n, pieces, side_out, side_in, line_in, side_sems, line_send, line_recv)
+    m, core = s.m, s.core
+    width = w_ref.shape[0]
+    cut = min(512, width)
+
+    def one(j, _):
+        k = near(n - 1 - j, m, n)
+        for a in range(0, width, cut):
+            s.side_out[k, :, a:a + cut] = dot_nt(grad_ref[2 * k + 1 - core], w_ref[a:a + cut, :]).astype(jnp.bfloat16)
+        s.side(k).start()
+        for a in range(0, width, cut):
+            acc_ref[:, a:a + cut] = dot_nt(grad_ref[2 * k + core], w_ref[a:a + cut, :])
+        pl.when(j < n - 1)(lambda: s.pass_on(k, acc_ref))
+        return 0
+
+    lax.fori_loop(0, n, one, 0)
+    sums_ref[...] = jnp.zeros(sums_ref.shape, jnp.float32)
+
+    def consume(at, total):
+        back, gain, shift = norm_backward(x_ref[at, :].astype(jnp.float32), norm_ref[0:1, :], total)
+        result_ref[at, :] = middle_ref[at, :] + back
+        sums_ref[0:1, :] += gain
+        sums_ref[1:2, :] += shift
+
+    s.settle(acc_ref, consume)
+    s.finish()
+
+
+def first_branch(grad, w, x, grad_middle, norms, n, number, pieces=4):
+    rows, width = x.shape
+    f32 = jnp.float32
+    return pl.pallas_call(functools.partial(first_kernel, n, pieces),
+        out_shape=(jax.ShapeDtypeStruct((rows, width), f32), jax.ShapeDtypeStruct((2, width), f32)),
+        in_specs=[VM] * 5, out_specs=(VM,) * 2,
+        scratch_shapes=[pltpu.VMEM((rows, width), f32)] + scatter_scratch(n, pieces, rows, width),
+        compiler_params=params(number), cost_estimate=lasting(85), name="first_branch")(grad.reshape(2 * n, rows, grad.shape[1]), w, x, grad_middle, norms)
+
+
+def total_kernel(x_ref, out_ref, parts, groups, send_one, recv_one, send_two, recv_two, send_three, recv_three):
+    t, g = lax.axis_index("tensor"), lax.axis_index("dp")
+    count, group_count = parts.shape[0], groups.shape[0]
+    barrier = pltpu.get_barrier_semaphore()
+    for j in range(count):
+        pl.when(j != t)(lambda: pl.semaphore_signal(barrier, inc=1, device_id={"tensor": j}, device_id_type=MESH))
+    for i in range(group_count):
+        pl.when(i != g)(lambda: pl.semaphore_signal(barrier, inc=1, device_id={"dp": i}, device_id_type=MESH))
+    pl.semaphore_wait(barrier, count + group_count - 2)
+
+    def spread(src, dst, send, recv, at, axis, peer):
+        return pltpu.make_async_remote_copy(
+            src_ref=src, dst_ref=dst, send_sem=send.at[peer], recv_sem=recv.at[at], device_id={axis: peer}, device_id_type=MESH)
+
+    def exchange(me, size, make, stay):
+        for j in range(size):
+            pl.when(j != me)(lambda: make(j, me).start())
+        stay()
+        for j in range(size):
+            pl.when(j != me)(lambda: make(j, j).wait_recv())
+        for j in range(size):
+            pl.when(j != me)(lambda: make(j, me).wait_send())
+
+    def keep_one():
+        parts[t] = x_ref[t]
+
+    def keep_two():
+        groups[g] = sum_of(parts)
+
+    def sum_of(ref):
+        total = ref[0]
+        for j in range(1, ref.shape[0]):
+            total = total + ref[j]
+        return total
+
+    exchange(t, count, lambda j, at: spread(x_ref.at[j], parts.at[at], send_one, recv_one, at, "tensor", j), keep_one)
+    keep_two()
+    exchange(g, group_count, lambda j, at: spread(groups.at[g], groups.at[at], send_two, recv_two, at, "dp", j), lambda: None)
+    out_ref[t] = sum_of(groups)
+    exchange(t, count, lambda j, at: spread(out_ref.at[t], out_ref.at[at], send_three, recv_three, at, "tensor", j), lambda: None)
+
+
+def total_over_all(x, count, group_count, number):
+    rows, width = x.shape
+    piece = width // count
+    shape = jax.ShapeDtypeStruct((count, rows, piece), x.dtype)
+    out = pl.pallas_call(
+        total_kernel, out_shape=shape, in_specs=[VM], out_specs=VM,
+        scratch_shapes=[
+            pltpu.VMEM((count, rows, piece), x.dtype), pltpu.VMEM((group_count, rows, piece), x.dtype),
+            pltpu.SemaphoreType.DMA((count,)), pltpu.SemaphoreType.DMA((count,)),
+            pltpu.SemaphoreType.DMA((group_count,)), pltpu.SemaphoreType.DMA((group_count,)),
+            pltpu.SemaphoreType.DMA((count,)), pltpu.SemaphoreType.DMA((count,)),
+        ],
+        compiler_params=params(number), cost_estimate=lasting(12), name="total_over_all",
+    )(jnp.transpose(x.reshape(rows, count, piece), (1, 0, 2)))
+    return jnp.transpose(out, (1, 0, 2)).reshape(rows, width)
 
 
 def local(
@@ -341,6 +851,7 @@
     heads_here = bias_master.shape[1]
     width_here = heads_here * HEAD_DIM
     own_start = lax.axis_index("tensor") * local_tokens
+    chips = tensor_count // 2
     qkv_copy, gate_up_copy, out_copy, down_copy, bias_copy = (
         lax.all_gather(qkv_master.astype(jnp.bfloat16), "dp", axis=1, tiled=True),
         lax.all_gather(gate_up_master.astype(jnp.bfloat16), "dp", axis=1, tiled=True),
@@ -351,7 +862,7 @@
     qkv_flat = jnp.transpose(qkv_copy, (1, 0, 2)).reshape(qkv_copy.shape[1], 3 * width_here)
     inputs_wide = inputs.astype(jnp.float32)
     normed_one = norm_forward(inputs_wide, norm_master[0], norm_master[1]).astype(jnp.bfloat16)
-    gathered_one = lax.all_gather(normed_one, "tensor", axis=0, tiled=True)
+    gathered_one = gather(normed_one, chips, 0).reshape(group_tokens, D)
     projected = jnp.dot(
         gathered_one, qkv_flat, preferred_element_type=jnp.float32
     ) + bias_copy.reshape(1, 3 * width_here).astype(jnp.float32)
@@ -359,48 +870,33 @@
     queries, keys, values, keys_flipped, mixed_low, log_totals = attention_forward(
         lengths, projected, keep, ahead, behind, heads_here, block_rows
     )
-    rows_part = mixed_low
-    branch_one = sum_rows(jnp.dot(rows_part, out_copy, preferred_element_type=jnp.float32))
-    middle = inputs_wide + branch_one
-    normed_two = norm_forward(middle, norm_master[2], norm_master[3]).astype(jnp.bfloat16)
-    gathered_two = lax.all_gather(normed_two, "tensor", axis=0, tiled=True)
-    gate_up = jnp.einsum(
-        "td,cdf->ctf", gathered_two, gate_up_copy, preferred_element_type=jnp.float32
-    )
-    hidden_wide, swiglu_pull = jax.vjp(swiglu, gate_up[0], gate_up[1])
-    hidden = hidden_wide.astype(jnp.bfloat16)
-    rows_part = hidden
-    branch_two = sum_rows(jnp.dot(rows_part, down_copy, preferred_element_type=jnp.float32))
-    block_output = (middle + branch_two).astype(jnp.bfloat16)
     group_index = own_start + jnp.arange(local_tokens, dtype=jnp.int32)
     row_of = group_index // row_length
     slot_of = group_index % row_length
     row_match = row_of[:, None] == jnp.arange(row_count, dtype=jnp.int32)[None, :]
     length_of = jnp.sum(jnp.where(row_match, lengths[None, :], 0), axis=1)
-    valid = (slot_of < length_of).astype(jnp.float32)
-    grad_result = cotangent.astype(jnp.float32) * valid[:, None]
-    gathered_grad = lax.all_gather(grad_result.astype(jnp.bfloat16), "tensor", axis=0, tiled=True)
+    valid = slot_of < length_of
+    grad_low = jnp.where(valid[:, None], cotangent, jnp.zeros_like(cotangent))
+    middle, normed_two, gathered_grad = out_branch(mixed_low, out_copy, inputs, norm_master, grad_low, chips, 1)
+    gathered_two, hidden, grad_gate_up, grad_middle, grad_middle_low, sums_two = mlp(
+        normed_two, gathered_grad, gate_up_copy, down_copy, middle, norm_master, chips, 2
+    )
+    block_output, gathered_mid, grad_mixed = down_branch(
+        hidden, down_copy, middle, grad_middle_low, out_copy, chips, 3
+    )
+    hidden = hidden.reshape(group_tokens, hidden.shape[2])
+    grad_gate_up = grad_gate_up.reshape(2, group_tokens, hidden.shape[1])
+    gathered_grad = gathered_grad.reshape(group_tokens, D)
+    gathered_two = gathered_two.reshape(group_tokens, D)
+    gathered_mid = gathered_mid.reshape(group_tokens, D)
+    grad_mixed = grad_mixed.reshape(group_tokens, width_here)
     grad_down = jnp.einsum("tf,td->fd", hidden, gathered_grad, preferred_element_type=jnp.float32)
-    grad_hidden = jnp.einsum(
-        "td,fd->tf", gathered_grad, down_copy, preferred_element_type=jnp.float32
-    )
-    grad_gate, grad_up = swiglu_pull(grad_hidden)
-    grad_gate_up = jnp.stack([grad_gate, grad_up]).astype(jnp.bfloat16)
     grad_gate_up_w = jnp.einsum(
         "td,ctf->cdf", gathered_two, grad_gate_up, preferred_element_type=jnp.float32
     )
-    rows_part = grad_gate_up
-    grad_normed_two = sum_rows(jnp.einsum("ctf,cdf->td", rows_part, gate_up_copy, preferred_element_type=jnp.float32))
-    grad_middle_norm, gain_two, shift_two = norm_backward(middle, norm_master[2], grad_normed_two)
-    grad_middle = grad_result + grad_middle_norm
-    gathered_mid = lax.all_gather(grad_middle.astype(jnp.bfloat16), "tensor", axis=0, tiled=True)
     grad_out_w = jnp.einsum(
         "tw,td->wd", mixed_low, gathered_mid, preferred_element_type=jnp.float32
     )
-    grad_mixed = jnp.einsum(
-        "td,wd->tw", gathered_mid, out_copy, preferred_element_type=jnp.float32
-    ).astype(jnp.bfloat16)
-
     grad_projected, grad_bias = attention_backward(
         lengths, queries, keys, values, keys_flipped, mixed_low, log_totals, grad_mixed, keep, ahead, behind, block_rows
     )
@@ -411,13 +907,12 @@
         grad_projected.reshape(group_tokens, 3, width_here),
         preferred_element_type=jnp.float32,
     )
-    rows_part = grad_projected
-    grad_normed_one = sum_rows(jnp.einsum("tc,dc->td", rows_part, qkv_flat, preferred_element_type=jnp.float32))
-    grad_input_norm, gain_one, shift_one = norm_backward(
-        inputs_wide, norm_master[0], grad_normed_one
-    )
-    input_grad = grad_middle + grad_input_norm
-    norm_grads = lax.psum(jnp.stack([gain_one, shift_one, gain_two, shift_two]), ("dp", "tensor"))
+    input_grad, sums_one = first_branch(
+        grad_projected, qkv_flat, inputs, grad_middle, norm_master, chips, 4
+    )
+    norm_grads = total_over_all(
+        jnp.concatenate([sums_one, sums_two], axis=0), tensor_count, lax.axis_size("dp"), 5
+    )
     qkv_grad, gate_up_grad, out_grad, down_grad, bias_grad = (
         sum_shard(grad_qkv_w, 1),
         sum_shard(grad_gate_up_w, 1),

time: 1230 us -> 882 us (0.72)
  waiting for transfers between devices: 777 us -> 0.18 us
  Pallas kernels: 120 us -> 701 us
  matrix products: 147 us -> 57.5 us
  blocking collectives: 57.7 us -> 16.1 us
  other arithmetic: 55.7 us -> 38.4 us
    pallas_call x0 -> x6, Pallas kernels: none -> 580 us  [the longest x1 171 us: mlp(): pl.pallas_call(functools.partial(mlp_kernel, n, pieces), out_shape=(jax.S...]
    reduce_scatter x4 -> x0, waiting for transfers between devices: 327 us -> none  [sum_rows(): lax.psum_scatter(partial.astype(jnp.bfloat16), 'tensor', scatter_dimensio...]
    all_gather x4 -> x0, waiting for transfers between devices: 305 us -> none  [the longest x1 84.3 us: local(): gathered_one = lax.all_gather(normed_one, 'tensor', axis=0, tiled=True)]
    dot_general x7 -> x0, matrix products: 88.2 us -> none  [the longest x1 19.2 us: local(): jnp.einsum('td,cdf->ctf', gathered_two, gate_up_copy, preferred_element_t...]
    all_gather x1, waiting for transfers between devices: 58.4 us -> 0.02 us  [local(): lax.all_gather(gate_up_master.astype(jnp.bfloat16), 'dp', axis=1, tiled=T...]
    reduce_scatter x4, waiting for transfers between devices: 51.1 us -> 0.01 us  [sum_shard(): lax.psum_scatter(gradient.astype(jnp.bfloat16), 'dp', scatter_dimension=d...]
    psum x1 -> x0, blocking collectives: 37.9 us -> none  [local(): lax.psum(jnp.stack([gain_one, shift_one, gain_two, shift_two]), ('dp', 't...]
    all_gather x1, waiting for transfers between devices: 23.4 us -> 0.02 us  [local(): lax.all_gather(down_master.astype(jnp.bfloat16), 'dp', axis=1, tiled=True)]
  transfers between devices with their start and end apart: 16 -> 8, of which waited for: 13 -> 0; matrix products, arithmetic and copies ran while one was open for 15% -> 13% of each run, Pallas kernels for 10% -> 48%
where the time goes in v2:
time: 882 us; the launch traced here: 872 us
  Pallas kernels  701 us (79%)
  matrix products  57.5 us (7%)
  local copies, waits for them, and re-layouts  41.9 us (5%)
  other arithmetic  38.4 us (4%)
  between operations  16.3 us (2%)
  blocking collectives  16.1 us (2%)
    pallas_call x1, Pallas kernels, mlp(): pl.pallas_call(functools.partial(mlp_kernel, n, pieces), out_shape=(jax.S...  171 us
    pallas_call x1, Pallas kernels, out_branch(): pl.pallas_call(functools.partial(out_kernel, n, pieces), out_shape=(jax.S...  114 us
    pallas_call x1, Pallas kernels, down_branch(): pl.pallas_call(functools.partial(down_kernel, n, pieces), out_shape=(jax....  112 us
    pallas_call x1, Pallas kernels, first_branch(): pl.pallas_call(functools.partial(first_kernel, n, pieces), out_shape=(jax...  90 us
    pallas_call x1, Pallas kernels, gather(): pl.pallas_call(functools.partial(gather_kernel, n, pieces), out_shape=jax...  78.9 us
    pallas_call x1, Pallas kernels, attention_forward(): pl.pallas_call(functools.partial(forward_kernel, block), out_shape=(split...  60.7 us
    pallas_call x1, Pallas kernels, attention_backward(): pl.pallas_call(functools.partial(backward_kernel, block), out_shape=(jax....  59.9 us
    sub x6, other arithmetic, adamw(): weight_old - step_rate * (update + decay_part * weight_old)  22.8 us
  transfers between devices with their start and end apart: 8, of which 0 were waited for; matrix products, arithmetic and copies ran while one was open for 13% of the time, Pallas kernels for 48%

profile of v2, /device:TPU:0, one launch (start us, length us, event | category | flops | bytes accessed | tf_op | source)
XLA Modules:
  0.0 871.9 jit_solution(14725179558677084616)
XLA Ops:
  7.2 0.0 all-gather.5.cloned.1.call-start
  7.2 1.9 copy.96
  9.1 1.0 convert_element_type.67
  10.1 0.0 all-gather.7.cloned.1.call-start
  10.2 0.4 copy-done.8
  10.6 0.7 convert_element_type.72
  11.3 0.0 all-gather.11.cloned.1.call-start
  11.4 2.5 convert_element_type.74
  13.9 0.0 all-gather.9.cloned.1.call-start
  13.9 1.3 convert_element_type.73
  15.2 2.6 copy.100
  17.9 0.0 reduce-scatter.10.cloned.1.call-start
  18.0 0.2 convert_reduce_fusion
  18.2 0.4 fusion.10
  18.7 1.4 fusion.13.x_ref
  20.1 78.9 %gather_rows.1 = bf16[8,256,2048]{2,1,0:T(8,128)(2,1)} custom-call(bf16[256,2048]{1,0:T(8,128)(2,1)} %fusion.13.x_ref), custom_call_target="tpu_custom_call" | custom-call | flops 85800001536 | tf_op jit(solution)/shard_map/gather_rows/pallas_call | solution.py:532
  99.0 0.1 copy.97
  99.1 8.4 all_gather.16
  107.5 0.1 copy.98
  107.6 0.1 reshape.154
  107.7 5.5 multiply_sine_fusion
  113.3 0.1 broadcast_in_dim.40
  113.3 0.1 broadcast_in_dim.41
  113.4 4.5 concatenate.13.ahead_ref
  117.9 4.4 concatenate.14.behind_ref
  123.0 0.1 broadcast_in_dim.39
  123.1 3.0 concatenate.12.keep_ref
  126.1 1.1 broadcast_select_fusion.cot_ref
  127.2 11.8 %broadcast_add_fusion.pre_ref = f32[2048,768]{1,0:T(8,128)} fusion(f32[768]{0:T(1024)S(1)} %reshape.154, bf16[2048,2048]{1,0:T(8,128)(2,1)} %bitcast.59, bf16[2048,768]{0,1:T(8,128)(2,1)} %bitcast.50), kind=kOutput, calls=%fused_computation.8 | convolution fusion | flops 6444023808 | bytes 17828864 | tf_op jit(solution)/shard_map/dot_general | solution.py:866
  138.9 60.7 %attention_forward.1 = (bf16[4,2048,64]{2,1,0:T(8,128)(2,1)}, bf16[4,2048,64]{2,1,0:T(8,128)(2,1)}, bf16[4,2048,64]{2,1,0:T(8,128)(2,1)}, bf16[256,2048]{1,0:T(8...) custom-call(s32[1]{0:T(128)} %copy.119.length_ref, f32[2048,768]{1,0:T(8,128)} %broadcast_add_fusion.pre_ref, ...), custom_call_target="tpu_custom_call" | custom-call | flops 8589934592 | bytes 15728640 | tf_op jit(solution)/shard_map/attention_forward/pallas_call | solution.py:186
  199.7 114.1 %out_branch.1 = (f32[256,2048]{1,0:T(8,128)}, bf16[256,2048]{1,0:T(8,128)(2,1)}, bf16[8,256,2048]{2,1,0:T(8,128)(2,1)}) custom-call(bf16[8,256,256]{2,1,0:T(8,128)(2,1)} %bitcast.54, bf16[256,2048]{1,0:T(8,128)(2,1)} %all-gather.7.cloned.1.call-done.w_ref.out_ref, bf16[256,2048]{1,0:T(8,128)(2,1)} %x_ref.3, f32[4,2048]{1,0:T(4,128)} %norm_ref.5, ...), custom_call_target="tpu_custom_call" | custom-call | flops 126500003840 | tf_op jit(solution)/shard_map/out_branch/pallas_call | solution.py:577
  313.8 170.9 %mlp.1 = (bf16[8,256,2048]{2,1,0:T(8,128)(2,1)}, bf16[8,256,704]{2,1,0:T(8,128)(2,1)}, bf16[2,8,256,704]{3,2,1,0:T(8,128)(2,1)}, f32[256,2048]{1,0:T(8,128)}, bf...) custom-call(bf16[256,2048]{1,0:T(8,128)(2,1)} %get-tuple-element.43.x_ref, bf16[8,256,2048]{2,1,0:T(8,128)(2,1)} %get-tuple-element.44.cots_ref, ...), custom_call_target="tpu_custom_call" | custom-call | flops 181500002304 | tf_op jit(solution)/shard_map/mlp/pallas_call | solution.py:662
  484.7 112.1 %down_branch.1 = (bf16[256,2048]{1,0:T(8,128)(2,1)}, bf16[8,256,2048]{2,1,0:T(8,128)(2,1)}, bf16[8,256,256]{2,1,0:T(8,128)(2,1)}) custom-call(bf16[8,256,704]{2,1,0:T(8,128)(2,1)} %get-tuple-element.46.hidden_ref, bf16[704,2048]{1,0:T(8,128)(2,1)} %all-gather.11.cloned.1.call-done.down_ref, f32[256,2048]{1,0:T(8,128)} %get-tuple-element.45.middle_ref, ...), custom_call_target="tpu_custom_call" | custom-call | flops 126500003840 | tf_op jit(solution)/shard_map/down_branch/pallas_call | solution.py:713
  596.8 6.7 convolution_convert_fusion.1
  603.5 0.2 reduce-scatter.12.cloned.1.call-start
  603.7 10.7 %bitcast_convert_fusion.1 = bf16[704,2048]{1,0:T(8,128)(2,1)} fusion(bf16[8,256,704]{2,1,0:T(8,128)(2,1)} %get-tuple-element.46.hidden_ref, bf16[8,256,2048]{2,1,0:T(8,128)(2,1)} %get-tuple-element.44.cots_ref), kind=kOutput, calls=%fused_computation.4 | convolution fusion | flops 5907021824 | bytes 14155776 | tf_op jit(solution)/shard_map/tf,td->fd/dot_general | solution.py:893
  614.4 0.0 reduce-scatter.6.cloned.1.call-start
  614.5 59.9 %attention_backward.1 = (bf16[2048,768]{1,0:T(8,128)(2,1)}, f32[1,768]{1,0:T(1,128)}) custom-call(s32[1]{0:T(128)} %copy.119.length_ref, bf16[4,2048,64]{2,1,0:T(8,128)(2,1)} %get-tuple-element.49.q_ref, bf16[4,2048,64]{2,1,0:T(8,128)(2,1)} %get-tuple-element.50.k_ref, bf16[4,2048,64]{2,1,0:T(8,128)(2,1)} %get-tuple-element.51.v_ref, ...), custom_call_target="tpu_custom_call" | custom-call | flops 21474836480 | bytes 15728640 | tf_op jit(solution)/shard_map/attention_backward/pallas_call | solution.py:286
  674.4 3.2 copy.103
  677.6 10.3 %fusion.5 = bf16[3,2048,256]{1,2,0:T(8,128)(2,1)} fusion(bf16[2048,3,256]{0,2,1:T(8,128)(2,1)S(1)} %bitcast.53, bf16[2048,2048,1]{1,0,2:T(8,128)(2,1)} %bitcast.60), kind=kOutput, calls=%fused_computation.9 | convolution fusion | flops 6444023808 | bytes 14680064 | tf_op jit(solution)/shard_map/td,tcw->cdw/dot_general | solution.py:904
  687.9 0.3 reduce-scatter.8.cloned.1.call-start
  688.1 1.1 copy-done.10
  689.3 0.5 copy.102
  689.7 3.0 copy.104
  692.8 0.6 dynamic-slice
  694.0 4.8 copy.101.w_ref
  698.8 18.2 %fusion.2 = bf16[2,2048,704]{1,2,0:T(8,128)(2,1)} fusion(bf16[2,8,256,704]{3,2,1,0:T(8,128)(2,1)} %get-tuple-element.58, bf16[8,256,2048]{2,1,0:T(8,128)(2,1)} %get-tuple-element.59), kind=kOutput, calls=%fused_computation.3 | convolution fusion | flops 11814043648 | bytes 19922944 | tf_op jit(solution)/shard_map/td,ctf->cdf/dot_general | solution.py:894
  717.1 90.0 %first_branch.1 = (f32[256,2048]{1,0:T(8,128)}, f32[2,2048]{1,0:T(2,128)}) custom-call(bf16[8,256,768]{2,1,0:T(8,128)(2,1)} %bitcast.52, bf16[2048,768]{1,0:T(8,128)(2,1)} %copy.101.w_ref, bf16[256,2048]{1,0:T(8,128)(2,1)} %x_ref.3, f32[256,2048]{1,0:T(8,128)} %get-tuple-element.56.middle_ref, f32[4,2048]{1,0:T(4,128)} %norm_ref.5), custom_call_target="tpu_custom_call" | custom-call | flops 93499998208 | tf_op jit(solution)/shard_map/first_branch/pallas_call | solution.py:755
  807.1 0.1 reshape.151
  807.2 7.7 all-reduce
  814.9 1.4 pad_maximum_fusion
  816.3 0.7 multiply_subtract_fusion.5
  817.0 14.2 %total_over_all.1 = f32[8,4,256]{2,1,0:T(4,128)} custom-call(f32[8,4,256]{2,1,0:T(4,128)} %bitcast.58), custom_call_target="tpu_custom_call" | custom-call | flops 13200000000 | tf_op jit(solution)/shard_map/total_over_all/pallas_call | solution.py:808
  831.2 1.4 multiply_subtract_fusion.4
  832.7 2.4 multiply_subtract_fusion.3
  835.1 5.4 multiply_subtract_fusion.2
  840.4 4.7 multiply_subtract_fusion.1
  845.1 3.1 copy.109
  848.3 1.6 copy.110
  849.9 3.2 copy.111
  853.1 8.3 multiply_subtract_fusion
  861.3 1.0 copy.120
  862.3 1.0 copy-done.7
  863.3 1.3 copy.121
  (75 shorter events, 0.4 us)
Async XLA Ops:
  7.2 120.0 %all-gather.5.cloned.1.call-start = ((), (), s32[]{:S(2)}) async-start(), calls=%async_computation.4 | async-start | bytes 3932160 | tf_op jit(solution)/shard_map/all_gather | solution.py:856
  9.1 2.2 copy-start
  9.1 1.4 copy-start.8
  10.1 189.5 %all-gather.7.cloned.1.call-start = ((), (), s32[]{:S(2)}) async-start(), calls=%async_computation.5 | async-start | bytes 1310720 | tf_op jit(solution)/shard_map/all_gather | solution.py:858
  11.3 302.4 %all-gather.11.cloned.1.call-start = ((), (), s32[]{:S(2)}) async-start(), calls=%async_computation.7 | async-start | bytes 3604480 | tf_op jit(solution)/shard_map/all_gather | solution.py:859
  11.4 2.6 copy-start.2
  13.9 299.9 %all-gather.9.cloned.1.call-start = ((), (), s32[]{:S(2)}) async-start(), calls=%async_computation.6 | async-start | bytes 7864320 | tf_op jit(solution)/shard_map/all_gather | solution.py:857
  15.2 2.7 copy-start.15
  15.2 2.8 copy-start.4
  17.9 814.8 %reduce-scatter.10.cloned.1.call-start = ((), (), s32[]{:S(2)}) async-start(), calls=%async_computation.10 | async-start | bytes 1310720 | tf_op jit(solution)/shard_map/reduce_scatter | solution.py:76
  20.1 78.9 %copy-start.19 = (f32[3,4,16]{2,1,0:T(4,128)S(1)}, f32[3,4,16]{2,1,0:T(4,128)}, u32[]{:S(2)}) copy-start(f32[3,4,16]{2,1,0:T(4,128)} %param.30) | copy-start | bytes 2308
  20.1 87.6 %copy-start.22 = (s32[2048]{0:T(1024)S(1)}, s32[2048]{0:T(1024)}, u32[]{:S(2)}) copy-start(s32[2048]{0:T(1024)} %param.25) | copy-start | bytes 24580
  123.1 3.0 copy-start.11
  484.7 112.1 %copy-start.6 = (bf16[2048,256]{1,0:T(8,128)(2,1)S(1)}, bf16[2048,256]{1,0:T(8,128)(2,1)}, u32[]{:S(2)}) copy-start(bf16[2048,256]{1,0:T(8,128)(2,1)} %get-tuple-element.42.o_ref) | copy-start | bytes 3145732
  603.5 231.6 %reduce-scatter.12.cloned.1.call-start = ((), (), s32[]{:S(2)}) async-start(), calls=%async_computation.11 | async-start | bytes 3604480 | tf_op jit(solution)/shard_map/reduce_scatter | solution.py:76
  614.4 226.0 %reduce-scatter.6.cloned.1.call-start = ((), (), s32[]{:S(2)}) async-start(), calls=%async_computation.8 | async-start | bytes 3932160 | tf_op jit(solution)/shard_map/reduce_scatter | solution.py:76
  687.8 1.4 copy-start.10
  687.9 165.2 %reduce-scatter.8.cloned.1.call-start = ((), (), s32[]{:S(2)}) async-start(), calls=%async_computation.9 | async-start | bytes 7208960 | tf_op jit(solution)/shard_map/reduce_scatter | solution.py:76
  689.7 3.0 copy-start.26
  717.0 90.1 %copy-start.25 = (f32[1,768]{1,0:T(1,128)S(1)}, f32[1,768]{1,0:T(1,128)}, u32[]{:S(2)}) copy-start(f32[1,768]{1,0:T(1,128)} %get-tuple-element.61) | copy-start | bytes 9220
  717.0 97.9 %copy-start.21 = (f32[2,2048]{1,0:T(2,128)S(1)}, f32[2,2048]{1,0:T(2,128)}, u32[]{:S(2)}) copy-start(f32[2,2048]{1,0:T(2,128)} %get-tuple-element.63) | copy-start | bytes 49156
  717.0 99.3 %copy-start.20 = (f32[3,4,16]{2,1,0:T(4,128)S(1)}, f32[3,4,16]{2,1,0:T(4,128)}, u32[]{:S(2)}) copy-start(f32[3,4,16]{2,1,0:T(4,128)} %param.30) | copy-start | bytes 2308
  717.0 99.2 %copy-start.23 = (f32[3,4,16]{2,1,0:T(4,128)S(1)}, f32[3,4,16]{2,1,0:T(4,128)}, u32[]{:S(2)}) copy-start(f32[3,4,16]{2,1,0:T(4,128)} %param.36) | copy-start | bytes 2308
  717.1 99.2 %copy-start.24 = (f32[3,4,16]{2,1,0:T(4,128)S(1)}, f32[3,4,16]{2,1,0:T(4,128)}, u32[]{:S(2)}) copy-start(f32[3,4,16]{2,1,0:T(4,128)} %param.42) | copy-start | bytes 2308
  817.0 14.2 %copy-start.16 = (f32[4,2048]{1,0:T(4,128)S(1)}, f32[4,2048]{1,0:T(4,128)}, u32[]{:S(2)}) copy-start(f32[4,2048]{1,0:T(4,128)} %norm_ref.5) | copy-start | bytes 98308
  817.0 14.2 %copy-start.17 = (f32[4,2048]{1,0:T(4,128)S(1)}, f32[4,2048]{1,0:T(4,128)}, u32[]{:S(2)}) copy-start(f32[4,2048]{1,0:T(4,128)} %param.37) | copy-start | bytes 98308
  817.0 14.2 %copy-start.18 = (f32[4,2048]{1,0:T(4,128)S(1)}, f32[4,2048]{1,0:T(4,128)}, u32[]{:S(2)}) copy-start(f32[4,2048]{1,0:T(4,128)} %param.43) | copy-start | bytes 98308
  817.0 15.7 %copy-start.9 = (f32[256,512]{1,0:T(8,128)S(1)}, f32[256,512]{1,0:T(8,128)}, u32[]{:S(2)}) copy-start(f32[256,512]{1,0:T(8,128)} %param.28) | copy-start | bytes 1572868
  817.0 15.7 %copy-start.13 = (f32[256,512]{1,0:T(8,128)S(1)}, f32[256,512]{1,0:T(8,128)}, u32[]{:S(2)}) copy-start(f32[256,512]{1,0:T(8,128)} %param.34) | copy-start | bytes 1572868
  817.0 15.7 %copy-start.14 = (f32[256,512]{1,0:T(8,128)S(1)}, f32[256,512]{1,0:T(8,128)}, u32[]{:S(2)}) copy-start(f32[256,512]{1,0:T(8,128)} %param.40) | copy-start | bytes 1572868
  835.1 5.4 copy-start.1
  845.1 3.1 copy-start.5
  849.9 3.2 copy-start.3
  853.1 8.3 copy-start.12
  861.3 2.0 copy-start.7
Sparse Core Ops, SparseCore 0:
  10.4 46.5 all-gather.4
  59.4 26.4 all-gather.6
  87.8 42.0 all-gather.10
  132.1 70.2 all-gather.8
  603.6 30.4 reduce-scatter.9
  637.9 41.7 reduce-scatter.11
  688.0 46.6 reduce-scatter.5
  737.9 65.7 reduce-scatter.7

commit v3 on v2

--- a/solution.py
+++ b/solution.py
@@ -26,7 +26,7 @@
 mask_fill = -1e30
 log2_e = math.log2(math.e)
 LANES = 128
-VMEM_LIMIT = 60 * 1024 * 1024
+VMEM_LIMIT = 62 * 1024 * 1024
 
 
 def norm_forward(values, gain_row, shift_row):
@@ -55,23 +55,6 @@
     )
 
 
-def rotary_tables(positions):
-    half_rot = ROTARY // 2
-    frequency = rope_base ** (-(2.0 * jnp.arange(half_rot, dtype=jnp.float32)) / ROTARY)
-    angles = positions.astype(jnp.float32)[:, None] * frequency[None, :]
-    cosine = jnp.cos(angles)
-    sine_part = jnp.sin(angles)
-    count = positions.shape[0]
-    still = HEAD_DIM - ROTARY
-    none = jnp.zeros((count, half_rot), jnp.float32)
-    rest = jnp.zeros((count, still), jnp.float32)
-    keep = [cosine, cosine, jnp.ones((count, still), jnp.float32)]
-    ahead = [-sine_part, none, rest]
-    behind = [none, sine_part, rest]
-    copies = LANES // HEAD_DIM
-    return tuple(jnp.concatenate(part * copies, axis=1) for part in (keep, ahead, behind))
-
-
 def sum_shard(gradient, dimension):
     return lax.psum_scatter(
         gradient.astype(jnp.bfloat16), "dp", scatter_dimension=dimension, tiled=True
@@ -106,96 +89,6 @@
         query_slots = query_start + lax.broadcasted_iota(jnp.int32, s.shape, 1)
         allowed = allowed & (key_slots <= query_slots)
     return jnp.where(allowed, s, mask_fill)
-
-
-def forward_kernel(block, length_ref, pre_ref, keep_ref, ahead_ref, behind_ref,
-                   q_ref, k_ref, v_ref, kt_ref, o_ref, lse_ref, vt_ref):
-    heads, rows, _ = q_ref.shape
-    width = heads * HEAD_DIM
-    groups = width // LANES
-    per_group = LANES // HEAD_DIM
-    blocks = rows // block
-    length = length_ref[0]
-
-    def prepare(i, _):
-        at = pl.ds(pl.multiple_of(i * block, block), block)
-        keep, ahead, behind = keep_ref[at, :], ahead_ref[at, :], behind_ref[at, :]
-        for g in range(groups):
-            lanes = slice(g * LANES, (g + 1) * LANES)
-            q = spin(pre_ref[at, g * LANES:(g + 1) * LANES], keep, ahead, behind)
-            k = spin(pre_ref[at, width + g * LANES:width + (g + 1) * LANES], keep, ahead, behind)
-            v = pre_ref[at, 2 * width + g * LANES:2 * width + (g + 1) * LANES]
-            kt_ref[lanes, at] = k.T.astype(jnp.bfloat16)
-            vt_ref[lanes, at] = v.T.astype(jnp.bfloat16)
-            for p in range(per_group):
-                cut = slice(p * HEAD_DIM, (p + 1) * HEAD_DIM)
-                q_ref[g * per_group + p, at, :] = q[:, cut].astype(jnp.bfloat16)
-                k_ref[g * per_group + p, at, :] = k[:, cut].astype(jnp.bfloat16)
-                v_ref[g * per_group + p, at, :] = v[:, cut].astype(jnp.bfloat16)
-        return 0
-
-    lax.fori_loop(0, blocks, prepare, 0)
-    full_blocks = length // block
-    used_blocks = (length + block - 1) // block
-
-    def query_block(i, _):
-        at = pl.ds(pl.multiple_of(i * block, block), block)
-        queries = [q_ref[h, at, :] for h in range(heads)]
-
-        def key_block(j, carry, kind):
-            key_start = pl.multiple_of(j * block, block)
-            keys_at = pl.ds(key_start, block)
-            out = []
-            for h in range(heads):
-                top, total, mixed = carry[h]
-                s = dot_nt(k_ref[h, keys_at, :], queries[h]) * (score_scale * log2_e)
-                if kind > 0:
-                    s = masked_scores(s, key_start, i * block, length, kind == 2)
-                new_top = jnp.maximum(top, jnp.max(s, axis=0, keepdims=True))
-                shrink = jnp.exp2(top - new_top)
-                p = jnp.exp2(s - new_top)
-                total = total * shrink + jnp.sum(p, axis=0, keepdims=True)
-                mixed = mixed * shrink + dot_nn(
-                    vt_ref[h * HEAD_DIM:(h + 1) * HEAD_DIM, keys_at], p.astype(jnp.bfloat16))
-                out.append((new_top, total, mixed))
-            return tuple(out)
-
-        start = tuple(
-            (jnp.full((1, block), mask_fill, jnp.float32), jnp.zeros((1, block), jnp.float32),
-             jnp.zeros((HEAD_DIM, block), jnp.float32)) for _ in range(heads))
-        plain = jnp.minimum(i, full_blocks)
-        carry = lax.fori_loop(0, plain, lambda j, c: key_block(j, c, 0), start)
-        carry = lax.fori_loop(plain, jnp.minimum(i, used_blocks), lambda j, c: key_block(j, c, 1), carry)
-        carry = key_block(i, carry, 2)
-        for h in range(heads):
-            top, total, mixed = carry[h]
-            lse_ref[h:h + 1, at] = top + jnp.log2(total)
-        for g in range(groups):
-            pair = [carry[g * per_group + p][2] * (1.0 / carry[g * per_group + p][1]) for p in range(per_group)]
-            o_ref[at, g * LANES:(g + 1) * LANES] = jnp.concatenate(pair, axis=0).T.astype(jnp.bfloat16)
-        return 0
-
-    lax.fori_loop(0, blocks, query_block, 0)
-
-
-def attention_forward(lengths, projected, keep, ahead, behind, heads, block):
-    rows = projected.shape[0]
-    width = heads * HEAD_DIM
-    vm = pl.BlockSpec(memory_space=pltpu.VMEM)
-    split = jax.ShapeDtypeStruct((heads, rows, HEAD_DIM), jnp.bfloat16)
-    return pl.pallas_call(
-        functools.partial(forward_kernel, block),
-        out_shape=(split, split, split,
-                   jax.ShapeDtypeStruct((width, rows), jnp.bfloat16),
-                   jax.ShapeDtypeStruct((rows, width), jnp.bfloat16),
-                   jax.ShapeDtypeStruct((heads, rows), jnp.float32)),
-        in_specs=[pl.BlockSpec(memory_space=pltpu.SMEM)] + [vm] * 4,
-        out_specs=(vm,) * 6,
-        scratch_shapes=[pltpu.VMEM((width, rows), jnp.bfloat16)],
-        compiler_params=pltpu.CompilerParams(vmem_limit_bytes=VMEM_LIMIT),
-        cost_estimate=pl.CostEstimate(flops=heads * rows * rows * HEAD_DIM * 8, bytes_accessed=rows * width * 30, transcendentals=heads * rows * rows),
-        name="attention_forward",
-    )(lengths, projected, keep, ahead, behind)
 
 
 def backward_kernel(block, length_ref, q_ref, k_ref, v_ref, kt_ref, o_ref, lse_ref, do_ref,
@@ -515,50 +408,186 @@
     ]
 
 
-def gather_kernel(n, pieces, x_ref, g_ref, sems):
-    greet(n)
-    g = Gather(n, x_ref, g_ref, sems, pieces)
-    g.start()
-    g_ref[g.t] = x_ref[...]
-    for d in range(1, n):
-        g.arrive(d)
-    for k in range(n):
-        g.side_wait(k)
-    g.finish()
-
-
-def gather(x, n, number, pieces=4):
-    rows, d = x.shape
-    return pl.pallas_call(functools.partial(gather_kernel, n, pieces),
-        out_shape=jax.ShapeDtypeStruct((2 * n, rows, d), x.dtype),
-        in_specs=[VM], out_specs=VM,
-        scratch_shapes=[pltpu.SemaphoreType.DMA((5, n * pieces))],
-        compiler_params=params(number),
-        cost_estimate=lasting(78), name="gather_rows")(x)
-
-
-def out_kernel(n, pieces, mixed_ref, w_ref, x_ref, norm_ref, cot_ref, middle_ref, normed_ref, cots_ref,
-               acc_ref, side_out, side_in, line_in, side_sems, line_send, line_recv, gather_sems):
-    greet(n)
-    g = Gather(n, cot_ref, cots_ref, gather_sems, pieces)
+def greet_all(n, group_count):
+    t, core, chip = place()
+    g = lax.axis_index("dp")
+    barrier = pltpu.get_barrier_semaphore()
+
+    def hail(index):
+        pl.semaphore_signal(barrier, inc=1, device_id={"tensor": index}, device_id_type=MESH)
+
+    hail(t + 1 - 2 * core)
+    pl.when(chip > 0)(lambda: hail(t - 2))
+    pl.when(chip < n - 1)(lambda: hail(t + 2))
+    for i in range(group_count):
+        pl.when(i != g)(lambda: pl.semaphore_signal(barrier, inc=1, device_id={"dp": i}, device_id_type=MESH))
+    pl.semaphore_wait(barrier, group_count + jnp.minimum(chip, 1) + jnp.minimum(n - 1 - chip, 1))
+
+
+def forward_kernel(n, group_count, pieces, length_ref, place_ref, frequency_ref, x_ref, norm_ref, qkv_ref, out_ref, bias_ref, cot_ref,
+                   xs_ref, wq_ref, wo_ref, q_ref, k_ref, v_ref, kt_ref, mixed_ref, lse_ref, keep_ref, ahead_ref, behind_ref,
+                   middle_ref, normed_ref, cots_ref,
+                   vt_ref, biases_ref, acc_ref, side_out, side_in, line_in, side_sems, line_send, line_recv,
+                   first_sems, cot_sems, share_send, share_recv):
+    greet_all(n, group_count)
+    heads, total_rows, _ = q_ref.shape
+    rows, features = x_ref.shape
+    width = heads * HEAD_DIM
+    lane_groups = width // LANES
+    per_group = LANES // HEAD_DIM
+    block = rows
+    length = length_ref[0]
+    group = lax.axis_index("dp")
+    t, core, m = place()
+    first = Gather(n, xs_ref.at[t], xs_ref, first_sems, pieces)
+    cots = Gather(n, cot_ref, cots_ref, cot_sems, pieces)
     s = Scatter(n, pieces, side_out, side_in, line_in, side_sems, line_send, line_recv)
-    g.start()
-    cots_ref[g.t] = cot_ref[...]
-    m, core = s.m, s.core
-    width = w_ref.shape[1]
-    cut = min(512, width)
-
-    def one(j, _):
+    step = 32
+
+    def first_norm(i, _):
+        at = pl.ds(pl.multiple_of(i * step, step), step)
+        xs_ref[t, at, :] = norm_forward(x_ref[at, :].astype(jnp.float32), norm_ref[0:1, :], norm_ref[1:2, :]).astype(jnp.bfloat16)
+        return 0
+
+    lax.fori_loop(0, rows // step, first_norm, 0)
+    first.start()
+    depth = features // group_count
+    mine = pl.ds(pl.multiple_of(group * depth, depth), depth)
+    for c in range(3):
+        wq_ref[c, mine, :] = qkv_ref[c].astype(jnp.bfloat16)
+    wo_ref[:, mine] = out_ref[...].astype(jnp.bfloat16)
+    biases_ref[group] = bias_ref[...].astype(jnp.bfloat16).astype(jnp.float32)
+
+    def share(kind, src, owner, peer):
+        ref = src(owner)
+        return pltpu.make_async_remote_copy(
+            src_ref=ref, dst_ref=ref, send_sem=share_send.at[kind, peer], recv_sem=share_recv.at[kind, owner],
+            device_id={"dp": peer}, device_id_type=MESH)
+
+    def part(owner):
+        return pl.ds(pl.multiple_of(owner * depth, depth), depth)
+
+    kinds = (lambda o: wq_ref.at[:, part(o), :], lambda o: biases_ref.at[o], lambda o: wo_ref.at[:, part(o)])
+    for kind in range(3):
+        for i in range(group_count):
+            pl.when(i != group)(lambda: share(kind, kinds[kind], group, i).start())
+
+    def tables(i, _):
+        at = pl.ds(pl.multiple_of(i * block, block), block)
+        angles = jnp.broadcast_to(place_ref[:, at], (LANES, block)).T * frequency_ref[...]
+        cosine, sine = jnp.cos(angles), jnp.sin(angles)
+        dim = lax.rem(lax.broadcasted_iota(jnp.int32, (block, LANES), 1), HEAD_DIM)
+        none = jnp.zeros((block, LANES), jnp.float32)
+        keep_ref[at, :] = jnp.where(dim < ROTARY, cosine, 1.0)
+        ahead_ref[at, :] = jnp.where(dim < ROTARY // 2, -sine, none)
+        behind_ref[at, :] = jnp.where((dim >= ROTARY // 2) & (dim < ROTARY), sine, none)
+        return 0
+
+    lax.fori_loop(0, total_rows // block, tables, 0)
+    def project(slot):
+        at = pl.ds(pl.multiple_of(slot * block, block), block)
+        keep, ahead, behind = keep_ref[at, :], ahead_ref[at, :], behind_ref[at, :]
+        x = xs_ref[slot]
+        for c in range(3):
+            wide = dot_nn(x, wq_ref[c]) + biases_ref[group_count, c:c + 1, :]
+            for a in range(lane_groups):
+                lanes = slice(a * LANES, (a + 1) * LANES)
+                part_wide = wide[:, lanes]
+                if c < 2:
+                    part_wide = spin(part_wide, keep, ahead, behind)
+                if c == 1:
+                    kt_ref[lanes, at] = part_wide.T.astype(jnp.bfloat16)
+                if c == 2:
+                    vt_ref[lanes, at] = part_wide.T.astype(jnp.bfloat16)
+                for b in range(per_group):
+                    (q_ref, k_ref, v_ref)[c][a * per_group + b, at, :] = part_wide[:, b * HEAD_DIM:(b + 1) * HEAD_DIM].astype(jnp.bfloat16)
+
+    def ring(d, _):
+        def one(q, _):
+            other, above = lax.div(q, 2), lax.rem(q, 2)
+            k = jnp.where(above == 1, m + d, m - d)
+
+            @pl.when((k >= 0) & (k < n) & ((d > 0) | (above == 0)))
+            def _():
+                pl.when(other == 1)(lambda: first.side_wait(k))
+                project(2 * k + jnp.where(other == 1, 1 - core, core))
+
+            return 0
+
+        lax.fori_loop(0, 4, one, 0)
+        pl.when(d == n - 2)(lambda: first.arrive(n - 1))
+        return 0
+
+    for d in range(1, n - 1):
+        first.arrive(d)
+    for kind in range(3):
+        for i in range(group_count):
+            pl.when(i != group)(lambda: share(kind, kinds[kind], i, i).wait_recv())
+    bias = biases_ref[0]
+    for i in range(1, group_count):
+        bias = bias + biases_ref[i]
+    biases_ref[group_count] = bias
+
+    lax.fori_loop(0, n, ring, 0)
+    cots.start()
+    cots_ref[t] = cot_ref[...]
+    pair = 2 * block
+
+    def attend(i):
+        at = pl.ds(pl.multiple_of(i * pair, pair), pair)
+        queries = [q_ref[h, at, :] for h in range(heads)]
+
+        def key_block(j, carry, kind):
+            key_start = pl.multiple_of(j * pair, pair)
+            keys_at = pl.ds(key_start, pair)
+            out = []
+            for h in range(heads):
+                top, total, mixed = carry[h]
+                scores = dot_nt(k_ref[h, keys_at, :], queries[h]) * (score_scale * log2_e)
+                if kind > 0:
+                    scores = masked_scores(scores, key_start, i * pair, length, kind == 2)
+                new_top = jnp.maximum(top, jnp.max(scores, axis=0, keepdims=True))
+                shrink = jnp.exp2(top - new_top)
+                p = jnp.exp2(scores - new_top)
+                total = total * shrink + jnp.sum(p, axis=0, keepdims=True)
+                mixed = mixed * shrink + dot_nn(
+                    vt_ref[h * HEAD_DIM:(h + 1) * HEAD_DIM, keys_at], p.astype(jnp.bfloat16))
+                out.append((new_top, total, mixed))
+            return tuple(out)
+
+        start = tuple(
+            (jnp.full((1, pair), mask_fill, jnp.float32), jnp.zeros((1, pair), jnp.float32),
+             jnp.zeros((HEAD_DIM, pair), jnp.float32)) for _ in range(heads))
+        carry = lax.fori_loop(0, i, lambda j, c: key_block(j, c, 1), start)
+        carry = key_block(i, carry, 2)
+        for h in range(heads):
+            top, total, mixed = carry[h]
+            lse_ref[h:h + 1, at] = top + jnp.log2(total)
+        for a in range(lane_groups):
+            both = [carry[a * per_group + b][2] * (1.0 / carry[a * per_group + b][1]) for b in range(per_group)]
+            mixed_ref[at, a * LANES:(a + 1) * LANES] = jnp.concatenate(both, axis=0).T.astype(jnp.bfloat16)
+
+    cut = min(512, features)
+
+    def branch(j, _):
         k = near(n - 1 - j, m, n)
-        for a in range(0, width, cut):
-            s.side_out[k, :, a:a + cut] = dot_nn(mixed_ref[2 * k + 1 - core], w_ref[:, a:a + cut]).astype(jnp.bfloat16)
+
+        attend(k)
+
+        def attended(slot):
+            return mixed_ref[pl.ds(pl.multiple_of(slot * block, block), block), :]
+
+        low = attended(2 * k + 1 - core)
+        for a in range(0, features, cut):
+            s.side_out[k, :, a:a + cut] = dot_nn(low, wo_ref[:, a:a + cut]).astype(jnp.bfloat16)
         s.side(k).start()
-        for a in range(0, width, cut):
-            acc_ref[:, a:a + cut] = dot_nn(mixed_ref[2 * k + core], w_ref[:, a:a + cut])
-        pl.when(j < n - 1)(lambda: s.pass_on(k, acc_ref, lambda p: g.arrive(j + 1, p)))
-        return 0
-
-    lax.fori_loop(0, n, one, 0)
+        low = attended(2 * k + core)
+        for a in range(0, features, cut):
+            acc_ref[:, a:a + cut] = dot_nn(low, wo_ref[:, a:a + cut])
+        pl.when(j < n - 1)(lambda: s.pass_on(k, acc_ref, lambda p: cots.arrive(j + 1, p)))
+        return 0
+
+    lax.fori_loop(0, n, branch, 0)
 
     def consume(at, total):
         middle = x_ref[at, :].astype(jnp.float32) + total
@@ -567,20 +596,42 @@
 
     s.settle(acc_ref, consume)
     for k in range(n):
-        g.side_wait(k)
-    g.finish()
+        cots.side_wait(k)
+    first.finish()
+    cots.finish()
     s.finish()
-
-
-def out_branch(mixed, w, x, norms, cot, n, number, pieces=4):
-    rows, width = x.shape
-    return pl.pallas_call(functools.partial(out_kernel, n, pieces),
-        out_shape=(jax.ShapeDtypeStruct((rows, width), jnp.float32), jax.ShapeDtypeStruct((rows, width), jnp.bfloat16),
-                   jax.ShapeDtypeStruct((2 * n, rows, width), jnp.bfloat16)),
-        in_specs=[VM] * 5, out_specs=(VM,) * 3,
-        scratch_shapes=[pltpu.VMEM((rows, width), jnp.float32)] + scatter_scratch(n, pieces, rows, width) + [pltpu.SemaphoreType.DMA((5, n * pieces))],
-        compiler_params=params(number),
-        cost_estimate=lasting(115), name="out_branch")(mixed.reshape(2 * n, rows, mixed.shape[1]), w, x, norms, cot)
+    for kind in range(3):
+        for i in range(group_count):
+            pl.when(i != group)(lambda: share(kind, kinds[kind], group, i).wait_send())
+
+
+def forward(lengths, positions, x, norms, qkv, out, bias, cot, n, group_count, number, pieces=4):
+    rows, features = x.shape
+    width = qkv.shape[2]
+    heads = width // HEAD_DIM
+    total_rows = 2 * n * rows
+    f32, low = jnp.float32, jnp.bfloat16
+    shape = jax.ShapeDtypeStruct
+    half_rot = ROTARY // 2
+    frequency = rope_base ** (-(2.0 * jnp.arange(half_rot, dtype=jnp.float32)) / ROTARY)
+    split = shape((heads, total_rows, HEAD_DIM), low)
+    table = shape((total_rows, LANES), f32)
+    gathered = shape((2 * n, rows, features), low)
+    return pl.pallas_call(
+        functools.partial(forward_kernel, n, group_count, pieces),
+        out_shape=(gathered, shape((3, features, width), low), shape((width, features), low), split, split, split,
+                   shape((width, total_rows), low), shape((total_rows, width), low), shape((heads, total_rows), f32),
+                   table, table, table, shape((rows, features), f32), shape((rows, features), low), gathered),
+        in_specs=[pl.BlockSpec(memory_space=pltpu.SMEM)] + [VM] * 8, out_specs=(VM,) * 15,
+        scratch_shapes=[
+            pltpu.VMEM((width, total_rows), low), pltpu.VMEM((group_count + 1, 8, width), f32), pltpu.VMEM((rows, features), f32),
+        ] + scatter_scratch(n, pieces, rows, features) + [
+            pltpu.SemaphoreType.DMA((5, n * pieces)), pltpu.SemaphoreType.DMA((5, n * pieces)),
+            pltpu.SemaphoreType.DMA((3, group_count)), pltpu.SemaphoreType.DMA((3, group_count)),
+        ],
+        compiler_params=params(number), cost_estimate=lasting(200), name="forward",
+    )(lengths, positions.astype(f32).reshape(1, total_rows), jnp.tile(frequency, LANES // half_rot).reshape(1, LANES),
+      x, norms, qkv, out, bias, cot)
 
 
 def mlp_kernel(n, pieces, x_ref, cots_ref, gate_up_ref, down_ref, middle_ref, norm_ref,
@@ -723,16 +774,21 @@
     greet(n)
     s = Scatter(n, pieces, side_out, side_in, line_in, side_sems, line_send, line_recv)
     m, core = s.m, s.core
-    width = w_ref.shape[0]
+    width = w_ref.shape[1]
+    part = w_ref.shape[2]
     cut = min(512, width)
 
     def one(j, _):
         k = near(n - 1 - j, m, n)
+
+        def partial(slot, a):
+            return sum(dot_nt(grad_ref[slot, :, c * part:(c + 1) * part], w_ref[c, a:a + cut, :]) for c in range(3))
+
         for a in range(0, width, cut):
-            s.side_out[k, :, a:a + cut] = dot_nt(grad_ref[2 * k + 1 - core], w_ref[a:a + cut, :]).astype(jnp.bfloat16)
+            s.side_out[k, :, a:a + cut] = partial(2 * k + 1 - core, a).astype(jnp.bfloat16)
         s.side(k).start()
         for a in range(0, width, cut):
-            acc_ref[:, a:a + cut] = dot_nt(grad_ref[2 * k + core], w_ref[a:a + cut, :])
+            acc_ref[:, a:a + cut] = partial(2 * k + core, a)
         pl.when(j < n - 1)(lambda: s.pass_on(k, acc_ref))
         return 0
 
@@ -847,29 +903,17 @@
     group_tokens = local_tokens * tensor_count
     row_count = lengths.shape[0]
     row_length = group_tokens // row_count
-    block_rows = min(256, row_length)
+    block_rows = min(512, row_length)
     heads_here = bias_master.shape[1]
     width_here = heads_here * HEAD_DIM
     own_start = lax.axis_index("tensor") * local_tokens
     chips = tensor_count // 2
-    qkv_copy, gate_up_copy, out_copy, down_copy, bias_copy = (
-        lax.all_gather(qkv_master.astype(jnp.bfloat16), "dp", axis=1, tiled=True),
+    gate_up_copy, down_copy = (
         lax.all_gather(gate_up_master.astype(jnp.bfloat16), "dp", axis=1, tiled=True),
-        lax.all_gather(out_master.astype(jnp.bfloat16), "dp", axis=1, tiled=True),
         lax.all_gather(down_master.astype(jnp.bfloat16), "dp", axis=1, tiled=True),
-        lax.all_gather(bias_master.astype(jnp.bfloat16), "dp", axis=2, tiled=True),
-    )
-    qkv_flat = jnp.transpose(qkv_copy, (1, 0, 2)).reshape(qkv_copy.shape[1], 3 * width_here)
-    inputs_wide = inputs.astype(jnp.float32)
-    normed_one = norm_forward(inputs_wide, norm_master[0], norm_master[1]).astype(jnp.bfloat16)
-    gathered_one = gather(normed_one, chips, 0).reshape(group_tokens, D)
-    projected = jnp.dot(
-        gathered_one, qkv_flat, preferred_element_type=jnp.float32
-    ) + bias_copy.reshape(1, 3 * width_here).astype(jnp.float32)
-    keep, ahead, behind = rotary_tables(positions)
-    queries, keys, values, keys_flipped, mixed_low, log_totals = attention_forward(
-        lengths, projected, keep, ahead, behind, heads_here, block_rows
-    )
+    )
+    group = lax.axis_index("dp")
+    group_count = lax.axis_size("dp")
     group_index = own_start + jnp.arange(local_tokens, dtype=jnp.int32)
     row_of = group_index // row_length
     slot_of = group_index % row_length
@@ -877,7 +921,16 @@
     length_of = jnp.sum(jnp.where(row_match, lengths[None, :], 0), axis=1)
     valid = slot_of < length_of
     grad_low = jnp.where(valid[:, None], cotangent, jnp.zeros_like(cotangent))
-    middle, normed_two, gathered_grad = out_branch(mixed_low, out_copy, inputs, norm_master, grad_low, chips, 1)
+    own_dims = jnp.arange(HEAD_DIM) // (HEAD_DIM // group_count) == group
+    bias_row = jnp.where(own_dims, jnp.tile(bias_master, (1, 1, group_count)), 0.0).reshape(3, width_here)
+    bias_row = jnp.concatenate([bias_row, jnp.zeros((5, width_here), jnp.float32)], axis=0)
+    (
+        gathered_one, qkv_copy, out_copy, queries, keys, values, keys_flipped, mixed_low, log_totals,
+        keep, ahead, behind, middle, normed_two, gathered_grad,
+    ) = forward(
+        lengths, positions, inputs, norm_master, qkv_master, out_master, bias_row, grad_low, chips, group_count, 0
+    )
+    gathered_one = gathered_one.reshape(group_tokens, D)
     gathered_two, hidden, grad_gate_up, grad_middle, grad_middle_low, sums_two = mlp(
         normed_two, gathered_grad, gate_up_copy, down_copy, middle, norm_master, chips, 2
     )
@@ -908,10 +961,10 @@
         preferred_element_type=jnp.float32,
     )
     input_grad, sums_one = first_branch(
-        grad_projected, qkv_flat, inputs, grad_middle, norm_master, chips, 4
+        grad_projected, qkv_copy, inputs, grad_middle, norm_master, chips, 4
     )
     norm_grads = total_over_all(
-        jnp.concatenate([sums_one, sums_two], axis=0), tensor_count, lax.axis_size("dp"), 5
+        jnp.concatenate([sums_one, sums_two], axis=0), tensor_count, group_count, 5
     )
     qkv_grad, gate_up_grad, out_grad, down_grad, bias_grad = (
         sum_shard(grad_qkv_w, 1),

time: 882 us -> 786 us (0.89)
  Pallas kernels: 701 us -> 642 us
  local copies, waits for them, and re-layouts: 41.9 us -> 27.2 us
  matrix products: 57.5 us -> 46 us
    pallas_call x3 -> x1, Pallas kernels: 254 us -> 205 us  [forward(): pl.pallas_call(functools.partial(forward_kernel, n, group_count, pieces),...]
    pallas_call x1, Pallas kernels: 59.9 us -> 45.9 us  [attention_backward(): pl.pallas_call(functools.partial(backward_kernel, block), out_shape=(jax....]
    dot_general x1 -> x0, matrix products: 11.8 us -> none  [local(): jnp.dot(gathered_one, qkv_flat, preferred_element_type=jnp.float32)]
    concatenate x3 -> x1, local copies, waits for them, and re-layouts: 11.9 us -> 0.6 us  [local(): jnp.concatenate([bias_row, jnp.zeros((5, width_here), jnp.float32)], axis=0)]
    unnamed x63 -> x47, local copies, waits for them, and re-layouts: 18.7 us -> 19.9 us
  transfers between devices with their start and end apart: 8 -> 6, of which waited for: 0 -> 0; matrix products, arithmetic and copies ran while one was open for 13% -> 11% of each run, Pallas kernels for 48% -> 45%
where the time goes in v3:
time: 786 us; the launch traced here: 778 us
  Pallas kernels  642 us (82%)
  matrix products  46 us (6%)
  other arithmetic  30.2 us (4%)
  local copies, waits for them, and re-layouts  27.2 us (3%)
  between operations  16.2 us (2%)
  blocking collectives  15.6 us (2%)
    pallas_call x1, Pallas kernels, forward(): pl.pallas_call(functools.partial(forward_kernel, n, group_count, pieces),...  205 us
    pallas_call x1, Pallas kernels, mlp(): pl.pallas_call(functools.partial(mlp_kernel, n, pieces), out_shape=(jax.S...  174 us
    pallas_call x1, Pallas kernels, down_branch(): pl.pallas_call(functools.partial(down_kernel, n, pieces), out_shape=(jax....  119 us
    pallas_call x1, Pallas kernels, first_branch(): pl.pallas_call(functools.partial(first_kernel, n, pieces), out_shape=(jax...  84.4 us
    pallas_call x1, Pallas kernels, attention_backward(): pl.pallas_call(functools.partial(backward_kernel, block), out_shape=(jax....  45.9 us
    sub x6, other arithmetic, adamw(): weight_old - step_rate * (update + decay_part * weight_old)  23.3 us
    unnamed x47, local copies, waits for them, and re-layouts  19.9 us
    dot_general x1, matrix products, local(): jnp.einsum('td,ctf->cdf', gathered_two, grad_gate_up, preferred_element_t...  18.1 us
  transfers between devices with their start and end apart: 6, of which 0 were waited for; matrix products, arithmetic and copies ran while one was open for 11% of the time, Pallas kernels for 45%

profile of v3, /device:TPU:0, one launch (start us, length us, event | category | flops | bytes accessed | tf_op | source)
XLA Modules:
  0.0 777.9 jit_solution(2044549767589928255)
XLA Ops:
  7.2 0.0 copy-start
  7.2 0.0 all-gather.5.cloned.1.call-start
  7.2 2.5 convert_element_type.41
  9.7 0.0 all-gather.5.cloned.1.call-update
  9.7 0.0 all-gather.3.cloned.1.call-start
  9.8 0.0 copy-done
  9.8 1.3 convert_element_type.40
  11.1 2.6 copy.75
  13.7 0.0 all-gather.3.cloned.1.call-update
  13.8 0.0 reduce-scatter.10.cloned.1.call-start
  14.5 0.1 broadcast_in_dim.40
  14.6 0.0 copy-done.11
  14.6 0.1 tile.8
  14.7 0.6 reshape_tile.3.frequency_ref
  15.3 0.0 copy-done.14
  15.3 0.6 convert_element_type.39
  15.9 0.0 copy-done.6
  15.9 1.1 broadcast_select_fusion.cot_ref
  17.0 0.6 concatenate.6.bias_ref
  17.7 205.3 %forward.1 = (bf16[8,256,2048]{2,1,0:T(8,128)(2,1)}, bf16[3,2048,256]{2,1,0:T(8,128)(2,1)}, bf16[256,2048]{1,0:T(8,128)(2,1)}, bf16[4,2048,64]{2,1,0:T(8,128)(2,...) custom-call(s32[1]{0:T(128)} %copy.93.length_ref, ...), custom_call_target="tpu_custom_call" | custom-call | flops 219999993856 | tf_op jit(solution)/shard_map/forward/pallas_call | solution.py:620
  223.0 0.0 all-gather.5.cloned.1.call-done.down_ref
  223.0 0.0 all-gather.3.cloned.1.call-done.gate_up_ref
  223.1 174.3 %mlp.1 = (bf16[8,256,2048]{2,1,0:T(8,128)(2,1)}, bf16[8,256,704]{2,1,0:T(8,128)(2,1)}, bf16[2,8,256,704]{3,2,1,0:T(8,128)(2,1)}, f32[256,2048]{1,0:T(8,128)}, bf...) custom-call(bf16[256,2048]{1,0:T(8,128)(2,1)} %get-tuple-element.48.x_ref, bf16[8,256,2048]{2,1,0:T(8,128)(2,1)} %get-tuple-element.49.cots_ref, ...), custom_call_target="tpu_custom_call" | custom-call | flops 181500002304 | tf_op jit(solution)/shard_map/mlp/pallas_call | solution.py:713
  397.4 118.9 %down_branch.1 = (bf16[256,2048]{1,0:T(8,128)(2,1)}, bf16[8,256,2048]{2,1,0:T(8,128)(2,1)}, bf16[8,256,256]{2,1,0:T(8,128)(2,1)}) custom-call(bf16[8,256,704]{2,1,0:T(8,128)(2,1)} %get-tuple-element.51.hidden_ref, bf16[704,2048]{1,0:T(8,128)(2,1)} %all-gather.5.cloned.1.call-done.down_ref, f32[256,2048]{1,0:T(8,128)} %get-tuple-element.50.middle_ref, ...), custom_call_target="tpu_custom_call" | custom-call | flops 126500003840 | tf_op jit(solution)/shard_map/down_branch/pallas_call | solution.py:764
  516.3 6.7 convolution_convert_fusion.1
  523.0 0.0 reduce-scatter.10.cloned.1.call-update
  523.0 0.0 reduce-scatter.12.cloned.1.call-start
  523.0 10.7 %bitcast_convert_fusion.1 = bf16[704,2048]{1,0:T(8,128)(2,1)} fusion(bf16[8,256,704]{2,1,0:T(8,128)(2,1)} %get-tuple-element.51.hidden_ref, bf16[8,256,2048]{2,1,0:T(8,128)(2,1)} %get-tuple-element.49.cots_ref), kind=kOutput, calls=%fused_computation.4 | convolution fusion | flops 5907021824 | bytes 14155776 | tf_op jit(solution)/shard_map/tf,td->fd/dot_general | solution.py:946
  533.7 0.0 reduce-scatter.12.cloned.1.call-update
  533.7 0.2 reduce-scatter.6.cloned.1.call-start
  533.9 45.9 %attention_backward.1 = (bf16[2048,768]{1,0:T(8,128)(2,1)}, f32[1,768]{1,0:T(1,128)}) custom-call(s32[1]{0:T(128)} %copy.93.length_ref, bf16[4,2048,64]{2,1,0:T(8,128)(2,1)} %get-tuple-element.55.q_ref, bf16[4,2048,64]{2,1,0:T(8,128)(2,1)} %get-tuple-element.56.k_ref, bf16[4,2048,64]{2,1,0:T(8,128)(2,1)} %get-tuple-element.57.v_ref, ...), custom_call_target="tpu_custom_call" | custom-call | flops 21474836480 | bytes 15728640 | tf_op jit(solution)/shard_map/attention_backward/pallas_call | solution.py:179
  579.8 3.2 copy.77
  583.1 10.5 %fusion.5 = bf16[3,2048,256]{1,2,0:T(8,128)(2,1)} fusion(bf16[2048,3,256]{0,2,1:T(8,128)(2,1)S(1)} %bitcast.44, bf16[2048,2048,1]{1,0,2:T(8,128)(2,1)} %bitcast.48), kind=kOutput, calls=%fused_computation.8 | convolution fusion | flops 6444023808 | bytes 14680064 | tf_op jit(solution)/shard_map/td,tcw->cdw/dot_general | solution.py:957
  593.6 0.0 reduce-scatter.6.cloned.1.call-update
  593.6 0.0 reduce-scatter.8.cloned.1.call-start
  593.6 1.9 copy.80
  595.6 3.0 copy.76
  598.6 3.0 copy.78
  601.7 0.6 dynamic-slice
  602.9 18.1 %fusion.2 = bf16[2,2048,704]{1,2,0:T(8,128)(2,1)} fusion(bf16[2,8,256,704]{3,2,1,0:T(8,128)(2,1)} %get-tuple-element.70, bf16[8,256,2048]{2,1,0:T(8,128)(2,1)} %get-tuple-element.71), kind=kOutput, calls=%fused_computation.3 | convolution fusion | flops 11814043648 | bytes 19922944 | tf_op jit(solution)/shard_map/td,ctf->cdf/dot_general | solution.py:947
  621.0 0.0 reduce-scatter.8.cloned.1.call-update
  621.1 0.0 copy-start.17
  621.1 0.0 copy-start.12
  621.1 0.0 copy-start.15
  621.1 0.0 copy-start.16
  621.1 84.4 %first_branch.1 = (f32[256,2048]{1,0:T(8,128)}, f32[2,2048]{1,0:T(2,128)}) custom-call(bf16[8,256,768]{2,1,0:T(8,128)(2,1)} %bitcast.43, bf16[3,2048,256]{2,1,0:T(8,128)(2,1)} %get-tuple-element.66.w_ref, bf16[256,2048]{1,0:T(8,128)(2,1)} %x_ref.3, f32[256,2048]{1,0:T(8,128)} %get-tuple-element.67.middle_ref, f32[4,2048]{1,0:T(4,128)} %norm_ref.5), custom_call_target="tpu_custom_call" | custom-call | flops 93499998208 | tf_op jit(solution)/shard_map/first_branch/pallas_call | solution.py:811
  705.5 0.1 reshape.131
  705.6 15.6 %all-reduce.1 = f32[3,4,64]{2,1,0:T(4,128)S(1)} all-reduce(f32[3,4,64]{2,1,0:T(4,128)S(1)} %reshape.131), channel_id=6, replica_groups=mesh['dp'=4,'tensor'=8] {'dp'}, use_global_device_ids=true, to_apply=%region_4.5.clone | all-reduce | flops 768 | bytes 6144
  721.2 1.4 pad_maximum_fusion
  722.6 0.0 copy-done.16
  722.6 0.7 multiply_subtract_fusion.5
  723.3 13.5 %total_over_all.1 = f32[8,4,256]{2,1,0:T(4,128)} custom-call(f32[8,4,256]{2,1,0:T(4,128)} %bitcast.46), custom_call_target="tpu_custom_call" | custom-call | flops 13200000000 | tf_op jit(solution)/shard_map/total_over_all/pallas_call | solution.py:864
  736.7 0.0 copy-start.3
  736.8 1.5 multiply_subtract_fusion.4
  738.3 2.9 multiply_subtract_fusion.3
  741.2 4.8 multiply_subtract_fusion.2
  746.0 5.2 multiply_subtract_fusion.1
  751.2 3.1 copy.83
  754.3 1.6 copy.84
  755.9 3.2 copy.85
  759.1 8.3 %multiply_subtract_fusion = (f32[2,512,704]{1,2,0:T(8,128)}, f32[2,512,704]{1,2,0:T(8,128)}, f32[2,512,704]{1,2,0:T(8,128)}) fusion(f32[2,512,704]{1,2,0:T(8,128)S(1)} %copy-done.1, bf16[2,512,704]{1,2,0:T(8,128)(2,1)} %reduce-scatter.8.cloned.1.call-done, f32[2,512,704]{1,2,0:T(8,128)} %param.33, f32[2,512,704]{1,2,0:T(8,128)} %param.39), kind=kLoop, calls=%fused_computation.11 | loop fusion | flops 11534336 | bytes 18743296 | tf_op jit(solution)/shard_map/sub | solution.py:70
  767.4 1.0 copy.94
  768.3 1.0 copy-done.5
  769.3 1.3 copy.95
  (38 shorter events, 0.1 us)
Async XLA Ops:
  7.2 2.6 copy-start
  7.2 215.8 %all-gather.5.cloned.1.call-start = ((), (), s32[]{:S(2)}) async-start(), calls=%async_computation.5 | async-start | bytes 3604480 | tf_op jit(solution)/shard_map/all_gather | solution.py:913
  9.7 213.3 %all-gather.3.cloned.1.call-start = ((), (), s32[]{:S(2)}) async-start(), calls=%async_computation.4 | async-start | bytes 7864320 | tf_op jit(solution)/shard_map/all_gather | solution.py:912
  11.1 3.5 copy-start.11
  11.1 4.2 copy-start.14
  11.1 4.8 copy-start.6
  13.8 724.6 %reduce-scatter.10.cloned.1.call-start = ((), (), s32[]{:S(2)}) async-start(), calls=%async_computation.8 | async-start | bytes 1310720 | tf_op jit(solution)/shard_map/reduce_scatter | solution.py:59
  397.4 118.9 %copy-start.4 = (bf16[2048,256]{1,0:T(8,128)(2,1)S(1)}, bf16[2048,256]{1,0:T(8,128)(2,1)}, u32[]{:S(2)}) copy-start(bf16[2048,256]{1,0:T(8,128)(2,1)} %get-tuple-element.59.o_ref) | copy-start | bytes 3145732
  523.0 218.2 %reduce-scatter.12.cloned.1.call-start = ((), (), s32[]{:S(2)}) async-start(), calls=%async_computation.9 | async-start | bytes 3604480 | tf_op jit(solution)/shard_map/reduce_scatter | solution.py:59
  533.7 212.3 %reduce-scatter.6.cloned.1.call-start = ((), (), s32[]{:S(2)}) async-start(), calls=%async_computation.6 | async-start | bytes 3932160 | tf_op jit(solution)/shard_map/reduce_scatter | solution.py:59
  593.6 165.5 %reduce-scatter.8.cloned.1.call-start = ((), (), s32[]{:S(2)}) async-start(), calls=%async_computation.7 | async-start | bytes 7208960 | tf_op jit(solution)/shard_map/reduce_scatter | solution.py:59
  598.6 3.0 copy-start.18
  621.1 84.4 %copy-start.17 = (f32[1,768]{1,0:T(1,128)S(1)}, f32[1,768]{1,0:T(1,128)}, u32[]{:S(2)}) copy-start(f32[1,768]{1,0:T(1,128)} %get-tuple-element.73) | copy-start | bytes 9220
  621.1 100.1 %copy-start.13 = (f32[2,2048]{1,0:T(2,128)S(1)}, f32[2,2048]{1,0:T(2,128)}, u32[]{:S(2)}) copy-start(f32[2,2048]{1,0:T(2,128)} %get-tuple-element.75) | copy-start | bytes 49156
  621.1 101.5 %copy-start.12 = (f32[3,4,16]{2,1,0:T(4,128)S(1)}, f32[3,4,16]{2,1,0:T(4,128)}, u32[]{:S(2)}) copy-start(f32[3,4,16]{2,1,0:T(4,128)} %param.30) | copy-start | bytes 2308
  621.1 101.5 %copy-start.15 = (f32[3,4,16]{2,1,0:T(4,128)S(1)}, f32[3,4,16]{2,1,0:T(4,128)}, u32[]{:S(2)}) copy-start(f32[3,4,16]{2,1,0:T(4,128)} %param.36) | copy-start | bytes 2308
  621.1 101.5 %copy-start.16 = (f32[3,4,16]{2,1,0:T(4,128)S(1)}, f32[3,4,16]{2,1,0:T(4,128)}, u32[]{:S(2)}) copy-start(f32[3,4,16]{2,1,0:T(4,128)} %param.42) | copy-start | bytes 2308
  723.3 13.5 %copy-start.8 = (f32[4,2048]{1,0:T(4,128)S(1)}, f32[4,2048]{1,0:T(4,128)}, u32[]{:S(2)}) copy-start(f32[4,2048]{1,0:T(4,128)} %norm_ref.5) | copy-start | bytes 98308
  723.3 13.5 %copy-start.9 = (f32[4,2048]{1,0:T(4,128)S(1)}, f32[4,2048]{1,0:T(4,128)}, u32[]{:S(2)}) copy-start(f32[4,2048]{1,0:T(4,128)} %param.37) | copy-start | bytes 98308
  723.3 13.5 %copy-start.10 = (f32[4,2048]{1,0:T(4,128)S(1)}, f32[4,2048]{1,0:T(4,128)}, u32[]{:S(2)}) copy-start(f32[4,2048]{1,0:T(4,128)} %param.43) | copy-start | bytes 98308
  736.7 4.5 copy-start.3
  751.2 3.1 copy-start.2
  755.9 3.2 copy-start.1
  759.1 8.3 %copy-start.7 = (bf16[256,2048]{1,0:T(8,128)(2,1)S(1)}, bf16[256,2048]{1,0:T(8,128)(2,1)}, u32[]{:S(2)}) copy-start(bf16[256,2048]{1,0:T(8,128)(2,1)} %get-tuple-element.194) | copy-start | bytes 3145732
  767.4 2.0 copy-start.5
Sparse Core Ops, SparseCore 0:
  10.4 82.0 all-gather.4
  94.9 70.1 all-gather.2
  523.1 31.6 reduce-scatter.9
  558.5 41.7 reduce-scatter.11
  603.4 44.0 reduce-scatter.5
  650.6 65.7 reduce-scatter.7

commit v4 on v3

--- a/solution.py
+++ b/solution.py
@@ -55,10 +55,8 @@
     )
 
 
-def sum_shard(gradient, dimension):
-    return lax.psum_scatter(
-        gradient.astype(jnp.bfloat16), "dp", scatter_dimension=dimension, tiled=True
-    ).astype(jnp.float32)
+def sum_parts(parts):
+    return sum(parts[i].astype(jnp.float32) for i in range(parts.shape[0]))
 
 
 def adamw(weight_old, first_old, second_old, gradient, step_rate, decay_part):
@@ -196,6 +194,7 @@
 
 
 VM = pl.BlockSpec(memory_space=pltpu.VMEM)
+ANYWHERE = pl.BlockSpec(memory_space=pl.ANY)
 MESH = pl.DeviceIdType.MESH
 
 
@@ -258,17 +257,17 @@
     def to_side(self, k, p, src):
         return self.copy(src, k, p, self.core, self.side, self.side_in, self.sibling)
 
-    def start(self):
+    def start(self, which=None):
         m = self.m
-        for p in range(self.pieces):
+        for p in range(self.pieces) if which is None else which:
             pl.when(m < self.n - 1)(lambda: self.to_up(m, p, self.own).start())
             pl.when(m > 0)(lambda: self.to_down(m, p, self.own).start())
             self.to_side(m, p, self.own).start()
 
-    def arrive(self, d, only=None):
+    def arrive(self, d, which=None):
         m = self.m
         lo, hi = m - d, m + d
-        for p in range(self.pieces) if only is None else (only,):
+        for p in range(self.pieces) if which is None else which:
             @pl.when(lo >= 0)
             def _():
                 src = self.buf.at[2 * lo + self.core]
@@ -283,8 +282,8 @@
                 pl.when(m > 0)(lambda: self.to_down(hi, p, src).start())
                 self.to_side(hi, p, src).start()
 
-    def side_wait(self, k):
-        for p in range(self.pieces):
+    def side_wait(self, k, which=None):
+        for p in range(self.pieces) if which is None else which:
             self.copy(self.own, k, p, 1 - self.core, self.side, self.side_in, self.sibling).wait_recv()
 
     def finish(self):
@@ -389,15 +388,16 @@
     def finish(self):
         def one(k, _):
             self.side(k).wait_send()
-
-            @pl.when(k != self.m)
-            def _():
-                for p in range(self.pieces):
-                    self.line(k, p, k, self.t).wait_send()
-
+            self.finish_line(k)
             return 0
 
         lax.fori_loop(0, self.n, one, 0)
+
+    def finish_line(self, k):
+        @pl.when(k != self.m)
+        def _():
+            for p in range(self.pieces):
+                self.line(k, p, k, self.t).wait_send()
 
 
 def scatter_scratch(n, pieces, rows, width):
@@ -406,6 +406,43 @@
         pltpu.VMEM((n + 1, rows, width), jnp.bfloat16),
         pltpu.SemaphoreType.DMA((2, n)), pltpu.SemaphoreType.DMA((n * pieces,)), pltpu.SemaphoreType.DMA(((n + 1) * pieces,)),
     ]
+
+
+class Exchange:
+    def __init__(self, group_count, pairs, local_sems, send, recv):
+        self.group, self.count, self.pairs = lax.axis_index("dp"), group_count, pairs
+        self.local_sems, self.send, self.recv = local_sems, send, recv
+
+    def stay(self, index):
+        src, dst = self.pairs[index]
+        return pltpu.make_async_copy(src.at[self.group], dst.at[self.group], self.local_sems.at[index])
+
+    def copy(self, index, peer, slot):
+        src, dst = self.pairs[index]
+        return pltpu.make_async_remote_copy(
+            src_ref=src.at[peer], dst_ref=dst.at[slot], send_sem=self.send.at[index, peer],
+            recv_sem=self.recv.at[index, slot], device_id={"dp": peer}, device_id_type=MESH)
+
+    def others(self, body):
+        for index in range(len(self.pairs)):
+            for i in range(self.count):
+                pl.when(i != self.group)(lambda: body(index, i))
+
+    def start(self):
+        self.others(lambda index, i: self.copy(index, i, self.group).start())
+        for index in range(len(self.pairs)):
+            self.stay(index).start()
+
+    def finish(self):
+        for index in range(len(self.pairs)):
+            self.stay(index).wait()
+        self.others(lambda index, i: self.copy(index, i, i).wait_recv())
+        self.others(lambda index, i: self.copy(index, i, self.group).wait_send())
+
+
+def exchange_scratch(pairs, group_count):
+    dma = pltpu.SemaphoreType.DMA
+    return [dma((pairs,)), dma((pairs, group_count)), dma((pairs, group_count))]
 
 
 def greet_all(n, group_count):
@@ -584,7 +621,7 @@
         low = attended(2 * k + core)
         for a in range(0, features, cut):
             acc_ref[:, a:a + cut] = dot_nn(low, wo_ref[:, a:a + cut])
-        pl.when(j < n - 1)(lambda: s.pass_on(k, acc_ref, lambda p: cots.arrive(j + 1, p)))
+        pl.when(j < n - 1)(lambda: s.pass_on(k, acc_ref, lambda p: cots.arrive(j + 1, (p,))))
         return 0
 
     lax.fori_loop(0, n, branch, 0)
@@ -634,53 +671,281 @@
       x, norms, qkv, out, bias, cot)
 
 
-def mlp_kernel(n, pieces, x_ref, cots_ref, gate_up_ref, down_ref, middle_ref, norm_ref,
-               xs_ref, hidden_ref, grads_ref, grad_middle_ref, low_ref, sums_ref,
-               acc_ref, side_out, side_in, line_in, side_sems, line_send, line_recv, gather_sems):
+def mlp_kernel(n, pieces, x_ref, cots_hbm, gate_up_hbm, down_hbm, middle_hbm, norm_ref,
+               hidden_ref, grad_middle_ref, sums_ref, grad_gate_up_ref, grad_down_ref,
+               cots_ref, gate_up_ref, down_ref, middle_ref, xs_ref, grads_ref, load_sems,
+               acc_ref, side_out, side_in, line_in, side_sems, line_send, line_recv, gather_sems,
+               wide_stage, down_stage, wide_sem, down_sem):
+    loads = [
+        pltpu.make_async_copy(src, dst, load_sems.at[i])
+        for i, (src, dst) in enumerate(
+            ((gate_up_hbm, gate_up_ref), (cots_hbm, cots_ref), (down_hbm, down_ref), (middle_hbm, middle_ref)))
+    ]
+    for load in loads:
+        load.start()
     greet(n)
     g = Gather(n, x_ref, xs_ref, gather_sems, pieces)
+    halves = tuple(
+        Scatter(n, pieces // 2, side_out, side_in.at[h], line_in.at[h], side_sems.at[h], line_send.at[h], line_recv.at[h])
+        for h in range(2))
+    m, core = g.m, g.core
+    rows, width = x_ref.shape
+    half = rows // 2
+    group_count, hidden_units, depth = down_ref.shape
+    cut = min(512, depth)
+    places = [(f, min(256, hidden_units - f)) for f in range(0, hidden_units, 256)]
+    early, late = tuple(range(pieces // 2)), tuple(range(pieces // 2, pieces))
+    g.start(early)
+    xs_ref[g.t] = x_ref[...]
+    for load in loads:
+        load.wait()
+
+    def work(k, h):
+        both = pl.ds(2 * k, 2)
+        at = slice(h * half, (h + 1) * half)
+        x = xs_ref[both, at, :].reshape(2 * half, width)
+        cot = cots_ref[both, at, :].reshape(2 * half, width)
+        for place, size in places:
+            units = slice(place, place + size)
+            shape = (2, half, size)
+
+            def product(left, right):
+                return sum(dot_nt(left[:, o * depth:(o + 1) * depth], right(o)) for o in range(group_count))
+
+            gate = product(x, lambda o: gate_up_ref[o, 0, units, :])
+            up = product(x, lambda o: gate_up_ref[o, 1, units, :])
+            grad_hidden = product(cot, lambda o: down_ref[o, units, :])
+            sig = 1.0 / (1.0 + jnp.exp(-gate))
+            silu = gate * sig
+            hidden_ref[both, at, units] = (silu * up).astype(jnp.bfloat16).reshape(shape)
+            grads_ref[0, both, at, units] = (grad_hidden * up * (sig * (1.0 + gate * (1.0 - sig)))).astype(jnp.bfloat16).reshape(shape)
+            grads_ref[1, both, at, units] = (grad_hidden * silu).astype(jnp.bfloat16).reshape(shape)
+
+    def work_at(d, h, which):
+        def one(above, _):
+            k = jnp.where(above == 1, m + d, m - d)
+
+            @pl.when((k >= 0) & (k < n) & ((d > 0) | (above == 0)))
+            def _():
+                g.side_wait(k, which)
+                work(k, h)
+
+            return 0
+
+        lax.fori_loop(0, 2, one, 0)
+
+    def ring(d, _):
+        pl.when(d > 0)(lambda: g.arrive(d, early))
+        pl.when(d == n - 2)(lambda: g.start(late))
+        work_at(d, 0, early)
+        return 0
+
+    lax.fori_loop(0, n, ring, 0)
+
+    def partials(k, h):
+        at = slice(h * half, (h + 1) * half)
+        both = pl.ds(2 * k, 2)
+        for a in range(0, width, cut):
+            acc_ref[h, :, :, a:a + cut] = sum(
+                dot_nn(grads_ref[c, both, at, :].reshape(2 * half, hidden_units), gate_up_ref[a // depth, c, :, a % depth:a % depth + cut])
+                for c in range(2)
+            ).reshape(2, half, cut)
+        if h == 1:
+            halves[0].side(k).wait_send()
+        step = min(32, half)
+
+        def lower(i, _):
+            here = pl.ds(pl.multiple_of(i * step, step), step)
+            side_out[k, here, :] = acc_ref[h, 1 - core, here, :].astype(jnp.bfloat16)
+            return 0
+
+        lax.fori_loop(0, half // step, lower, 0)
+        halves[h].side(k).start()
+
+    def one(j, _):
+        k = near(n - 1 - j, m, n)
+        partials(k, 0)
+        pl.when(j < n - 1)(
+            lambda: halves[0].pass_on(k, acc_ref.at[0, core], lambda p: g.arrive(j + 1, (late[0] + p,))))
+        work_at(j, 1, late)
+        return 0
+
+    lax.fori_loop(0, n, one, 0)
+    wide_cut = min(256, depth)
+    per = -(-(width // wide_cut) // n)
+    tokens = 2 * n * rows
+
+    def wide_copy(place, slot):
+        lanes = pl.ds(pl.multiple_of(lax.rem(place, depth), wide_cut), wide_cut)
+        return pltpu.make_async_copy(
+            wide_stage.at[slot], grad_gate_up_ref.at[lax.div(place, depth), :, :, lanes], wide_sem.at[slot])
+
+    def wide_gradient(u, j):
+        place = (j * per + u) * wide_cut
+
+        @pl.when(place < width)
+        def _():
+            pl.when(j > 0)(lambda: wide_copy(0, u).wait())
+            lanes = pl.ds(pl.multiple_of(place, wide_cut), wide_cut)
+            x = xs_ref[:, :, lanes].reshape(tokens, wide_cut).T
+            for c in range(2):
+                wide_stage[u, c] = dot_nn(x, grads_ref[c].reshape(tokens, hidden_units)).T.astype(jnp.bfloat16)
+            wide_copy(place, u).start()
+
+    def down_copy(place, size):
+        return pltpu.make_async_copy(down_stage.at[:, pl.ds(0, size)], grad_down_ref.at[:, pl.ds(place, size)], down_sem)
+
+    def down_gradient(index):
+        place, size = places[index]
+        if index > 0:
+            down_copy(*places[index - 1]).wait()
+        low = hidden_ref[:, :, place:place + size].reshape(tokens, size).T
+        for a in range(0, width, cut):
+            down_stage[a // depth, :size, a % depth:a % depth + cut] = dot_nn(low, cots_ref[:, :, a:a + cut].reshape(tokens, cut)).astype(jnp.bfloat16)
+        down_copy(place, size).start()
+
+    def two(j, _):
+        k = near(n - 1 - j, m, n)
+        partials(k, 1)
+        pl.when(j < n - 1)(lambda: halves[1].pass_on(k, acc_ref.at[1, core]))
+        for u in range(per):
+            wide_gradient(u, j)
+        for index in range(len(places)):
+            pl.when(j == index)(functools.partial(down_gradient, index))
+        return 0
+
+    own = acc_ref.at[0, core]
+
+    def settle(h):
+        def consume(at, total):
+            here = pl.ds(pl.multiple_of(h * half + at.start, at.size), at.size)
+            back, gain, shift = norm_backward(middle_ref[here, :], norm_ref[2:3, :], total)
+            grad_middle_ref[here, :] = cots_ref[g.t, here, :].astype(jnp.float32) + back
+            sums_ref[0:1, :] += gain
+            sums_ref[1:2, :] += shift
+
+        halves[h].settle(acc_ref.at[h, core], consume)
+
+    sums_ref[...] = jnp.zeros(sums_ref.shape, jnp.float32)
+    settle(0)
+    lax.fori_loop(0, n, two, 0)
+    settle(1)
+    for u in range(per):
+        wide_copy(0, u).wait()
+    down_copy(*places[-1]).wait()
+    g.finish()
+
+    def sent(k, _):
+        halves[1].side(k).wait_send()
+        for h in range(2):
+            halves[h].finish_line(k)
+        return 0
+
+    lax.fori_loop(0, n, sent, 0)
+
+
+def mlp(x, cots, gate_up, down, middle, norms, n, number, pieces=4):
+    rows, width = x.shape
+    group_count, hidden, depth = down.shape
+    half, part = rows // 2, pieces // 2
+    f32, low = jnp.float32, jnp.bfloat16
+    shape = jax.ShapeDtypeStruct
+    anywhere = pl.BlockSpec(memory_space=pl.ANY)
+    wide_cut = min(256, depth)
+    per = -(-(width // wide_cut) // n)
+    dma = pltpu.SemaphoreType.DMA
+    return pl.pallas_call(functools.partial(mlp_kernel, n, pieces),
+        out_shape=(shape((2 * n, rows, hidden), low), shape((rows, width), f32),
+                   shape((2, width), f32), shape(gate_up.shape, low), shape(down.shape, low)),
+        in_specs=[VM] + [anywhere] * 4 + [VM], out_specs=(VM,) * 3 + (anywhere,) * 2,
+        scratch_shapes=[
+            pltpu.VMEM((2 * n, rows, width), low), pltpu.VMEM(gate_up.shape, low), pltpu.VMEM(down.shape, low), pltpu.VMEM((rows, width), f32),
+            pltpu.VMEM((2 * n, rows, width), low), pltpu.VMEM((2, 2 * n, rows, hidden), low), dma((4,)),
+            pltpu.VMEM((2, 2, half, width), f32), pltpu.VMEM((n, half, width), low), pltpu.VMEM((2, n, half, width), low),
+            pltpu.VMEM((2, n + 1, half, width), low), dma((2, 2, n)), dma((2, n * part)), dma((2, (n + 1) * part)),
+            dma((5, n * pieces)), pltpu.VMEM((per, 2, hidden, wide_cut), low), pltpu.VMEM((group_count, min(256, hidden), depth), low),
+            dma((per,)), dma,
+        ],
+        compiler_params=params(number), cost_estimate=lasting(140), name="mlp")(x, cots, gate_up, down, middle, norms)
+
+
+def down_kernel(n, pieces, hidden_ref, down_ref, middle_ref, grad_ref, out_ref, mixed_ref, wide_ref, low_ref, block_ref, back_ref, grad_out_ref, wide_parts, low_parts,
+                local_sems, share_send, share_recv, xs_ref, x_ref, acc_ref, side_out, side_in, line_in, side_sems, line_send, line_recv, gather_sems):
+    group_count, _, depth = down_ref.shape
+    greet_all(n, group_count)
+    grads = Exchange(group_count, ((wide_ref, wide_parts), (low_ref, low_parts)), local_sems, share_send, share_recv)
+    g = Gather(n, x_ref, xs_ref, gather_sems, pieces)
     s = Scatter(n, pieces, side_out, side_in, line_in, side_sems, line_send, line_recv)
+    x_ref[...] = grad_ref[...].astype(jnp.bfloat16)
     g.start()
+    grads.start()
     xs_ref[g.t] = x_ref[...]
     m, core = s.m, s.core
-
-    def work(slot):
-        x = xs_ref[slot]
-        gate = dot_nn(x, gate_up_ref[0])
-        up = dot_nn(x, gate_up_ref[1])
-        grad_hidden = dot_nt(cots_ref[slot], down_ref[...])
-        sig = 1.0 / (1.0 + jnp.exp(-gate))
-        silu = gate * sig
-        hidden_ref[slot] = (silu * up).astype(jnp.bfloat16)
-        grads_ref[0, slot] = (grad_hidden * up * (sig * (1.0 + gate * (1.0 - sig)))).astype(jnp.bfloat16)
-        grads_ref[1, slot] = (grad_hidden * silu).astype(jnp.bfloat16)
-
-    def ring(d, _):
-        pl.when(d > 0)(lambda: g.arrive(d))
-
-        def one(q, _):
-            other, above = lax.div(q, 2), lax.rem(q, 2)
-            k = jnp.where(above == 1, m + d, m - d)
-
-            @pl.when((k >= 0) & (k < n) & ((d > 0) | (above == 0)))
-            def _():
-                pl.when(other == 1)(lambda: g.side_wait(k))
-                work(2 * k + jnp.where(other == 1, 1 - core, core))
-
-            return 0
-
-        lax.fori_loop(0, 4, one, 0)
-        return 0
-
-    lax.fori_loop(0, n, ring, 0)
-    width = x_ref.shape[1]
-    cut = min(512, width)
+    width = group_count * depth
+    cut = min(512, depth)
 
     def one(j, _):
         k = near(n - 1 - j, m, n)
+        for a in range(0, width, cut):
+            s.side_out[k, :, a:a + cut] = dot_nn(hidden_ref[2 * k + 1 - core], down_ref[a // depth, :, a % depth:a % depth + cut]).astype(jnp.bfloat16)
+        s.side(k).start()
+        for a in range(0, width, cut):
+            acc_ref[:, a:a + cut] = dot_nn(hidden_ref[2 * k + core], down_ref[a // depth, :, a % depth:a % depth + cut])
+        pl.when(j < n - 1)(lambda: s.pass_on(k, acc_ref, lambda p: g.arrive(j + 1, (p,))))
+        return 0
+
+    lax.fori_loop(0, n, one, 0)
+
+    def consume(at, total):
+        block_ref[at, :] = (middle_ref[at, :] + total).astype(jnp.bfloat16)
+
+    s.settle(acc_ref, consume)
+
+    def last(k, _):
+        g.side_wait(k)
+        for c in range(2):
+            back_ref[2 * k + c] = dot_nt(xs_ref[2 * k + c], out_ref[...]).astype(jnp.bfloat16)
+        return 0
+
+    lax.fori_loop(0, n, last, 0)
+    flipped = mixed_ref[...].T
+    for a in range(0, width, cut):
+        grad_out_ref[a // depth, :, a % depth:a % depth + cut] = dot_nn(
+            flipped, xs_ref[:, :, a:a + cut].reshape(mixed_ref.shape[0], cut)).astype(jnp.bfloat16)
+    g.finish()
+    s.finish()
+    grads.finish()
+
+
+def down_branch(hidden, down, middle, x, out, mixed, wide, narrow, n, number, pieces=4):
+    rows, width = x.shape
+    f32, low = jnp.float32, jnp.bfloat16
+    return pl.pallas_call(functools.partial(down_kernel, n, pieces),
+        out_shape=(jax.ShapeDtypeStruct((rows, width), low), jax.ShapeDtypeStruct((2 * n, rows, out.shape[0]), low),
+                   jax.ShapeDtypeStruct((down.shape[0], out.shape[0], down.shape[2]), low),
+                   jax.ShapeDtypeStruct(wide.shape, low), jax.ShapeDtypeStruct(narrow.shape, low)),
+        in_specs=[VM] * 6 + [ANYWHERE] * 2, out_specs=(VM,) * 3 + (ANYWHERE,) * 2,
+        scratch_shapes=exchange_scratch(2, down.shape[0]) + [pltpu.VMEM((2 * n, rows, width), low), pltpu.VMEM((rows, width), low), pltpu.VMEM((rows, width), f32)] + scatter_scratch(n, pieces, rows, width) + [pltpu.SemaphoreType.DMA((5, n * pieces))],
+        compiler_params=params(number), cost_estimate=lasting(115), name="down_branch")(hidden, down, middle, x, out, mixed, wide, narrow)
+
+
+def first_kernel(n, pieces, grad_ref, w_ref, x_ref, middle_ref, norm_ref, wide_ref, low_ref, result_ref, sums_ref, wide_parts, low_parts,
+                 local_sems, share_send, share_recv, acc_ref, side_out, side_in, line_in, side_sems, line_send, line_recv):
+    group_count = wide_ref.shape[0]
+    greet_all(n, group_count)
+    grads = Exchange(group_count, ((wide_ref, wide_parts), (low_ref, low_parts)), local_sems, share_send, share_recv)
+    grads.start()
+    s = Scatter(n, pieces, side_out, side_in, line_in, side_sems, line_send, line_recv)
+    m, core = s.m, s.core
+    width = w_ref.shape[1]
+    part = w_ref.shape[2]
+    cut = min(512, width)
+
+    def one(j, _):
+        k = near(n - 1 - j, m, n)
 
         def partial(slot, a):
-            return dot_nt(grads_ref[0, slot], gate_up_ref[0, a:a + cut, :]) + dot_nt(grads_ref[1, slot], gate_up_ref[1, a:a + cut, :])
+            return sum(dot_nt(grad_ref[slot, :, c * part:(c + 1) * part], w_ref[c, a:a + cut, :]) for c in range(3))
 
         for a in range(0, width, cut):
             s.side_out[k, :, a:a + cut] = partial(2 * k + 1 - core, a).astype(jnp.bfloat16)
@@ -694,108 +959,6 @@
     sums_ref[...] = jnp.zeros(sums_ref.shape, jnp.float32)
 
     def consume(at, total):
-        back, gain, shift = norm_backward(middle_ref[at, :], norm_ref[2:3, :], total)
-        result = cots_ref[s.t, at, :].astype(jnp.float32) + back
-        grad_middle_ref[at, :] = result
-        low_ref[at, :] = result.astype(jnp.bfloat16)
-        sums_ref[0:1, :] += gain
-        sums_ref[1:2, :] += shift
-
-    s.settle(acc_ref, consume)
-    g.finish()
-    s.finish()
-
-
-def mlp(x, cots, gate_up, down, middle, norms, n, number, pieces=4):
-    rows, width = x.shape
-    hidden = down.shape[0]
-    f32, low = jnp.float32, jnp.bfloat16
-    return pl.pallas_call(functools.partial(mlp_kernel, n, pieces),
-        out_shape=(jax.ShapeDtypeStruct((2 * n, rows, width), low), jax.ShapeDtypeStruct((2 * n, rows, hidden), low),
-                   jax.ShapeDtypeStruct((2, 2 * n, rows, hidden), low), jax.ShapeDtypeStruct((rows, width), f32),
-                   jax.ShapeDtypeStruct((rows, width), low), jax.ShapeDtypeStruct((2, width), f32)),
-        in_specs=[VM] * 6, out_specs=(VM,) * 6,
-        scratch_shapes=[pltpu.VMEM((rows, width), f32)] + scatter_scratch(n, pieces, rows, width) + [pltpu.SemaphoreType.DMA((5, n * pieces))],
-        compiler_params=params(number), cost_estimate=lasting(165), name="mlp")(x, cots, gate_up, down, middle, norms)
-
-
-def down_kernel(n, pieces, hidden_ref, down_ref, middle_ref, x_ref, out_ref, block_ref, xs_ref, back_ref,
-                acc_ref, side_out, side_in, line_in, side_sems, line_send, line_recv, gather_sems):
-    greet(n)
-    g = Gather(n, x_ref, xs_ref, gather_sems, pieces)
-    s = Scatter(n, pieces, side_out, side_in, line_in, side_sems, line_send, line_recv)
-    g.start()
-    xs_ref[g.t] = x_ref[...]
-    m, core = s.m, s.core
-    width = down_ref.shape[1]
-    cut = min(512, width)
-
-    def one(j, _):
-        k = near(n - 1 - j, m, n)
-        for a in range(0, width, cut):
-            s.side_out[k, :, a:a + cut] = dot_nn(hidden_ref[2 * k + 1 - core], down_ref[:, a:a + cut]).astype(jnp.bfloat16)
-        s.side(k).start()
-        for a in range(0, width, cut):
-            acc_ref[:, a:a + cut] = dot_nn(hidden_ref[2 * k + core], down_ref[:, a:a + cut])
-        pl.when(j < n - 1)(lambda: s.pass_on(k, acc_ref, lambda p: g.arrive(j + 1, p)))
-        return 0
-
-    lax.fori_loop(0, n, one, 0)
-
-    def consume(at, total):
-        block_ref[at, :] = (middle_ref[at, :] + total).astype(jnp.bfloat16)
-
-    s.settle(acc_ref, consume)
-
-    def last(k, _):
-        g.side_wait(k)
-        for c in range(2):
-            back_ref[2 * k + c] = dot_nt(xs_ref[2 * k + c], out_ref[...]).astype(jnp.bfloat16)
-        return 0
-
-    lax.fori_loop(0, n, last, 0)
-    g.finish()
-    s.finish()
-
-
-def down_branch(hidden, down, middle, x, out, n, number, pieces=4):
-    rows, width = x.shape
-    f32, low = jnp.float32, jnp.bfloat16
-    return pl.pallas_call(functools.partial(down_kernel, n, pieces),
-        out_shape=(jax.ShapeDtypeStruct((rows, width), low), jax.ShapeDtypeStruct((2 * n, rows, width), low),
-                   jax.ShapeDtypeStruct((2 * n, rows, out.shape[0]), low)),
-        in_specs=[VM] * 5, out_specs=(VM,) * 3,
-        scratch_shapes=[pltpu.VMEM((rows, width), f32)] + scatter_scratch(n, pieces, rows, width) + [pltpu.SemaphoreType.DMA((5, n * pieces))],
-        compiler_params=params(number), cost_estimate=lasting(115), name="down_branch")(hidden, down, middle, x, out)
-
-
-def first_kernel(n, pieces, grad_ref, w_ref, x_ref, middle_ref, norm_ref, result_ref, sums_ref,
-                 acc_ref, side_out, side_in, line_in, side_sems, line_send, line_recv):
-    greet(n)
-    s = Scatter(n, pieces, side_out, side_in, line_in, side_sems, line_send, line_recv)
-    m, core = s.m, s.core
-    width = w_ref.shape[1]
-    part = w_ref.shape[2]
-    cut = min(512, width)
-
-    def one(j, _):
-        k = near(n - 1 - j, m, n)
-
-        def partial(slot, a):
-            return sum(dot_nt(grad_ref[slot, :, c * part:(c + 1) * part], w_ref[c, a:a + cut, :]) for c in range(3))
-
-        for a in range(0, width, cut):
-            s.side_out[k, :, a:a + cut] = partial(2 * k + 1 - core, a).astype(jnp.bfloat16)
-        s.side(k).start()
-        for a in range(0, width, cut):
-            acc_ref[:, a:a + cut] = partial(2 * k + core, a)
-        pl.when(j < n - 1)(lambda: s.pass_on(k, acc_ref))
-        return 0
-
-    lax.fori_loop(0, n, one, 0)
-    sums_ref[...] = jnp.zeros(sums_ref.shape, jnp.float32)
-
-    def consume(at, total):
         back, gain, shift = norm_backward(x_ref[at, :].astype(jnp.float32), norm_ref[0:1, :], total)
         result_ref[at, :] = middle_ref[at, :] + back
         sums_ref[0:1, :] += gain
@@ -803,19 +966,21 @@
 
     s.settle(acc_ref, consume)
     s.finish()
-
-
-def first_branch(grad, w, x, grad_middle, norms, n, number, pieces=4):
+    grads.finish()
+
+
+def first_branch(grad, w, x, grad_middle, norms, wide, narrow, n, number, pieces=4):
     rows, width = x.shape
     f32 = jnp.float32
     return pl.pallas_call(functools.partial(first_kernel, n, pieces),
-        out_shape=(jax.ShapeDtypeStruct((rows, width), f32), jax.ShapeDtypeStruct((2, width), f32)),
-        in_specs=[VM] * 5, out_specs=(VM,) * 2,
-        scratch_shapes=[pltpu.VMEM((rows, width), f32)] + scatter_scratch(n, pieces, rows, width),
-        compiler_params=params(number), cost_estimate=lasting(85), name="first_branch")(grad.reshape(2 * n, rows, grad.shape[1]), w, x, grad_middle, norms)
-
-
-def total_kernel(x_ref, out_ref, parts, groups, send_one, recv_one, send_two, recv_two, send_three, recv_three):
+        out_shape=(jax.ShapeDtypeStruct((rows, width), f32), jax.ShapeDtypeStruct((2, width), f32),
+                   jax.ShapeDtypeStruct(wide.shape, wide.dtype), jax.ShapeDtypeStruct(narrow.shape, narrow.dtype)),
+        in_specs=[VM] * 5 + [ANYWHERE] * 2, out_specs=(VM,) * 2 + (ANYWHERE,) * 2,
+        scratch_shapes=exchange_scratch(2, wide.shape[0]) + [pltpu.VMEM((rows, width), f32)] + scatter_scratch(n, pieces, rows, width),
+        compiler_params=params(number), cost_estimate=lasting(85), name="first_branch")(grad.reshape(2 * n, rows, grad.shape[1]), w, x, grad_middle, norms, wide, narrow)
+
+
+def total_kernel(x_ref, bias_ref, out_ref, bias_out_ref, parts, groups, biases, send_one, recv_one, send_two, recv_two, send_three, recv_three, send_bias, recv_bias):
     t, g = lax.axis_index("tensor"), lax.axis_index("dp")
     count, group_count = parts.shape[0], groups.shape[0]
     barrier = pltpu.get_barrier_semaphore()
@@ -841,6 +1006,10 @@
     def keep_one():
         parts[t] = x_ref[t]
 
+    biases[g] = bias_ref[...]
+    for i in range(group_count):
+        pl.when(i != g)(lambda: spread(biases.at[g], biases.at[g], send_bias, recv_bias, g, "dp", i).start())
+
     def keep_two():
         groups[g] = sum_of(parts)
 
@@ -854,24 +1023,32 @@
     keep_two()
     exchange(g, group_count, lambda j, at: spread(groups.at[g], groups.at[at], send_two, recv_two, at, "dp", j), lambda: None)
     out_ref[t] = sum_of(groups)
+    for i in range(group_count):
+        pl.when(i != g)(lambda: spread(biases.at[g], biases.at[i], send_bias, recv_bias, i, "dp", i).wait_recv())
+    bias_out_ref[...] = sum_of(biases)
+    for i in range(group_count):
+        pl.when(i != g)(lambda: spread(biases.at[g], biases.at[g], send_bias, recv_bias, g, "dp", i).wait_send())
     exchange(t, count, lambda j, at: spread(out_ref.at[t], out_ref.at[at], send_three, recv_three, at, "tensor", j), lambda: None)
 
 
-def total_over_all(x, count, group_count, number):
+def total_over_all(x, bias, count, group_count, number):
     rows, width = x.shape
     piece = width // count
     shape = jax.ShapeDtypeStruct((count, rows, piece), x.dtype)
-    out = pl.pallas_call(
-        total_kernel, out_shape=shape, in_specs=[VM], out_specs=VM,
+    bias_shape = jax.ShapeDtypeStruct(bias.shape, bias.dtype)
+    out, bias_out = pl.pallas_call(
+        total_kernel, out_shape=(shape, bias_shape), in_specs=[VM] * 2, out_specs=(VM,) * 2,
         scratch_shapes=[
             pltpu.VMEM((count, rows, piece), x.dtype), pltpu.VMEM((group_count, rows, piece), x.dtype),
+            pltpu.VMEM((group_count,) + bias.shape, bias.dtype),
             pltpu.SemaphoreType.DMA((count,)), pltpu.SemaphoreType.DMA((count,)),
             pltpu.SemaphoreType.DMA((group_count,)), pltpu.SemaphoreType.DMA((group_count,)),
             pltpu.SemaphoreType.DMA((count,)), pltpu.SemaphoreType.DMA((count,)),
+            pltpu.SemaphoreType.DMA((group_count,)), pltpu.SemaphoreType.DMA((group_count,)),
         ],
         compiler_params=params(number), cost_estimate=lasting(12), name="total_over_all",
-    )(jnp.transpose(x.reshape(rows, count, piece), (1, 0, 2)))
-    return jnp.transpose(out, (1, 0, 2)).reshape(rows, width)
+    )(jnp.transpose(x.reshape(rows, count, piece), (1, 0, 2)), bias)
+    return jnp.transpose(out, (1, 0, 2)).reshape(rows, width), bias_out
 
 
 def local(
@@ -909,8 +1086,8 @@
     own_start = lax.axis_index("tensor") * local_tokens
     chips = tensor_count // 2
     gate_up_copy, down_copy = (
-        lax.all_gather(gate_up_master.astype(jnp.bfloat16), "dp", axis=1, tiled=True),
-        lax.all_gather(down_master.astype(jnp.bfloat16), "dp", axis=1, tiled=True),
+        lax.all_gather(jnp.swapaxes(gate_up_master, 1, 2).astype(jnp.bfloat16), "dp", axis=0, tiled=False),
+        lax.all_gather(down_master.astype(jnp.bfloat16), "dp", axis=0, tiled=False),
     )
     group = lax.axis_index("dp")
     group_count = lax.axis_size("dp")
@@ -931,51 +1108,42 @@
         lengths, positions, inputs, norm_master, qkv_master, out_master, bias_row, grad_low, chips, group_count, 0
     )
     gathered_one = gathered_one.reshape(group_tokens, D)
-    gathered_two, hidden, grad_gate_up, grad_middle, grad_middle_low, sums_two = mlp(
+    hidden, grad_middle, sums_two, grad_gate_up_w, grad_down = mlp(
         normed_two, gathered_grad, gate_up_copy, down_copy, middle, norm_master, chips, 2
     )
-    block_output, gathered_mid, grad_mixed = down_branch(
-        hidden, down_copy, middle, grad_middle_low, out_copy, chips, 3
-    )
-    hidden = hidden.reshape(group_tokens, hidden.shape[2])
-    grad_gate_up = grad_gate_up.reshape(2, group_tokens, hidden.shape[1])
-    gathered_grad = gathered_grad.reshape(group_tokens, D)
-    gathered_two = gathered_two.reshape(group_tokens, D)
-    gathered_mid = gathered_mid.reshape(group_tokens, D)
+    block_output, grad_mixed, grad_out_w, gate_up_parts, down_parts = down_branch(
+        hidden, down_copy, middle, grad_middle, out_copy, mixed_low, grad_gate_up_w, grad_down, chips, 3
+    )
     grad_mixed = grad_mixed.reshape(group_tokens, width_here)
-    grad_down = jnp.einsum("tf,td->fd", hidden, gathered_grad, preferred_element_type=jnp.float32)
-    grad_gate_up_w = jnp.einsum(
-        "td,ctf->cdf", gathered_two, grad_gate_up, preferred_element_type=jnp.float32
-    )
-    grad_out_w = jnp.einsum(
-        "tw,td->wd", mixed_low, gathered_mid, preferred_element_type=jnp.float32
-    )
     grad_projected, grad_bias = attention_backward(
         lengths, queries, keys, values, keys_flipped, mixed_low, log_totals, grad_mixed, keep, ahead, behind, block_rows
     )
-    grad_bias = grad_bias.reshape(3, heads_here, HEAD_DIM)
-    grad_qkv_w = jnp.einsum(
-        "td,tcw->cdw",
-        gathered_one,
-        grad_projected.reshape(group_tokens, 3, width_here),
-        preferred_element_type=jnp.float32,
-    )
-    input_grad, sums_one = first_branch(
-        grad_projected, qkv_copy, inputs, grad_middle, norm_master, chips, 4
-    )
-    norm_grads = total_over_all(
-        jnp.concatenate([sums_one, sums_two], axis=0), tensor_count, group_count, 5
-    )
-    qkv_grad, gate_up_grad, out_grad, down_grad, bias_grad = (
-        sum_shard(grad_qkv_w, 1),
-        sum_shard(grad_gate_up_w, 1),
-        sum_shard(grad_out_w, 1),
-        sum_shard(grad_down, 1),
-        lax.psum_scatter(grad_bias, "dp", scatter_dimension=2, tiled=True),
+    grad_qkv_w = lax.dot_general(
+        gathered_one, grad_projected, (((0,), (0,)), ((), ())), preferred_element_type=jnp.float32
+    )
+    grad_qkv_w = grad_qkv_w.astype(jnp.bfloat16).reshape(group_count, D // group_count, 3 * width_here)
+    input_grad, sums_one, qkv_parts, out_parts = first_branch(
+        grad_projected, qkv_copy, inputs, grad_middle, norm_master, grad_qkv_w, grad_out_w, chips, 4
+    )
+    gate_up_grad, down_grad, out_grad = sum_parts(gate_up_parts), sum_parts(down_parts), sum_parts(out_parts)
+    qkv_grad = jnp.transpose(sum_parts(qkv_parts).reshape(D // group_count, 3, width_here), (1, 0, 2))
+    norm_grads, bias_grad = total_over_all(
+        jnp.concatenate([sums_one, sums_two], axis=0), grad_bias, tensor_count, group_count, 5
+    )
+    bias_grad = lax.dynamic_slice_in_dim(
+        bias_grad.reshape(3, heads_here, HEAD_DIM), group * bias_master.shape[2], bias_master.shape[2], axis=2
     )
     qkv_new = adamw(qkv_master, qkv_first, qkv_second, qkv_grad, 2.0 / math.sqrt(D), decay_rate)
-    gate_up_new = adamw(
-        gate_up_master, gate_up_first, gate_up_second, gate_up_grad, 2.0 / math.sqrt(D), decay_rate
+    gate_up_new = tuple(
+        jnp.swapaxes(item, 1, 2)
+        for item in adamw(
+            jnp.swapaxes(gate_up_master, 1, 2),
+            jnp.swapaxes(gate_up_first, 1, 2),
+            jnp.swapaxes(gate_up_second, 1, 2),
+            gate_up_grad,
+            2.0 / math.sqrt(D),
+            decay_rate,
+        )
     )
     out_new = adamw(
         out_master, out_first, out_second, out_grad, 16.0 / math.sqrt(HEADS * HEAD_DIM), decay_rate

time: 786 us -> 726 us (0.924)
  matrix products: 46 us -> 11.6 us
  blocking collectives: 15.6 us -> 0 us
  local copies, waits for them, and re-layouts: 27.2 us -> 18.2 us
    dot_general x4 -> x1, matrix products: 46 us -> 11.6 us  [local(): lax.dot_general(gathered_one, grad_projected, (((0,), (0,)), ((), ())), p...]
    unnamed x1 -> x0, blocking collectives: 15.6 us -> none
    sub x6 -> x5, other arithmetic: 23.3 us -> 12.4 us  [adamw(): weight_old - step_rate * (update + decay_part * weight_old)]
    transpose x0 -> x1, other arithmetic: none -> 9.81 us  [local(): jnp.swapaxes(item, 1, 2)]
    unnamed x47 -> x58, local copies, waits for them, and re-layouts: 19.9 us -> 15.1 us
  transfers between devices with their start and end apart: 6 -> 2, of which waited for: 0 -> 0; matrix products, arithmetic and copies ran while one was open for 11% -> 2% of each run, Pallas kernels for 45% -> 29%
where the time goes in v4:
time: 726 us; the launch traced here: 719 us
  Pallas kernels  641 us (88%)
  other arithmetic  32 us (4%)
  local copies, waits for them, and re-layouts  18.2 us (3%)
  between operations  15.5 us (2%)
  matrix products  11.6 us (2%)
    pallas_call x1, Pallas kernels, forward(): pl.pallas_call(functools.partial(forward_kernel, n, group_count, pieces),...  205 us
    pallas_call x1, Pallas kernels, mlp(): pl.pallas_call(functools.partial(mlp_kernel, n, pieces), out_shape=(shape...  167 us
    pallas_call x1, Pallas kernels, down_branch(): pl.pallas_call(functools.partial(down_kernel, n, pieces), out_shape=(jax....  119 us
    pallas_call x1, Pallas kernels, first_branch(): pl.pallas_call(functools.partial(first_kernel, n, pieces), out_shape=(jax...  90.6 us
    pallas_call x1, Pallas kernels, attention_backward(): pl.pallas_call(functools.partial(backward_kernel, block), out_shape=(jax....  45.9 us
    unnamed x58, local copies, waits for them, and re-layouts  15.1 us
  transfers between devices with their start and end apart: 2, of which 0 were waited for; matrix products, arithmetic and copies ran while one was open for 2% of the time, Pallas kernels for 29%

profile of v4, /device:TPU:0, one launch (start us, length us, event | category | flops | bytes accessed | tf_op | source)
XLA Modules:
  0.0 718.6 jit_solution(13928984670335268964)
XLA Ops:
  7.2 0.0 copy-start
  7.2 0.0 all-gather.7.cloned.1.call-start
  7.2 2.5 convert_element_type.82
  9.7 0.0 all-gather.7.cloned.1.call-update
  9.7 0.0 copy-start.19
  9.7 0.0 copy-start.22
  9.8 0.0 all-gather.5.cloned.1.call-start
  9.8 0.0 copy-done
  9.8 1.3 bitcast_convert_fusion
  11.1 0.0 all-gather.5.cloned.1.call-update
  11.9 0.1 broadcast_in_dim.40
  12.0 0.0 copy-done.19
  12.0 0.1 tile.8
  12.1 0.6 reshape_tile.3.frequency_ref
  12.7 0.0 copy-done.22
  12.7 0.6 convert_element_type.80
  13.3 0.0 copy-done.11
  13.3 1.1 broadcast_select_fusion.cot_ref
  14.5 0.6 concatenate.6.bias_ref
  15.1 204.8 %forward.1 = (bf16[8,256,2048]{2,1,0:T(8,128)(2,1)}, bf16[3,2048,256]{2,1,0:T(8,128)(2,1)}, bf16[256,2048]{1,0:T(8,128)(2,1)}, bf16[4,2048,64]{2,1,0:T(8,128)(2,...) custom-call(s32[1]{0:T(128)} %copy.61.length_ref, ...), custom_call_target="tpu_custom_call" | custom-call | flops 219999993856 | tf_op jit(solution)/shard_map/forward/pallas_call | solution.py:657
  219.9 0.0 copy-done.7
  219.9 1.6 copy.55
  221.5 3.1 copy.51
  224.7 0.0 copy-done.8
  224.7 1.6 copy.53
  226.3 167.5 %mlp.1 = (bf16[8,256,704]{2,1,0:T(8,128)(2,1)}, f32[256,2048]{1,0:T(8,128)}, f32[2,2048]{1,0:T(2,128)}, bf16[4,2,704,512]{3,2,1,0:T(8,128)(2,1)}, bf16[4,704,512]{2,1,0:T(8,128)(2,1)}) custom-call(bf16[256,2048]{1,0:T(8,128)(2,1)} %get-tuple-element.53.x_ref, bf16[8,256,2048]{2,1,0:T(8,128)(2,1)} %get-tuple-element.54.cots_hbm, ...), custom_call_target="tpu_custom_call" | custom-call | flops 153999998976 | tf_op jit(solution)/shard_map/mlp/pallas_call | solution.py:857
  393.8 118.7 %down_branch.1 = (bf16[256,2048]{1,0:T(8,128)(2,1)}, bf16[8,256,256]{2,1,0:T(8,128)(2,1)}, bf16[4,256,512]{2,1,0:T(8,128)(2,1)}, bf16[4,2,704,512]{3,2,1,0:T(8,128)(2,1)}, bf16[4,704,512]{2,1,0:T(8,128)(2,1)}) custom-call(bf16[8,256,704]{2,1,0:T(8,128)(2,1)} %get-tuple-element.56.hidden_ref, bf16[4,704,512]{2,1,0:T(8,128)(2,1)} %bitcast.83, ...), custom_call_target="tpu_custom_call" | custom-call | flops 126500003840 | tf_op jit(solution)/shard_map/down_branch/pallas_call | solution.py:923
  512.4 45.9 %attention_backward.1 = (bf16[2048,768]{1,0:T(8,128)(2,1)}, f32[1,768]{1,0:T(1,128)}) custom-call(s32[1]{0:T(128)} %copy.61.length_ref, bf16[4,2048,64]{2,1,0:T(8,128)(2,1)} %get-tuple-element.63.q_ref, bf16[4,2048,64]{2,1,0:T(8,128)(2,1)} %get-tuple-element.64.k_ref, bf16[4,2048,64]{2,1,0:T(8,128)(2,1)} %get-tuple-element.65.v_ref, ...), custom_call_target="tpu_custom_call" | custom-call | flops 21474836480 | bytes 15728640 | tf_op jit(solution)/shard_map/attention_backward/pallas_call | solution.py:177
  558.3 11.6 %convolution_convert_fusion = bf16[2048,768]{1,0:T(8,128)(2,1)} fusion(bf16[2048,2048]{1,0:T(8,128)(2,1)} %bitcast.84, bf16[2048,768]{1,0:T(8,128)(2,1)} %get-tuple-element.72), kind=kOutput, calls=%fused_computation.1 | convolution fusion | flops 6444023808 | bytes 14680064 | tf_op jit(solution)/shard_map/dot_general | solution.py:1121
  569.9 90.6 %first_branch.1 = (f32[256,2048]{1,0:T(8,128)}, f32[2,2048]{1,0:T(2,128)}, bf16[4,512,768]{2,1,0:T(8,128)(2,1)}, bf16[4,256,512]{2,1,0:T(8,128)(2,1)}) custom-call(bf16[8,256,768]{2,1,0:T(8,128)(2,1)} %bitcast.85, bf16[3,2048,256]{2,1,0:T(8,128)(2,1)} %get-tuple-element.73.w_ref, bf16[256,2048]{1,0:T(8,128)(2,1)} %x_ref.3, ...), custom_call_target="tpu_custom_call" | custom-call | flops 93499998208 | tf_op jit(solution)/shard_map/first_branch/pallas_call | solution.py:975
  660.5 0.0 copy-done.21
  660.5 1.4 pad_maximum_fusion
  661.9 13.7 %total_over_all.1 = (f32[8,4,256]{2,1,0:T(4,128)}, f32[1,768]{1,0:T(1,128)}) custom-call(f32[8,4,256]{2,1,0:T(4,128)} %bitcast.79, f32[1,768]{1,0:T(1,128)} %get-tuple-element.83.bias_ref), custom_call_target="tpu_custom_call" | custom-call | flops 13200000000 | tf_op jit(solution)/shard_map/total_over_all/pallas_call | solution.py:1039
  675.6 0.7 reduce
  676.3 0.1 reshape.157
  676.4 2.2 convert_add_fusion.1
  678.6 0.0 copy-start.2
  678.6 1.6 copy.52
  680.2 0.0 copy-done.2
  680.2 5.2 multiply_subtract_fusion
  685.4 3.1 copy.56
  688.6 0.0 copy-done.3
  688.6 1.6 copy.57
  690.2 0.0 copy-start.13
  690.2 0.0 copy-start.14
  690.2 1.6 copy.58
  691.8 0.0 copy-done.15
  691.8 0.0 copy-done.17
  691.8 0.7 multiply_subtract_fusion.3
  692.5 0.0 copy-done.13
  692.5 2.8 multiply_subtract_fusion.2
  695.4 0.0 copy-start.9
  695.4 0.0 copy-start.10
  695.4 9.8 %fusion.9 = (f32[2,512,704]{1,2,0:T(8,128)}, f32[2,512,704]{1,2,0:T(8,128)}, f32[2,512,704]{1,2,0:T(8,128)}) fusion(f32[2,512,704]{1,2,0:T(8,128)} %param.39, bf16[4,2,704,512]{3,2,1,0:T(8,128)(2,1)} %get-tuple-element.78, f32[2,512,704]{1,2,0:T(8,128)} %param.33, f32[2,512,704]{1,2,0:T(8,128)S(1)} %copy-done.1), kind=kLoop, calls=%fused_computation.26 | loop fusion | flops 15859712 | bytes 23068672 | tf_op jit(solution)/shard_map/transpose | solution.py:1138
  705.2 0.0 copy-done.4
  705.3 0.0 copy-start.20
  705.3 0.0 copy-start.23
  705.3 0.0 copy-start.24
  705.3 0.0 copy-start.12
  705.3 3.0 multiply_subtract_fusion.1
  708.3 0.0 copy-done.23
  708.4 0.7 multiply_subtract_fusion.4
  709.1 1.0 copy.62
  710.0 1.3 copy.63
  (33 shorter events, 0.1 us)
Async XLA Ops:
  7.2 2.6 copy-start
  7.2 219.1 %all-gather.7.cloned.1.call-start = ((), (), s32[]{:S(2)}) async-start(), calls=%async_computation.1 | async-start | bytes 3604480 | tf_op jit(solution)/shard_map/all_gather | solution.py:1090
  9.7 2.3 copy-start.19
  9.7 3.0 copy-start.22
  9.8 216.5 %all-gather.5.cloned.1.call-start = ((), (), s32[]{:S(2)}) async-start(), calls=%async_computation | async-start | bytes 7208960 | tf_op jit(solution)/shard_map/all_gather | solution.py:1089
  11.1 2.2 copy-start.11
  15.1 204.9 %copy-start.7 = (f32[3,512,256]{2,1,0:T(8,128)S(1)}, f32[3,512,256]{2,1,0:T(8,128)}, u32[]{:S(2)}) copy-start(f32[3,512,256]{2,1,0:T(8,128)} %qkv_ref.1) | copy-start | bytes 4718596
  221.5 3.1 copy-start.8
  569.9 90.6 %copy-start.21 = (f32[2,2048]{1,0:T(2,128)S(1)}, f32[2,2048]{1,0:T(2,128)}, u32[]{:S(2)}) copy-start(f32[2,2048]{1,0:T(2,128)} %get-tuple-element.82) | copy-start | bytes 49156
  678.6 1.6 copy-start.2
  685.4 3.1 copy-start.3
  690.2 1.7 copy-start.15
  690.2 1.7 copy-start.16
  690.2 1.7 copy-start.17
  690.2 1.7 copy-start.18
  690.2 2.3 copy-start.13
  690.2 2.3 copy-start.14
  692.5 2.8 copy-start.1
  695.4 9.8 %copy-start.4 = (f32[704,512]{1,0:T(8,128)S(1)}, f32[704,512]{1,0:T(8,128)}, u32[]{:S(2)}) copy-start(f32[704,512]{1,0:T(8,128)} %param.29) | copy-start | bytes 4325380
  695.4 9.8 %copy-start.5 = (bf16[4,704,512]{2,1,0:T(8,128)(2,1)S(1)}, bf16[4,704,512]{2,1,0:T(8,128)(2,1)}, u32[]{:S(2)}) copy-start(bf16[4,704,512]{2,1,0:T(8,128)(2,1)} %get-tuple-element.80) | copy-start | bytes 8650756
  695.4 9.8 %copy-start.9 = (f32[704,512]{1,0:T(8,128)S(1)}, f32[704,512]{1,0:T(8,128)}, u32[]{:S(2)}) copy-start(f32[704,512]{1,0:T(8,128)} %param.35) | copy-start | bytes 4325380
  695.4 9.8 %copy-start.10 = (f32[704,512]{1,0:T(8,128)S(1)}, f32[704,512]{1,0:T(8,128)}, u32[]{:S(2)}) copy-start(f32[704,512]{1,0:T(8,128)} %param.41) | copy-start | bytes 4325380
  705.3 3.1 copy-start.20
  705.3 3.1 copy-start.23
  705.3 3.1 copy-start.24
  705.3 3.8 copy-start.12
  708.4 1.7 copy-start.6
Sparse Core Ops, SparseCore 0:
  10.4 82.1 all-gather.6
  95.1 65.8 all-gather.4

commit v5 on v4

--- a/solution.py
+++ b/solution.py
@@ -89,110 +89,6 @@
     return jnp.where(allowed, s, mask_fill)
 
 
-def backward_kernel(block, length_ref, q_ref, k_ref, v_ref, kt_ref, o_ref, lse_ref, do_ref,
-                    keep_ref, ahead_ref, behind_ref, out_ref, bias_ref,
-                    dos_ref, delta_ref, dqt_ref, dk_ref, dv_ref):
-    heads, rows, _ = q_ref.shape
-    width = heads * HEAD_DIM
-    groups = width // LANES
-    per_group = LANES // HEAD_DIM
-    blocks = rows // block
-    length = length_ref[0]
-
-    def prepare(i, _):
-        at = pl.ds(pl.multiple_of(i * block, block), block)
-        for g in range(groups):
-            lanes = slice(g * LANES, (g + 1) * LANES)
-            grad = do_ref[at, lanes]
-            for p in range(per_group):
-                dos_ref[g * per_group + p, at, :] = grad[:, p * HEAD_DIM:(p + 1) * HEAD_DIM]
-            both = (grad.astype(jnp.float32) * o_ref[at, lanes].astype(jnp.float32)).T
-            for p in range(per_group):
-                h = g * per_group + p
-                delta_ref[h:h + 1, at] = jnp.sum(both[p * HEAD_DIM:(p + 1) * HEAD_DIM], axis=0, keepdims=True)
-        dqt_ref[:, at] = jnp.zeros((width, block), jnp.float32)
-        return 0
-
-    lax.fori_loop(0, blocks, prepare, 0)
-
-    def key_block(j, _):
-        key_start = pl.multiple_of(j * block, block)
-        keys_at = pl.ds(key_start, block)
-
-        def query_block(i, carry, kind):
-            at = pl.ds(pl.multiple_of(i * block, block), block)
-            out = []
-            for h in range(heads):
-                dk, dv = carry[h]
-                keys, queries, grad = k_ref[h, keys_at, :], q_ref[h, at, :], dos_ref[h, at, :]
-                s = dot_nt(keys, queries) * (score_scale * log2_e)
-                if kind > 0:
-                    s = masked_scores(s, key_start, i * block, length, kind == 2)
-                p = jnp.exp2(s - lse_ref[h:h + 1, at])
-                dp = dot_nt(v_ref[h, keys_at, :], grad)
-                ds = (p * (dp - delta_ref[h:h + 1, at])).astype(jnp.bfloat16)
-                dv = dv + dot_nn(p.astype(jnp.bfloat16), grad)
-                dk = dk + dot_nn(ds, queries)
-                here = slice(h * HEAD_DIM, (h + 1) * HEAD_DIM)
-                dqt_ref[here, at] += dot_nn(kt_ref[here, keys_at], ds)
-                out.append((dk, dv))
-            return tuple(out)
-
-        zero = jnp.zeros((block, HEAD_DIM), jnp.float32)
-        carry = query_block(j, tuple((zero, zero) for _ in range(heads)), 2)
-        whole = key_start + block <= length
-        carry = lax.fori_loop(j + 1, jnp.where(whole, blocks, j + 1), lambda i, c: query_block(i, c, 0), carry)
-        carry = lax.fori_loop(j + 1, jnp.where(whole, j + 1, blocks), lambda i, c: query_block(i, c, 1), carry)
-        for h in range(heads):
-            dk_ref[h, keys_at, :] = carry[h][0]
-            dv_ref[h, keys_at, :] = carry[h][1]
-        return 0
-
-    lax.fori_loop(0, blocks, key_block, 0)
-    bias_ref[...] = jnp.zeros(bias_ref.shape, jnp.float32)
-
-    def finish(i, _):
-        at = pl.ds(pl.multiple_of(i * block, block), block)
-        keep, ahead, behind = keep_ref[at, :], -ahead_ref[at, :], -behind_ref[at, :]
-        for g in range(groups):
-            lanes = slice(g * LANES, (g + 1) * LANES)
-            dq = dqt_ref[lanes, at].T
-            dk = jnp.concatenate([dk_ref[g * per_group + p, at, :] for p in range(per_group)], axis=1)
-            dv = jnp.concatenate([dv_ref[g * per_group + p, at, :] for p in range(per_group)], axis=1)
-            parts = (spin(dq * score_scale, keep, ahead, behind), spin(dk * score_scale, keep, ahead, behind), dv)
-            for c in range(3):
-                low = parts[c].astype(jnp.bfloat16)
-                place = slice(c * width + g * LANES, c * width + (g + 1) * LANES)
-                out_ref[at, place] = low
-                bias_ref[:, place] += jnp.sum(low.astype(jnp.float32), axis=0, keepdims=True)
-        return 0
-
-    lax.fori_loop(0, blocks, finish, 0)
-
-
-def attention_backward(lengths, q, k, v, kt, o, lse, grad, keep, ahead, behind, block):
-    heads, rows, _ = q.shape
-    width = heads * HEAD_DIM
-    vm = pl.BlockSpec(memory_space=pltpu.VMEM)
-    return pl.pallas_call(
-        functools.partial(backward_kernel, block),
-        out_shape=(jax.ShapeDtypeStruct((rows, 3 * width), jnp.bfloat16),
-                   jax.ShapeDtypeStruct((1, 3 * width), jnp.float32)),
-        in_specs=[pl.BlockSpec(memory_space=pltpu.SMEM)] + [vm] * 10,
-        out_specs=(vm,) * 2,
-        scratch_shapes=[
-            pltpu.VMEM((heads, rows, HEAD_DIM), jnp.bfloat16),
-            pltpu.VMEM((heads, rows), jnp.float32),
-            pltpu.VMEM((width, rows), jnp.float32),
-            pltpu.VMEM((heads, rows, HEAD_DIM), jnp.float32),
-            pltpu.VMEM((heads, rows, HEAD_DIM), jnp.float32),
-        ],
-        compiler_params=pltpu.CompilerParams(vmem_limit_bytes=VMEM_LIMIT),
-        cost_estimate=pl.CostEstimate(flops=heads * rows * rows * HEAD_DIM * 20, bytes_accessed=rows * width * 30, transcendentals=heads * rows * rows),
-        name="attention_backward",
-    )(lengths, q, k, v, kt, o, lse, grad, keep, ahead, behind)
-
-
 VM = pl.BlockSpec(memory_space=pltpu.VMEM)
 ANYWHERE = pl.BlockSpec(memory_space=pl.ANY)
 MESH = pl.DeviceIdType.MESH
@@ -423,14 +319,14 @@
             src_ref=src.at[peer], dst_ref=dst.at[slot], send_sem=self.send.at[index, peer],
             recv_sem=self.recv.at[index, slot], device_id={"dp": peer}, device_id_type=MESH)
 
-    def others(self, body):
-        for index in range(len(self.pairs)):
+    def others(self, body, which=None):
+        for index in range(len(self.pairs)) if which is None else which:
             for i in range(self.count):
                 pl.when(i != self.group)(lambda: body(index, i))
 
-    def start(self):
-        self.others(lambda index, i: self.copy(index, i, self.group).start())
-        for index in range(len(self.pairs)):
+    def start(self, which=None):
+        self.others(lambda index, i: self.copy(index, i, self.group).start(), which)
+        for index in range(len(self.pairs)) if which is None else which:
             self.stay(index).start()
 
     def finish(self):
@@ -929,34 +825,153 @@
         compiler_params=params(number), cost_estimate=lasting(115), name="down_branch")(hidden, down, middle, x, out, mixed, wide, narrow)
 
 
-def first_kernel(n, pieces, grad_ref, w_ref, x_ref, middle_ref, norm_ref, wide_ref, low_ref, result_ref, sums_ref, wide_parts, low_parts,
-                 local_sems, share_send, share_recv, acc_ref, side_out, side_in, line_in, side_sems, line_send, line_recv):
-    group_count = wide_ref.shape[0]
+def backward_kernel(n, pieces, length_ref, q_ref, k_ref, v_ref, kt_ref, o_ref, lse_ref, do_ref,
+                    keep_ref, ahead_ref, behind_ref, w_ref, x_ref, middle_ref, norm_ref, xs_hbm, low_ref,
+                    result_ref, sums_ref, bias_ref, wide_parts, low_parts,
+                    dos_ref, delta_ref, dqt_ref, dk_ref, dv_ref, grad_ref, wide_ref, strips_ref, acc_ref, side_out, side_in, line_in,
+                    strip_sems, side_sems, line_send, line_recv, local_sems, share_send, share_recv):
+    group_count = low_ref.shape[0]
     greet_all(n, group_count)
-    grads = Exchange(group_count, ((wide_ref, wide_parts), (low_ref, low_parts)), local_sems, share_send, share_recv)
-    grads.start()
+    heads, tokens, _ = q_ref.shape
+    width = heads * HEAD_DIM
+    rows, features = x_ref.shape
+    lane_groups = width // LANES
+    per_group = LANES // HEAD_DIM
+    pair = 2 * rows
+    depth = features // group_count
+    length = length_ref[0]
     s = Scatter(n, pieces, side_out, side_in, line_in, side_sems, line_send, line_recv)
     m, core = s.m, s.core
-    width = w_ref.shape[1]
-    part = w_ref.shape[2]
-    cut = min(512, width)
-
-    def one(j, _):
-        k = near(n - 1 - j, m, n)
-
-        def partial(slot, a):
-            return sum(dot_nt(grad_ref[slot, :, c * part:(c + 1) * part], w_ref[c, a:a + cut, :]) for c in range(3))
-
-        for a in range(0, width, cut):
-            s.side_out[k, :, a:a + cut] = partial(2 * k + 1 - core, a).astype(jnp.bfloat16)
-        s.side(k).start()
-        for a in range(0, width, cut):
+    grads = Exchange(group_count, ((low_ref, low_parts), (wide_ref, wide_parts)), local_sems, share_send, share_recv)
+    grads.start((0,))
+    strip = min(256, depth)
+    strip_count = features // strip
+
+    def strip_copy(index, slot):
+        return pltpu.make_async_copy(
+            xs_hbm.at[:, :, pl.ds(pl.multiple_of(index * strip, strip), strip)], strips_ref.at[slot], strip_sems.at[slot])
+
+    for slot in range(2):
+        strip_copy(slot, slot).start()
+    bias_ref[...] = jnp.zeros(bias_ref.shape, jnp.float32)
+    sums_ref[...] = jnp.zeros(sums_ref.shape, jnp.float32)
+
+    def prepare(i, _):
+        at = pl.ds(pl.multiple_of(i * pair, pair), pair)
+        for a in range(lane_groups):
+            lanes = slice(a * LANES, (a + 1) * LANES)
+            grad = do_ref[at, lanes]
+            for b in range(per_group):
+                dos_ref[a * per_group + b, at, :] = grad[:, b * HEAD_DIM:(b + 1) * HEAD_DIM]
+            both = (grad.astype(jnp.float32) * o_ref[at, lanes].astype(jnp.float32)).T
+            for b in range(per_group):
+                h = a * per_group + b
+                delta_ref[h:h + 1, at] = jnp.sum(both[b * HEAD_DIM:(b + 1) * HEAD_DIM], axis=0, keepdims=True)
+        dqt_ref[:, at] = jnp.zeros((width, pair), jnp.float32)
+        for h in range(heads):
+            dk_ref[h, at, :] = jnp.zeros((pair, HEAD_DIM), jnp.float32)
+            dv_ref[h, at, :] = jnp.zeros((pair, HEAD_DIM), jnp.float32)
+        return 0
+
+    lax.fori_loop(0, n, prepare, 0)
+
+    falling = 2 * m < n - 1
+
+    def order(step):
+        return jnp.where(falling, n - 1 - step, step)
+
+    def finish_block(step):
+        j = order(step)
+
+        def tile(i, j, causal):
+            at = pl.ds(pl.multiple_of(i * pair, pair), pair)
+            key_start = pl.multiple_of(j * pair, pair)
+            keys_at = pl.ds(key_start, pair)
+            for h in range(heads):
+                keys, queries, grad = k_ref[h, keys_at, :], q_ref[h, at, :], dos_ref[h, at, :]
+                scores = dot_nt(keys, queries) * (score_scale * log2_e)
+                scores = masked_scores(scores, key_start, i * pair, length, causal)
+                p = jnp.exp2(scores - lse_ref[h:h + 1, at])
+                dp = dot_nt(v_ref[h, keys_at, :], grad)
+                ds = (p * (dp - delta_ref[h:h + 1, at])).astype(jnp.bfloat16)
+                dv_ref[h, keys_at, :] += dot_nn(p.astype(jnp.bfloat16), grad)
+                dk_ref[h, keys_at, :] += dot_nn(ds, queries)
+                here = slice(h * HEAD_DIM, (h + 1) * HEAD_DIM)
+                dqt_ref[here, at] += dot_nn(kt_ref[here, keys_at], ds)
+
+        def other(u, _):
+            tile(jnp.where(falling, j, j + u), jnp.where(falling, j - u, j), False)
+            return 0
+
+        tile(j, j, True)
+        lax.fori_loop(1, n - step, other, 0)
+        keys_at = pl.ds(pl.multiple_of(j * pair, pair), pair)
+        keep, ahead, behind = keep_ref[keys_at, :], -ahead_ref[keys_at, :], -behind_ref[keys_at, :]
+        for a in range(lane_groups):
+            lanes = slice(a * LANES, (a + 1) * LANES)
+            heads_here = range(a * per_group, (a + 1) * per_group)
+            dq = dqt_ref[lanes, keys_at].T
+            dk = jnp.concatenate([dk_ref[h, keys_at, :] for h in heads_here], axis=1)
+            dv = jnp.concatenate([dv_ref[h, keys_at, :] for h in heads_here], axis=1)
+            parts = (spin(dq * score_scale, keep, ahead, behind), spin(dk * score_scale, keep, ahead, behind), dv)
+            for c in range(3):
+                low = parts[c].astype(jnp.bfloat16)
+                place_here = slice(c * width + a * LANES, c * width + (a + 1) * LANES)
+                grad_ref[keys_at, place_here] = low
+                bias_ref[:, place_here] += jnp.sum(low.astype(jnp.float32), axis=0, keepdims=True)
+
+    cut = min(512, features)
+
+    def partial(slot, a):
+        at = pl.ds(pl.multiple_of(slot * rows, rows), rows)
+        return sum(dot_nt(grad_ref[at, c * width:(c + 1) * width], w_ref[c, a:a + cut, :]) for c in range(3))
+
+    def own_partial(k):
+        for a in range(0, features, cut):
             acc_ref[:, a:a + cut] = partial(2 * k + core, a)
-        pl.when(j < n - 1)(lambda: s.pass_on(k, acc_ref))
+
+    def strip_gradient(index, _):
+        slot = lax.rem(index, 2)
+        strip_copy(index, slot).wait()
+        x = strips_ref[slot].reshape(tokens, strip).T
+        owner = lax.div(index * strip, depth)
+        at = pl.ds(pl.multiple_of(lax.rem(index * strip, depth), strip), strip)
+        for c in range(3):
+            wide_ref[owner, c, at, :] = dot_nn(x, grad_ref[:, c * width:(c + 1) * width]).astype(jnp.bfloat16)
+        pl.when(index + 2 < strip_count)(lambda: strip_copy(index + 2, slot).start())
         return 0
 
-    lax.fori_loop(0, n, one, 0)
-    sums_ref[...] = jnp.zeros(sums_ref.shape, jnp.float32)
+    def step(j, _):
+        @pl.when(j < n)
+        def _():
+            finish_block(j)
+            k = order(j)
+            for a in range(0, features, cut):
+                s.side_out[k, :, a:a + cut] = partial(2 * k + 1 - core, a).astype(jnp.bfloat16)
+            s.side(k).start()
+
+        @pl.when(j == n - 1)
+        def _():
+            lax.fori_loop(0, strip_count, strip_gradient, 0)
+            grads.start((1,))
+
+        def one(late, _):
+            turn = jnp.where(late == 1, j - 2, j)
+            k = order(turn)
+            inner = ((k > m) & (m > 0)) | ((k < m) & (m < n - 1))
+
+            @pl.when((turn >= 0) & (turn < n) & (k != m) & (inner == (late == 1)))
+            def _():
+                own_partial(k)
+                s.pass_on(k, acc_ref)
+
+            return 0
+
+        lax.fori_loop(0, 2, one, 0)
+        return 0
+
+    lax.fori_loop(0, n + 2, step, 0)
+    own_partial(m)
 
     def consume(at, total):
         back, gain, shift = norm_backward(x_ref[at, :].astype(jnp.float32), norm_ref[0:1, :], total)
@@ -969,15 +984,30 @@
     grads.finish()
 
 
-def first_branch(grad, w, x, grad_middle, norms, wide, narrow, n, number, pieces=4):
-    rows, width = x.shape
-    f32 = jnp.float32
-    return pl.pallas_call(functools.partial(first_kernel, n, pieces),
-        out_shape=(jax.ShapeDtypeStruct((rows, width), f32), jax.ShapeDtypeStruct((2, width), f32),
-                   jax.ShapeDtypeStruct(wide.shape, wide.dtype), jax.ShapeDtypeStruct(narrow.shape, narrow.dtype)),
-        in_specs=[VM] * 5 + [ANYWHERE] * 2, out_specs=(VM,) * 2 + (ANYWHERE,) * 2,
-        scratch_shapes=exchange_scratch(2, wide.shape[0]) + [pltpu.VMEM((rows, width), f32)] + scatter_scratch(n, pieces, rows, width),
-        compiler_params=params(number), cost_estimate=lasting(85), name="first_branch")(grad.reshape(2 * n, rows, grad.shape[1]), w, x, grad_middle, norms, wide, narrow)
+def backward(lengths, q, k, v, kt, o, lse, grad, keep, ahead, behind, w, x, grad_middle, norms, xs, narrow, n, number, pieces=4):
+    rows, features = x.shape
+    heads, tokens, _ = q.shape
+    width = heads * HEAD_DIM
+    group_count = narrow.shape[0]
+    depth = features // group_count
+    f32, low = jnp.float32, jnp.bfloat16
+    shape = jax.ShapeDtypeStruct
+    wide = (group_count, 3, depth, width)
+    strip = min(256, depth)
+    scatter = scatter_scratch(n, pieces, rows, features)
+    return pl.pallas_call(functools.partial(backward_kernel, n, pieces),
+        out_shape=(shape((rows, features), f32), shape((2, features), f32), shape((1, 3 * width), f32),
+                   shape(wide, low), shape(narrow.shape, low)),
+        in_specs=[pl.BlockSpec(memory_space=pltpu.SMEM)] + [VM] * 14 + [ANYWHERE] * 2,
+        out_specs=(VM,) * 3 + (ANYWHERE,) * 2,
+        scratch_shapes=[
+            pltpu.VMEM((heads, tokens, HEAD_DIM), low), pltpu.VMEM((heads, tokens), f32), pltpu.VMEM((width, tokens), f32),
+            pltpu.VMEM((heads, tokens, HEAD_DIM), f32), pltpu.VMEM((heads, tokens, HEAD_DIM), f32),
+            pltpu.VMEM((tokens, 3 * width), low), pltpu.VMEM(wide, low), pltpu.VMEM((2, 2 * n, rows, strip), low),
+            pltpu.VMEM((rows, features), f32),
+        ] + scatter[:3] + [pltpu.SemaphoreType.DMA((2,))] + scatter[3:] + exchange_scratch(2, group_count),
+        compiler_params=params(number), cost_estimate=lasting(125), name="backward",
+    )(lengths, q, k, v, kt, o, lse, grad, keep, ahead, behind, w, x, grad_middle, norms, xs, narrow)
 
 
 def total_kernel(x_ref, bias_ref, out_ref, bias_out_ref, parts, groups, biases, send_one, recv_one, send_two, recv_two, send_three, recv_three, send_bias, recv_bias):
@@ -1080,7 +1110,6 @@
     group_tokens = local_tokens * tensor_count
     row_count = lengths.shape[0]
     row_length = group_tokens // row_count
-    block_rows = min(512, row_length)
     heads_here = bias_master.shape[1]
     width_here = heads_here * HEAD_DIM
     own_start = lax.axis_index("tensor") * local_tokens
@@ -1107,7 +1136,6 @@
     ) = forward(
         lengths, positions, inputs, norm_master, qkv_master, out_master, bias_row, grad_low, chips, group_count, 0
     )
-    gathered_one = gathered_one.reshape(group_tokens, D)
     hidden, grad_middle, sums_two, grad_gate_up_w, grad_down = mlp(
         normed_two, gathered_grad, gate_up_copy, down_copy, middle, norm_master, chips, 2
     )
@@ -1115,18 +1143,12 @@
         hidden, down_copy, middle, grad_middle, out_copy, mixed_low, grad_gate_up_w, grad_down, chips, 3
     )
     grad_mixed = grad_mixed.reshape(group_tokens, width_here)
-    grad_projected, grad_bias = attention_backward(
-        lengths, queries, keys, values, keys_flipped, mixed_low, log_totals, grad_mixed, keep, ahead, behind, block_rows
-    )
-    grad_qkv_w = lax.dot_general(
-        gathered_one, grad_projected, (((0,), (0,)), ((), ())), preferred_element_type=jnp.float32
-    )
-    grad_qkv_w = grad_qkv_w.astype(jnp.bfloat16).reshape(group_count, D // group_count, 3 * width_here)
-    input_grad, sums_one, qkv_parts, out_parts = first_branch(
-        grad_projected, qkv_copy, inputs, grad_middle, norm_master, grad_qkv_w, grad_out_w, chips, 4
+    input_grad, sums_one, grad_bias, qkv_parts, out_parts = backward(
+        lengths, queries, keys, values, keys_flipped, mixed_low, log_totals, grad_mixed, keep, ahead, behind,
+        qkv_copy, inputs, grad_middle, norm_master, gathered_one, grad_out_w, chips, 4
     )
     gate_up_grad, down_grad, out_grad = sum_parts(gate_up_parts), sum_parts(down_parts), sum_parts(out_parts)
-    qkv_grad = jnp.transpose(sum_parts(qkv_parts).reshape(D // group_count, 3, width_here), (1, 0, 2))
+    qkv_grad = sum_parts(qkv_parts)
     norm_grads, bias_grad = total_over_all(
         jnp.concatenate([sums_one, sums_two], axis=0), grad_bias, tensor_count, group_count, 5
     )

time: 726 us -> 671 us (0.924)
  Pallas kernels: 641 us -> 614 us
  matrix products: 11.6 us -> 0 us
  local copies, waits for them, and re-layouts: 18.2 us -> 6.74 us
    pallas_call x2 -> x1, Pallas kernels: 136 us -> 108 us  [backward(): pl.pallas_call(functools.partial(backward_kernel, n, pieces), out_shape=(...]
    dot_general x1 -> x0, matrix products: 11.6 us -> none  [local(): lax.dot_general(gathered_one, grad_projected, (((0,), (0,)), ((), ())), p...]
    unnamed x58 -> x50, local copies, waits for them, and re-layouts: 15.1 us -> 5.27 us
  transfers between devices with their start and end apart: 2 -> 2, of which waited for: 0 -> 0; matrix products, arithmetic and copies ran while one was open for 2% -> 1% of each run, Pallas kernels for 29% -> 31%
where the time goes in v5:
time: 671 us; the launch traced here: 664 us
  Pallas kernels  614 us (92%)
  other arithmetic  27.8 us (4%)
  between operations  15.3 us (2%)
  local copies, waits for them, and re-layouts  6.74 us (1%)
    pallas_call x1, Pallas kernels, forward(): pl.pallas_call(functools.partial(forward_kernel, n, group_count, pieces),...  205 us
    pallas_call x1, Pallas kernels, mlp(): pl.pallas_call(functools.partial(mlp_kernel, n, pieces), out_shape=(shape...  168 us
    pallas_call x1, Pallas kernels, down_branch(): pl.pallas_call(functools.partial(down_kernel, n, pieces), out_shape=(jax....  119 us
    pallas_call x1, Pallas kernels, backward(): pl.pallas_call(functools.partial(backward_kernel, n, pieces), out_shape=(...  108 us
    pallas_call x1, Pallas kernels, total_over_all(): pl.pallas_call(total_kernel, out_shape=(shape, bias_shape), in_specs=[VM]...  14.4 us
    sub x5, other arithmetic, adamw(): weight_old - step_rate * (update + decay_part * weight_old)  13.9 us
  transfers between devices with their start and end apart: 2, of which 0 were waited for; matrix products, arithmetic and copies ran while one was open for 1% of the time, Pallas kernels for 31%

profile of v5, /device:TPU:0, one launch (start us, length us, event | category | flops | bytes accessed | tf_op | source)
XLA Modules:
  0.0 664.3 jit_solution(9180067135304208064)
XLA Ops:
  7.2 0.0 copy-start
  7.2 0.0 all-gather.7.cloned.1.call-start
  7.2 2.5 convert_element_type.75
  9.7 0.0 all-gather.7.cloned.1.call-update
  9.7 0.0 copy-start.19
  9.7 0.0 copy-start.16
  9.8 0.0 all-gather.5.cloned.1.call-start
  9.8 0.0 copy-done
  9.8 1.3 bitcast_convert_fusion
  11.1 0.0 all-gather.5.cloned.1.call-update
  11.9 0.1 broadcast_in_dim.40
  12.0 0.6 reshape_tile.3.frequency_ref
  12.6 0.0 copy-done.19
  12.6 0.6 convert_element_type.73
  13.2 0.0 copy-done.16
  13.2 0.1 tile.8
  13.3 0.6 concatenate.6.bias_ref
  13.9 0.0 copy-done.11
  13.9 1.1 broadcast_select_fusion.cot_ref
  15.1 204.9 %forward.1 = (bf16[8,256,2048]{2,1,0:T(8,128)(2,1)}, bf16[3,2048,256]{2,1,0:T(8,128)(2,1)}, bf16[256,2048]{1,0:T(8,128)(2,1)}, bf16[4,2048,64]{2,1,0:T(8,128)(2,...) custom-call(s32[1]{0:T(128)} %copy.44.length_ref, ...), custom_call_target="tpu_custom_call" | custom-call | flops 219999993856 | tf_op jit(solution)/shard_map/forward/pallas_call | solution.py:553
  220.0 0.0 all-gather.7.cloned.1.call-done
  220.0 0.0 all-gather.5.cloned.1.call-done
  220.0 168.3 %mlp.1 = (bf16[8,256,704]{2,1,0:T(8,128)(2,1)}, f32[256,2048]{1,0:T(8,128)}, f32[2,2048]{1,0:T(2,128)}, bf16[4,2,704,512]{3,2,1,0:T(8,128)(2,1)}, bf16[4,704,512]{2,1,0:T(8,128)(2,1)}) custom-call(bf16[256,2048]{1,0:T(8,128)(2,1)} %get-tuple-element.52.x_ref, bf16[8,256,2048]{2,1,0:T(8,128)(2,1)} %get-tuple-element.53.cots_hbm, ...), custom_call_target="tpu_custom_call" | custom-call | flops 153999998976 | tf_op jit(solution)/shard_map/mlp/pallas_call | solution.py:753
  388.3 118.6 %down_branch.1 = (bf16[256,2048]{1,0:T(8,128)(2,1)}, bf16[8,256,256]{2,1,0:T(8,128)(2,1)}, bf16[4,256,512]{2,1,0:T(8,128)(2,1)}, bf16[4,2,704,512]{3,2,1,0:T(8,128)(2,1)}, bf16[4,704,512]{2,1,0:T(8,128)(2,1)}) custom-call(bf16[8,256,704]{2,1,0:T(8,128)(2,1)} %get-tuple-element.55.hidden_ref, bf16[4,704,512]{2,1,0:T(8,128)(2,1)} %bitcast.83, ...), custom_call_target="tpu_custom_call" | custom-call | flops 126500003840 | tf_op jit(solution)/shard_map/down_branch/pallas_call | solution.py:819
  506.9 0.0 copy-start.18
  507.0 108.1 %backward.1 = (f32[256,2048]{1,0:T(8,128)}, f32[2,2048]{1,0:T(2,128)}, f32[1,768]{1,0:T(1,128)}, bf16[4,3,512,256]{3,2,1,0:T(8,128)(2,1)}, bf16[4,256,512]{2,1,0:T(8,128)(2,1)}) custom-call(s32[1]{0:T(128)} %copy.44.length_ref, bf16[4,2048,64]{2,1,0:T(8,128)(2,1)} %get-tuple-element.62.q_ref, bf16[4,2048,64]{2,1,0:T(8,128)(2,1)} %get-tuple-element.63.k_ref, ...), custom_call_target="tpu_custom_call" | custom-call | flops 137500000256 | tf_op jit(solution)/shard_map/backward/pallas_call | solution.py:998
  615.1 0.0 copy-done.18
  615.1 1.4 pad_maximum_fusion
  616.5 14.4 %total_over_all.1 = (f32[8,4,256]{2,1,0:T(4,128)}, f32[1,768]{1,0:T(1,128)}) custom-call(f32[8,4,256]{2,1,0:T(4,128)} %bitcast.79, f32[1,768]{1,0:T(1,128)} %get-tuple-element.81.bias_ref), custom_call_target="tpu_custom_call" | custom-call | flops 13200000000 | tf_op jit(solution)/shard_map/total_over_all/pallas_call | solution.py:1069
  630.9 0.7 reduce
  631.5 0.1 reshape.140
  631.6 0.0 copy-done.13
  631.6 0.0 copy-done.14
  631.6 0.0 copy-done.15
  631.6 0.0 copy-start.6
  631.6 1.6 multiply_subtract_fusion.3
  633.2 3.3 multiply_subtract_fusion.2
  636.5 0.0 copy-done.6
  636.5 0.0 copy-done.2
  636.5 0.0 copy-start.8
  636.5 0.0 copy-start.9
  636.5 0.0 slice-start
  636.5 5.0 multiply_subtract_fusion.1
  641.5 0.0 copy-done.10
  641.5 0.0 copy-done.3
  641.5 0.0 copy-done.8
  641.5 0.0 copy-done.9
  641.5 0.0 copy-start.1
  641.6 0.0 slice-start.1
  641.6 0.0 copy-start.4
  641.6 0.0 copy-start.5
  641.6 3.3 multiply_subtract_fusion
  644.9 0.0 slice-done
  644.9 0.0 copy-done.1
  644.9 1.2 slice-done.1
  646.1 0.9 copy-done.4
  647.0 0.8 copy-done.5
  647.8 6.4 fusion.10
  654.2 0.0 copy-done.17
  654.2 0.0 copy-done.20
  654.2 0.0 copy-done.21
  654.2 0.7 multiply_subtract_fusion.4
  654.9 1.0 copy.45
  655.9 1.3 copy.46
  (22 shorter events, 0.1 us)
Async XLA Ops:
  7.2 2.6 copy-start
  7.2 212.8 %all-gather.7.cloned.1.call-start = ((), (), s32[]{:S(2)}) async-start(), calls=%async_computation.1 | async-start | bytes 3604480 | tf_op jit(solution)/shard_map/all_gather | solution.py:1119
  9.7 2.9 copy-start.19
  9.7 3.5 copy-start.16
  9.8 210.2 %all-gather.5.cloned.1.call-start = ((), (), s32[]{:S(2)}) async-start(), calls=%async_computation | async-start | bytes 7208960 | tf_op jit(solution)/shard_map/all_gather | solution.py:1118
  11.1 2.8 copy-start.11
  506.9 108.1 %copy-start.18 = (f32[2,2048]{1,0:T(2,128)S(1)}, f32[2,2048]{1,0:T(2,128)}, u32[]{:S(2)}) copy-start(f32[2,2048]{1,0:T(2,128)} %get-tuple-element.80) | copy-start | bytes 49156
  616.4 15.2 %copy-start.13 = (f32[4,2048]{1,0:T(4,128)S(1)}, f32[4,2048]{1,0:T(4,128)}, u32[]{:S(2)}) copy-start(f32[4,2048]{1,0:T(4,128)} %norm_ref.5) | copy-start | bytes 98308
  616.4 15.2 %copy-start.14 = (f32[4,2048]{1,0:T(4,128)S(1)}, f32[4,2048]{1,0:T(4,128)}, u32[]{:S(2)}) copy-start(f32[4,2048]{1,0:T(4,128)} %param.37) | copy-start | bytes 98308
  616.4 15.2 %copy-start.15 = (f32[4,2048]{1,0:T(4,128)S(1)}, f32[4,2048]{1,0:T(4,128)}, u32[]{:S(2)}) copy-start(f32[4,2048]{1,0:T(4,128)} %param.43) | copy-start | bytes 98308
  616.4 25.1 %copy-start.10 = (f32[3,512,256]{2,1,0:T(8,128)S(1)}, f32[3,512,256]{2,1,0:T(8,128)}, u32[]{:S(2)}) copy-start(f32[3,512,256]{2,1,0:T(8,128)} %param.38) | copy-start | bytes 4718596
  631.6 4.9 copy-start.6
  633.2 3.3 copy-start.2
  636.5 5.0 copy-start.3
  636.5 5.0 copy-start.8
  636.5 5.0 copy-start.9
  636.5 8.4 %slice-start = ((s8[5767168]{0:T(1024)(128)(4,1)}), s8[4194304]{0:T(1024)(128)(4,1)S(1)}, s32[]{:S(2)}) async-start(s8[5767168]{0:T(1024)(128)(4,1)} %bitcast.76), calls=%async_computation.2 | async-start | bytes 8388608
  641.5 3.4 copy-start.1
  641.6 4.5 slice-start.1
  641.6 5.4 copy-start.4
  641.6 6.2 copy-start.5
  647.8 6.4 copy-start.17
  647.8 6.4 copy-start.20
  647.8 6.4 copy-start.21
  647.8 7.1 %copy-start.12 = (bf16[256,2048]{1,0:T(8,128)(2,1)S(1)}, bf16[256,2048]{1,0:T(8,128)(2,1)}, u32[]{:S(2)}) copy-start(bf16[256,2048]{1,0:T(8,128)(2,1)} %get-tuple-element.122) | copy-start | bytes 3145732
  654.2 1.7 copy-start.7
Sparse Core Ops, SparseCore 0:
  10.4 82.1 all-gather.6
  95.1 65.8 all-gather.4

commit v6 on v5

--- a/solution.py
+++ b/solution.py
@@ -55,10 +55,6 @@
     )
 
 
-def sum_parts(parts):
-    return sum(parts[i].astype(jnp.float32) for i in range(parts.shape[0]))
-
-
 def adamw(weight_old, first_old, second_old, gradient, step_rate, decay_part):
     first_new = beta_one * first_old + (1.0 - beta_one) * gradient
     second_new = beta_two * second_old + (1.0 - beta_two) * gradient * gradient
@@ -357,9 +353,11 @@
     pl.semaphore_wait(barrier, group_count + jnp.minimum(chip, 1) + jnp.minimum(n - 1 - chip, 1))
 
 
-def forward_kernel(n, group_count, pieces, length_ref, place_ref, frequency_ref, x_ref, norm_ref, qkv_ref, out_ref, bias_ref, cot_ref,
-                   xs_ref, wq_ref, wo_ref, q_ref, k_ref, v_ref, kt_ref, mixed_ref, lse_ref, keep_ref, ahead_ref, behind_ref,
-                   middle_ref, normed_ref, cots_ref,
+def forward_kernel(n, group_count, pieces, length_ref, place_ref, frequency_ref, x_ref, norm_ref, qkv_ref, out_ref, bias_ref, cot_ref, wide_hbm, down_hbm,
+                   xs_out, wq_out, wo_ref, q_out, k_out, v_out, kt_out, mixed_ref, lse_ref, keep_out, ahead_out, behind_out,
+                   middle_ref, normed_ref, cots_ref, wide_copy, down_copy,
+                   xs_ref, wq_ref, q_ref, k_ref, v_ref, kt_ref, keep_ref, ahead_ref, behind_ref, keep_sems,
+                   wide_stage, low_stage, stage_sems, weight_send, weight_recv,
                    vt_ref, biases_ref, acc_ref, side_out, side_in, line_in, side_sems, line_send, line_recv,
                    first_sems, cot_sems, share_send, share_recv):
     greet_all(n, group_count)
@@ -404,6 +402,41 @@
     for kind in range(3):
         for i in range(group_count):
             pl.when(i != group)(lambda: share(kind, kinds[kind], group, i).start())
+
+    half_units = wide_stage.shape[0]
+    units = wide_hbm.shape[1]
+    chunks = [(wide_hbm.at[c], wide_copy.at[group, c], u) for c in range(2) for u in range(0, units, half_units)]
+    chunks += [(down_hbm, down_copy.at[group], u) for u in range(0, units, half_units)]
+
+    def chunk_in(index):
+        src, _, u = chunks[index]
+        return pltpu.make_async_copy(src.at[pl.ds(u, half_units)], wide_stage, stage_sems.at[0])
+
+    def chunk_out(index):
+        _, dst, u = chunks[index]
+        return pltpu.make_async_copy(low_stage, dst.at[pl.ds(u, half_units)], stage_sems.at[1])
+
+    chunk_in(0).start()
+    for index in range(len(chunks)):
+        chunk_in(index).wait()
+        if index > 0:
+            chunk_out(index - 1).wait()
+        low_stage[...] = wide_stage[...].astype(jnp.bfloat16)
+        if index + 1 < len(chunks):
+            chunk_in(index + 1).start()
+        chunk_out(index).start()
+    chunk_out(len(chunks) - 1).wait()
+
+    def weight(kind, peer, slot):
+        ref = (wide_copy, down_copy)[kind]
+        return pltpu.make_async_remote_copy(
+            src_ref=ref.at[group], dst_ref=ref.at[slot], send_sem=weight_send.at[kind, peer],
+            recv_sem=weight_recv.at[kind, slot], device_id={"dp": peer}, device_id_type=MESH)
+
+    def weights(body):
+        for kind in range(2):
+            for i in range(group_count):
+                pl.when(i != group)(lambda: body(kind, i))
 
     def tables(i, _):
         at = pl.ds(pl.multiple_of(i * block, block), block)
@@ -461,7 +494,16 @@
         bias = bias + biases_ref[i]
     biases_ref[group_count] = bias
 
+    weights(lambda kind, i: weight(kind, i, group).start())
     lax.fori_loop(0, n, ring, 0)
+    kept = [
+        pltpu.make_async_copy(src, dst, keep_sems.at[index])
+        for index, (src, dst) in enumerate((
+            (xs_ref, xs_out), (wq_ref, wq_out), (q_ref, q_out), (k_ref, k_out), (v_ref, v_out), (kt_ref, kt_out),
+            (keep_ref, keep_out), (ahead_ref, ahead_out), (behind_ref, behind_out)))
+    ]
+    for item in kept:
+        item.start()
     cots.start()
     cots_ref[t] = cot_ref[...]
     pair = 2 * block
@@ -536,9 +578,13 @@
     for kind in range(3):
         for i in range(group_count):
             pl.when(i != group)(lambda: share(kind, kinds[kind], group, i).wait_send())
-
-
-def forward(lengths, positions, x, norms, qkv, out, bias, cot, n, group_count, number, pieces=4):
+    for item in kept:
+        item.wait()
+    weights(lambda kind, i: weight(kind, i, i).wait_recv())
+    weights(lambda kind, i: weight(kind, i, group).wait_send())
+
+
+def forward(lengths, positions, x, norms, qkv, out, bias, cot, wide, down, n, group_count, number, pieces=4):
     rows, features = x.shape
     width = qkv.shape[2]
     heads = width // HEAD_DIM
@@ -554,9 +600,16 @@
         functools.partial(forward_kernel, n, group_count, pieces),
         out_shape=(gathered, shape((3, features, width), low), shape((width, features), low), split, split, split,
                    shape((width, total_rows), low), shape((total_rows, width), low), shape((heads, total_rows), f32),
-                   table, table, table, shape((rows, features), f32), shape((rows, features), low), gathered),
-        in_specs=[pl.BlockSpec(memory_space=pltpu.SMEM)] + [VM] * 8, out_specs=(VM,) * 15,
+                   table, table, table, shape((rows, features), f32), shape((rows, features), low), gathered,
+                   shape((group_count,) + wide.shape, low), shape((group_count,) + down.shape, low)),
+        in_specs=[pl.BlockSpec(memory_space=pltpu.SMEM)] + [VM] * 8 + [ANYWHERE] * 2,
+        out_specs=(ANYWHERE, ANYWHERE, VM) + (ANYWHERE,) * 4 + (VM, VM) + (ANYWHERE,) * 3 + (VM,) * 3 + (ANYWHERE,) * 2,
         scratch_shapes=[
+            pltpu.VMEM(item.shape, item.dtype)
+            for item in (gathered, shape((3, features, width), low), split, split, split, shape((width, total_rows), low), table, table, table)
+        ] + [
+            pltpu.SemaphoreType.DMA((9,)), pltpu.VMEM((down.shape[0] // 2, down.shape[1]), f32), pltpu.VMEM((down.shape[0] // 2, down.shape[1]), low),
+            pltpu.SemaphoreType.DMA((2,)), pltpu.SemaphoreType.DMA((2, group_count)), pltpu.SemaphoreType.DMA((2, group_count)),
             pltpu.VMEM((width, total_rows), low), pltpu.VMEM((group_count + 1, 8, width), f32), pltpu.VMEM((rows, features), f32),
         ] + scatter_scratch(n, pieces, rows, features) + [
             pltpu.SemaphoreType.DMA((5, n * pieces)), pltpu.SemaphoreType.DMA((5, n * pieces)),
@@ -564,7 +617,7 @@
         ],
         compiler_params=params(number), cost_estimate=lasting(200), name="forward",
     )(lengths, positions.astype(f32).reshape(1, total_rows), jnp.tile(frequency, LANES // half_rot).reshape(1, LANES),
-      x, norms, qkv, out, bias, cot)
+      x, norms, qkv, out, bias, cot, wide, down)
 
 
 def mlp_kernel(n, pieces, x_ref, cots_hbm, gate_up_hbm, down_hbm, middle_hbm, norm_ref,
@@ -825,13 +878,97 @@
         compiler_params=params(number), cost_estimate=lasting(115), name="down_branch")(hidden, down, middle, x, out, mixed, wide, narrow)
 
 
+def greet_everyone(count, group_count):
+    t, g = lax.axis_index("tensor"), lax.axis_index("dp")
+    barrier = pltpu.get_barrier_semaphore()
+    for j in range(count):
+        pl.when(j != t)(lambda: pl.semaphore_signal(barrier, inc=1, device_id={"tensor": j}, device_id_type=MESH))
+    for i in range(group_count):
+        pl.when(i != g)(lambda: pl.semaphore_signal(barrier, inc=1, device_id={"dp": i}, device_id_type=MESH))
+    pl.semaphore_wait(barrier, count + group_count - 2)
+
+
+class Totals:
+    def __init__(self, sums, total, parts, groups, biases, near_send, near_recv, far_send, far_recv):
+        self.sums, self.total, self.parts, self.groups, self.biases = sums, total, parts, groups, biases
+        self.near_send, self.near_recv, self.far_send, self.far_recv = near_send, near_recv, far_send, far_recv
+        self.t, self.g = lax.axis_index("tensor"), lax.axis_index("dp")
+        self.count, self.group_count = parts.shape[0], groups.shape[0]
+        self.piece = parts.shape[2]
+
+    def columns(self, ref, j):
+        return ref.at[:, pl.ds(pl.multiple_of(j * self.piece, self.piece), self.piece)]
+
+    def near(self, kind, src, dst, peer, slot):
+        return pltpu.make_async_remote_copy(
+            src_ref=src, dst_ref=dst, send_sem=self.near_send.at[kind, peer], recv_sem=self.near_recv.at[kind, slot],
+            device_id={"tensor": peer}, device_id_type=MESH)
+
+    def far(self, kind, ref, peer, slot):
+        return pltpu.make_async_remote_copy(
+            src_ref=ref.at[self.g], dst_ref=ref.at[slot], send_sem=self.far_send.at[kind, peer], recv_sem=self.far_recv.at[kind, slot],
+            device_id={"dp": peer}, device_id_type=MESH)
+
+    def first(self, peer, slot):
+        return self.near(0, self.columns(self.sums, peer), self.parts.at[slot], peer, slot)
+
+    def last(self, peer, slot):
+        return self.near(1, self.columns(self.total, self.t), self.columns(self.total, slot), peer, slot)
+
+    def each_near(self, body):
+        for j in range(self.count):
+            pl.when(j != self.t)(lambda: body(j))
+
+    def each_far(self, body):
+        for i in range(self.group_count):
+            pl.when(i != self.g)(lambda: body(i))
+
+    def start_bias(self, bias):
+        self.biases[self.g] = bias[...]
+        self.each_far(lambda i: self.far(1, self.biases, i, self.g).start())
+
+    def run(self, bias_total):
+        def added(ref):
+            total = ref[0]
+            for j in range(1, ref.shape[0]):
+                total = total + ref[j]
+            return total
+
+        here = pl.ds(pl.multiple_of(self.t * self.piece, self.piece), self.piece)
+        self.each_near(lambda j: self.first(j, self.t).start())
+        self.parts[self.t] = self.sums[:, here]
+        self.each_near(lambda j: self.first(j, j).wait_recv())
+        self.groups[self.g] = added(self.parts)
+        self.each_far(lambda i: self.far(0, self.groups, i, self.g).start())
+        self.each_far(lambda i: self.far(1, self.biases, i, i).wait_recv())
+        bias_total[...] = added(self.biases)
+        self.each_far(lambda i: self.far(0, self.groups, i, i).wait_recv())
+        self.total[:, here] = added(self.groups)
+        self.each_near(lambda j: self.last(j, self.t).start())
+        self.each_near(lambda j: self.last(j, j).wait_recv())
+
+    def finish(self):
+        self.each_near(lambda j: self.first(j, self.t).wait_send())
+        self.each_far(lambda i: self.far(0, self.groups, i, self.g).wait_send())
+        self.each_far(lambda i: self.far(1, self.biases, i, self.g).wait_send())
+        self.each_near(lambda j: self.last(j, self.t).wait_send())
+
+
 def backward_kernel(n, pieces, length_ref, q_ref, k_ref, v_ref, kt_ref, o_ref, lse_ref, do_ref,
-                    keep_ref, ahead_ref, behind_ref, w_ref, x_ref, middle_ref, norm_ref, xs_hbm, low_ref,
-                    result_ref, sums_ref, bias_ref, wide_parts, low_parts,
-                    dos_ref, delta_ref, dqt_ref, dk_ref, dv_ref, grad_ref, wide_ref, strips_ref, acc_ref, side_out, side_in, line_in,
-                    strip_sems, side_sems, line_send, line_recv, local_sems, share_send, share_recv):
+                    keep_hbm, ahead_hbm, behind_hbm, w_hbm, x_hbm, middle_hbm, norm_ref, sums_two_ref, xs_hbm, low_ref,
+                    result_ref, total_ref, bias_total_ref, wide_parts, low_parts,
+                    keep_ref, ahead_ref, behind_ref, w_ref, x_ref, middle_ref, late_sems,
+                    dos_ref, delta_ref, dqt_ref, dk_ref, dv_ref, grad_ref, wide_ref, strips_ref, acc_ref, sums_ref, bias_ref, pieces_ref, groups_ref, biases_ref, side_out, side_in, line_in,
+                    strip_sems, side_sems, line_send, line_recv, local_sems, share_send, share_recv, near_send, near_recv, far_send, far_recv):
     group_count = low_ref.shape[0]
-    greet_all(n, group_count)
+    late = [
+        pltpu.make_async_copy(src, dst, late_sems.at[index])
+        for index, (src, dst) in enumerate((
+            (keep_hbm, keep_ref), (ahead_hbm, ahead_ref), (behind_hbm, behind_ref), (w_hbm, w_ref), (x_hbm, x_ref), (middle_hbm, middle_ref)))
+    ]
+    for item in late:
+        item.start()
+    greet_everyone(2 * n, group_count)
     heads, tokens, _ = q_ref.shape
     width = heads * HEAD_DIM
     rows, features = x_ref.shape
@@ -854,7 +991,9 @@
     for slot in range(2):
         strip_copy(slot, slot).start()
     bias_ref[...] = jnp.zeros(bias_ref.shape, jnp.float32)
-    sums_ref[...] = jnp.zeros(sums_ref.shape, jnp.float32)
+    sums_ref[0:2, :] = jnp.zeros((2, features), jnp.float32)
+    sums_ref[2:4, :] = sums_two_ref[...]
+    totals = Totals(sums_ref, total_ref, pieces_ref, groups_ref, biases_ref, near_send, near_recv, far_send, far_recv)
 
     def prepare(i, _):
         at = pl.ds(pl.multiple_of(i * pair, pair), pair)
@@ -874,6 +1013,8 @@
         return 0
 
     lax.fori_loop(0, n, prepare, 0)
+    for item in late:
+        item.wait()
 
     falling = 2 * m < n - 1
 
@@ -954,6 +1095,7 @@
         def _():
             lax.fori_loop(0, strip_count, strip_gradient, 0)
             grads.start((1,))
+            totals.start_bias(bias_ref)
 
         def one(late, _):
             turn = jnp.where(late == 1, j - 2, j)
@@ -980,11 +1122,13 @@
         sums_ref[1:2, :] += shift
 
     s.settle(acc_ref, consume)
+    totals.run(bias_total_ref)
     s.finish()
     grads.finish()
-
-
-def backward(lengths, q, k, v, kt, o, lse, grad, keep, ahead, behind, w, x, grad_middle, norms, xs, narrow, n, number, pieces=4):
+    totals.finish()
+
+
+def backward(lengths, q, k, v, kt, o, lse, grad, keep, ahead, behind, w, x, grad_middle, norms, sums_two, xs, narrow, n, number, pieces=4):
     rows, features = x.shape
     heads, tokens, _ = q.shape
     width = heads * HEAD_DIM
@@ -994,91 +1138,86 @@
     shape = jax.ShapeDtypeStruct
     wide = (group_count, 3, depth, width)
     strip = min(256, depth)
+    dma = pltpu.SemaphoreType.DMA
     scatter = scatter_scratch(n, pieces, rows, features)
     return pl.pallas_call(functools.partial(backward_kernel, n, pieces),
-        out_shape=(shape((rows, features), f32), shape((2, features), f32), shape((1, 3 * width), f32),
+        out_shape=(shape((rows, features), f32), shape((4, features), f32), shape((1, 3 * width), f32),
                    shape(wide, low), shape(narrow.shape, low)),
-        in_specs=[pl.BlockSpec(memory_space=pltpu.SMEM)] + [VM] * 14 + [ANYWHERE] * 2,
+        in_specs=[pl.BlockSpec(memory_space=pltpu.SMEM)] + [VM] * 7 + [ANYWHERE] * 6 + [VM] * 2 + [ANYWHERE] * 2,
         out_specs=(VM,) * 3 + (ANYWHERE,) * 2,
-        scratch_shapes=[
+        scratch_shapes=[pltpu.VMEM(item.shape, item.dtype) for item in (keep, ahead, behind, w, x, grad_middle)] + [
+            dma((6,)),
             pltpu.VMEM((heads, tokens, HEAD_DIM), low), pltpu.VMEM((heads, tokens), f32), pltpu.VMEM((width, tokens), f32),
             pltpu.VMEM((heads, tokens, HEAD_DIM), f32), pltpu.VMEM((heads, tokens, HEAD_DIM), f32),
             pltpu.VMEM((tokens, 3 * width), low), pltpu.VMEM(wide, low), pltpu.VMEM((2, 2 * n, rows, strip), low),
-            pltpu.VMEM((rows, features), f32),
-        ] + scatter[:3] + [pltpu.SemaphoreType.DMA((2,))] + scatter[3:] + exchange_scratch(2, group_count),
+            pltpu.VMEM((rows, features), f32), pltpu.VMEM((4, features), f32), pltpu.VMEM((1, 3 * width), f32),
+            pltpu.VMEM((2 * n, 4, features // (2 * n)), f32), pltpu.VMEM((group_count, 4, features // (2 * n)), f32),
+            pltpu.VMEM((group_count, 1, 3 * width), f32),
+        ] + scatter[:3] + [pltpu.SemaphoreType.DMA((2,))] + scatter[3:] + exchange_scratch(2, group_count)
+        + [dma((2, 2 * n)), dma((2, 2 * n)), dma((2, group_count)), dma((2, group_count))],
         compiler_params=params(number), cost_estimate=lasting(125), name="backward",
-    )(lengths, q, k, v, kt, o, lse, grad, keep, ahead, behind, w, x, grad_middle, norms, xs, narrow)
-
-
-def total_kernel(x_ref, bias_ref, out_ref, bias_out_ref, parts, groups, biases, send_one, recv_one, send_two, recv_two, send_three, recv_three, send_bias, recv_bias):
-    t, g = lax.axis_index("tensor"), lax.axis_index("dp")
-    count, group_count = parts.shape[0], groups.shape[0]
-    barrier = pltpu.get_barrier_semaphore()
-    for j in range(count):
-        pl.when(j != t)(lambda: pl.semaphore_signal(barrier, inc=1, device_id={"tensor": j}, device_id_type=MESH))
-    for i in range(group_count):
-        pl.when(i != g)(lambda: pl.semaphore_signal(barrier, inc=1, device_id={"dp": i}, device_id_type=MESH))
-    pl.semaphore_wait(barrier, count + group_count - 2)
-
-    def spread(src, dst, send, recv, at, axis, peer):
-        return pltpu.make_async_remote_copy(
-            src_ref=src, dst_ref=dst, send_sem=send.at[peer], recv_sem=recv.at[at], device_id={axis: peer}, device_id_type=MESH)
-
-    def exchange(me, size, make, stay):
-        for j in range(size):
-            pl.when(j != me)(lambda: make(j, me).start())
-        stay()
-        for j in range(size):
-            pl.when(j != me)(lambda: make(j, j).wait_recv())
-        for j in range(size):
-            pl.when(j != me)(lambda: make(j, me).wait_send())
-
-    def keep_one():
-        parts[t] = x_ref[t]
-
-    biases[g] = bias_ref[...]
-    for i in range(group_count):
-        pl.when(i != g)(lambda: spread(biases.at[g], biases.at[g], send_bias, recv_bias, g, "dp", i).start())
-
-    def keep_two():
-        groups[g] = sum_of(parts)
-
-    def sum_of(ref):
-        total = ref[0]
-        for j in range(1, ref.shape[0]):
-            total = total + ref[j]
-        return total
-
-    exchange(t, count, lambda j, at: spread(x_ref.at[j], parts.at[at], send_one, recv_one, at, "tensor", j), keep_one)
-    keep_two()
-    exchange(g, group_count, lambda j, at: spread(groups.at[g], groups.at[at], send_two, recv_two, at, "dp", j), lambda: None)
-    out_ref[t] = sum_of(groups)
-    for i in range(group_count):
-        pl.when(i != g)(lambda: spread(biases.at[g], biases.at[i], send_bias, recv_bias, i, "dp", i).wait_recv())
-    bias_out_ref[...] = sum_of(biases)
-    for i in range(group_count):
-        pl.when(i != g)(lambda: spread(biases.at[g], biases.at[g], send_bias, recv_bias, g, "dp", i).wait_send())
-    exchange(t, count, lambda j, at: spread(out_ref.at[t], out_ref.at[at], send_three, recv_three, at, "tensor", j), lambda: None)
-
-
-def total_over_all(x, bias, count, group_count, number):
-    rows, width = x.shape
-    piece = width // count
-    shape = jax.ShapeDtypeStruct((count, rows, piece), x.dtype)
-    bias_shape = jax.ShapeDtypeStruct(bias.shape, bias.dtype)
-    out, bias_out = pl.pallas_call(
-        total_kernel, out_shape=(shape, bias_shape), in_specs=[VM] * 2, out_specs=(VM,) * 2,
-        scratch_shapes=[
-            pltpu.VMEM((count, rows, piece), x.dtype), pltpu.VMEM((group_count, rows, piece), x.dtype),
-            pltpu.VMEM((group_count,) + bias.shape, bias.dtype),
-            pltpu.SemaphoreType.DMA((count,)), pltpu.SemaphoreType.DMA((count,)),
-            pltpu.SemaphoreType.DMA((group_count,)), pltpu.SemaphoreType.DMA((group_count,)),
-            pltpu.SemaphoreType.DMA((count,)), pltpu.SemaphoreType.DMA((count,)),
-            pltpu.SemaphoreType.DMA((group_count,)), pltpu.SemaphoreType.DMA((group_count,)),
-        ],
-        compiler_params=params(number), cost_estimate=lasting(12), name="total_over_all",
-    )(jnp.transpose(x.reshape(rows, count, piece), (1, 0, 2)), bias)
-    return jnp.transpose(out, (1, 0, 2)).reshape(rows, width), bias_out
+    )(lengths, q, k, v, kt, o, lse, grad, keep, ahead, behind, w, x, grad_middle, norms, sums_two, xs, narrow)
+
+
+def update_kernel(rates, *refs):
+    kinds = len(rates)
+    ins, outs, refs = refs[:4 * kinds], refs[4 * kinds:7 * kinds], refs[7 * kinds:]
+    holds, held_parts, refs = refs[:kinds], refs[kinds:2 * kinds], refs[2 * kinds:]
+    load_sems, part_sems, store_sems = refs
+
+    def load(kind, i):
+        return pltpu.make_async_copy(ins[4 * kind + i], holds[kind].at[i], load_sems.at[kind, i])
+
+    def load_parts(kind):
+        return pltpu.make_async_copy(ins[4 * kind + 3], held_parts[kind], part_sems.at[kind])
+
+    def store(kind, i):
+        return pltpu.make_async_copy(holds[kind].at[i], outs[3 * kind + i], store_sems.at[kind, i])
+
+    for kind in range(kinds):
+        for i in range(3):
+            load(kind, i).start()
+        load_parts(kind).start()
+    for kind in range(kinds):
+        for i in range(3):
+            load(kind, i).wait()
+        load_parts(kind).wait()
+        hold, part = holds[kind], held_parts[kind]
+        step = min(32, hold.shape[1])
+
+        def one(i, _):
+            at = pl.ds(pl.multiple_of(i * step, step), step)
+            gradient = part[0, at, :].astype(jnp.float32)
+            for owner in range(1, part.shape[0]):
+                gradient = gradient + part[owner, at, :].astype(jnp.float32)
+            new = adamw(hold[0, at, :], hold[1, at, :], hold[2, at, :], gradient, *rates[kind])
+            for index in range(3):
+                hold[index, at, :] = new[index]
+            return 0
+
+        lax.fori_loop(0, hold.shape[1] // step, one, 0)
+        for i in range(3):
+            store(kind, i).start()
+    for kind in range(kinds):
+        for i in range(3):
+            store(kind, i).wait()
+
+
+def update(params_in, rates):
+    f32 = jnp.float32
+    kinds = len(rates)
+    dma = pltpu.SemaphoreType.DMA
+    flat = [array for group in params_in for array in group]
+    results = pl.pallas_call(
+        functools.partial(update_kernel, rates),
+        out_shape=tuple(jax.ShapeDtypeStruct(group[0].shape, f32) for group in params_in for _ in range(3)),
+        in_specs=[ANYWHERE] * len(flat), out_specs=(ANYWHERE,) * (3 * kinds),
+        scratch_shapes=[pltpu.VMEM((3,) + group[0].shape, f32) for group in params_in]
+        + [pltpu.VMEM(group[3].shape, group[3].dtype) for group in params_in]
+        + [dma((kinds, 3)), dma((kinds,)), dma((kinds, 3))],
+        compiler_params=pltpu.CompilerParams(vmem_limit_bytes=VMEM_LIMIT), cost_estimate=lasting(20), name="update",
+    )(*flat)
+    return tuple(results[3 * i:3 * i + 3] for i in range(kinds))
 
 
 def local(
@@ -1114,10 +1253,6 @@
     width_here = heads_here * HEAD_DIM
     own_start = lax.axis_index("tensor") * local_tokens
     chips = tensor_count // 2
-    gate_up_copy, down_copy = (
-        lax.all_gather(jnp.swapaxes(gate_up_master, 1, 2).astype(jnp.bfloat16), "dp", axis=0, tiled=False),
-        lax.all_gather(down_master.astype(jnp.bfloat16), "dp", axis=0, tiled=False),
-    )
     group = lax.axis_index("dp")
     group_count = lax.axis_size("dp")
     group_index = own_start + jnp.arange(local_tokens, dtype=jnp.int32)
@@ -1132,9 +1267,10 @@
     bias_row = jnp.concatenate([bias_row, jnp.zeros((5, width_here), jnp.float32)], axis=0)
     (
         gathered_one, qkv_copy, out_copy, queries, keys, values, keys_flipped, mixed_low, log_totals,
-        keep, ahead, behind, middle, normed_two, gathered_grad,
+        keep, ahead, behind, middle, normed_two, gathered_grad, gate_up_copy, down_copy,
     ) = forward(
-        lengths, positions, inputs, norm_master, qkv_master, out_master, bias_row, grad_low, chips, group_count, 0
+        lengths, positions, inputs, norm_master, qkv_master, out_master, bias_row, grad_low,
+        jnp.swapaxes(gate_up_master, 1, 2), down_master, chips, group_count, 0
     )
     hidden, grad_middle, sums_two, grad_gate_up_w, grad_down = mlp(
         normed_two, gathered_grad, gate_up_copy, down_copy, middle, norm_master, chips, 2
@@ -1143,35 +1279,39 @@
         hidden, down_copy, middle, grad_middle, out_copy, mixed_low, grad_gate_up_w, grad_down, chips, 3
     )
     grad_mixed = grad_mixed.reshape(group_tokens, width_here)
-    input_grad, sums_one, grad_bias, qkv_parts, out_parts = backward(
+    input_grad, norm_grads, bias_grad, qkv_parts, out_parts = backward(
         lengths, queries, keys, values, keys_flipped, mixed_low, log_totals, grad_mixed, keep, ahead, behind,
-        qkv_copy, inputs, grad_middle, norm_master, gathered_one, grad_out_w, chips, 4
+        qkv_copy, inputs, grad_middle, norm_master, sums_two, gathered_one, grad_out_w, chips, 4
     )
-    gate_up_grad, down_grad, out_grad = sum_parts(gate_up_parts), sum_parts(down_parts), sum_parts(out_parts)
-    qkv_grad = sum_parts(qkv_parts)
-    norm_grads, bias_grad = total_over_all(
-        jnp.concatenate([sums_one, sums_two], axis=0), grad_bias, tensor_count, group_count, 5
+
+    def level(array):
+        return array.reshape(-1, array.shape[-1])
+
+    def level_parts(array):
+        return array.reshape(group_count, -1, array.shape[-1])
+
+    def turned(array):
+        return level(jnp.swapaxes(array, 1, 2))
+
+    gate_up_new, down_new, out_new, qkv_new = update(
+        (
+            (turned(gate_up_master), turned(gate_up_first), turned(gate_up_second), level_parts(gate_up_parts)),
+            (down_master, down_first, down_second, down_parts),
+            (out_master, out_first, out_second, out_parts),
+            (level(qkv_master), level(qkv_first), level(qkv_second), level_parts(qkv_parts)),
+        ),
+        (
+            (2.0 / math.sqrt(D), decay_rate),
+            (6.0 / math.sqrt(FF), decay_rate),
+            (16.0 / math.sqrt(HEADS * HEAD_DIM), decay_rate),
+            (2.0 / math.sqrt(D), decay_rate),
+        ),
     )
+    turned_shape = (2, gate_up_master.shape[2], gate_up_master.shape[1])
+    gate_up_new = tuple(jnp.swapaxes(item.reshape(turned_shape), 1, 2) for item in gate_up_new)
+    qkv_new = tuple(item.reshape(qkv_master.shape) for item in qkv_new)
     bias_grad = lax.dynamic_slice_in_dim(
         bias_grad.reshape(3, heads_here, HEAD_DIM), group * bias_master.shape[2], bias_master.shape[2], axis=2
-    )
-    qkv_new = adamw(qkv_master, qkv_first, qkv_second, qkv_grad, 2.0 / math.sqrt(D), decay_rate)
-    gate_up_new = tuple(
-        jnp.swapaxes(item, 1, 2)
-        for item in adamw(
-            jnp.swapaxes(gate_up_master, 1, 2),
-            jnp.swapaxes(gate_up_first, 1, 2),
-            jnp.swapaxes(gate_up_second, 1, 2),
-            gate_up_grad,
-            2.0 / math.sqrt(D),
-            decay_rate,
-        )
-    )
-    out_new = adamw(
-        out_master, out_first, out_second, out_grad, 16.0 / math.sqrt(HEADS * HEAD_DIM), decay_rate
-    )
-    down_new = adamw(
-        down_master, down_first, down_second, down_grad, 6.0 / math.sqrt(FF), decay_rate
     )
     bias_new = adamw(bias_master, bias_first, bias_second, bias_grad, 1.5, 0.0)
     norm_new = adamw(norm_master, norm_first, norm_second, norm_grads, 0.7, 0.0)

time: 671 us -> 628 us (0.936)
  other arithmetic: 27.8 us -> 6.5 us
  between operations: 15.3 us -> 1.89 us
  Pallas kernels: 614 us -> 607 us
    sub x5 -> x2, other arithmetic: 13.9 us -> 2.14 us  [adamw(): weight_old - step_rate * (update + decay_part * weight_old)]
    pallas_call x1, Pallas kernels: 205 us -> 194 us  [forward(): pl.pallas_call(functools.partial(forward_kernel, n, group_count, pieces),...]
    pallas_call x1, Pallas kernels: 108 us -> 115 us  [backward(): pl.pallas_call(functools.partial(backward_kernel, n, pieces), out_shape=(...]
  transfers between devices with their start and end apart: 2 -> 0, of which waited for: 0 -> 0; matrix products, arithmetic and copies ran while one was open for 1% -> 0% of each run, Pallas kernels for 31% -> 0%
where the time goes in v6:
time: 628 us; the launch traced here: 621 us
  Pallas kernels  607 us (97%)
  other arithmetic  6.5 us (1%)
    pallas_call x1, Pallas kernels, forward(): pl.pallas_call(functools.partial(forward_kernel, n, group_count, pieces),...  194 us
    pallas_call x1, Pallas kernels, mlp(): pl.pallas_call(functools.partial(mlp_kernel, n, pieces), out_shape=(shape...  167 us
    pallas_call x1, Pallas kernels, backward(): pl.pallas_call(functools.partial(backward_kernel, n, pieces), out_shape=(...  115 us
    pallas_call x1, Pallas kernels, down_branch(): pl.pallas_call(functools.partial(down_kernel, n, pieces), out_shape=(jax....  114 us
    pallas_call x1, Pallas kernels, update(): pl.pallas_call(functools.partial(update_kernel, rates), out_shape=tuple((...  17.3 us

profile of v6, /device:TPU:0, one launch (start us, length us, event | category | flops | bytes accessed | tf_op | source)
XLA Modules:
  0.0 620.8 jit_solution(9910791591315858655)
XLA Ops:
  1.4 0.1 broadcast_in_dim.40
  1.5 0.6 reshape_tile.3.frequency_ref
  2.1 1.3 convert_element_type.3
  3.4 0.7 tile.7
  4.1 0.1 tile.8
  4.2 0.6 concatenate.3.bias_ref
  4.8 2.3 broadcast_select_fusion.cot_ref
  7.1 193.8 %forward.1 = (bf16[8,256,2048]{2,1,0:T(8,128)(2,1)}, bf16[3,2048,256]{2,1,0:T(8,128)(2,1)}, bf16[256,2048]{1,0:T(8,128)(2,1)}, bf16[4,2048,64]{2,1,0:T(8,128)(2,...) custom-call(s32[1]{0:T(128)} %copy.44.length_ref, ...), custom_call_target="tpu_custom_call" | custom-call | flops 219999993856 | tf_op jit(solution)/shard_map/forward/pallas_call | solution.py:599
  200.9 166.5 %mlp.1 = (bf16[8,256,704]{2,1,0:T(8,128)(2,1)}, f32[256,2048]{1,0:T(8,128)}, f32[2,2048]{1,0:T(2,128)}, bf16[4,2,704,512]{3,2,1,0:T(8,128)(2,1)}, bf16[4,704,512]{2,1,0:T(8,128)(2,1)}) custom-call(bf16[256,2048]{1,0:T(8,128)(2,1)} %get-tuple-element.64.x_ref, bf16[8,256,2048]{2,1,0:T(8,128)(2,1)} %get-tuple-element.65.cots_hbm, ...), custom_call_target="tpu_custom_call" | custom-call | flops 153999998976 | tf_op jit(solution)/shard_map/mlp/pallas_call | solution.py:806
  367.5 114.3 %down_branch.1 = (bf16[256,2048]{1,0:T(8,128)(2,1)}, bf16[8,256,256]{2,1,0:T(8,128)(2,1)}, bf16[4,256,512]{2,1,0:T(8,128)(2,1)}, bf16[4,2,704,512]{3,2,1,0:T(8,128)(2,1)}, bf16[4,704,512]{2,1,0:T(8,128)(2,1)}) custom-call(bf16[8,256,704]{2,1,0:T(8,128)(2,1)} %get-tuple-element.69.hidden_ref, bf16[4,704,512]{2,1,0:T(8,128)(2,1)} %get-tuple-element.67.down_hbm.down_ref, ...), custom_call_target="tpu_custom_call" | custom-call | flops 126500003840 | tf_op jit(solution)/shard_map/down_branch/pallas_call | solution.py:872
  481.8 0.0 copy-start.5
  481.8 0.0 copy-start.6
  481.8 0.0 copy-start.7
  481.9 0.0 copy-start.2
  481.9 0.0 copy-start.3
  481.9 0.0 copy-start.4
  481.9 115.0 %backward.1 = (f32[256,2048]{1,0:T(8,128)}, f32[4,2048]{1,0:T(4,128)}, f32[1,768]{1,0:T(1,128)}, bf16[4,3,512,256]{3,2,1,0:T(8,128)(2,1)}, bf16[4,256,512]{2,1,0:T(8,128)(2,1)}) custom-call(s32[1]{0:T(128)} %copy.44.length_ref, bf16[4,2048,64]{2,1,0:T(8,128)(2,1)} %get-tuple-element.76.q_ref, bf16[4,2048,64]{2,1,0:T(8,128)(2,1)} %get-tuple-element.77.k_ref, ...), custom_call_target="tpu_custom_call" | custom-call | flops 137500000256 | tf_op jit(solution)/shard_map/backward/pallas_call | solution.py:1143
  596.9 0.7 reduce
  597.6 0.1 reshape.161
  597.6 0.0 copy-done.5
  597.6 0.0 copy-done.6
  597.6 0.0 copy-done.7
  597.6 0.7 multiply_subtract_fusion.1
  598.3 0.0 copy-done.2
  598.3 0.0 copy-done.3
  598.3 0.0 copy-done.4
  598.4 1.4 multiply_subtract_fusion
  599.8 0.0 copy-start.1
  599.8 17.3 %update.1 = (f32[1408,512]{1,0:T(8,128)}, f32[1408,512]{1,0:T(8,128)}, f32[1408,512]{1,0:T(8,128)}, f32[704,512]{1,0:T(8,128)}, f32[704,512]{1,0:T(8,128)}, /*in...) custom-call(f32[1408,512]{1,0:T(8,128)} %bitcast.32, ...), custom_call_target="tpu_custom_call" | custom-call | flops 22000001024 | tf_op jit(solution)/shard_map/update/pallas_call | solution.py:1211
  617.1 0.0 copy-start
  617.1 0.0 copy-done.1
  617.1 1.0 copy.45
  618.1 1.0 copy-done
  619.0 1.3 copy.46
  (6 shorter events, 0.1 us)
Async XLA Ops:
  481.8 115.8 %copy-start.5 = (f32[3,4,16]{2,1,0:T(4,128)S(1)}, f32[3,4,16]{2,1,0:T(4,128)}, u32[]{:S(2)}) copy-start(f32[3,4,16]{2,1,0:T(4,128)} %param.30) | copy-start | bytes 2308
  481.8 115.8 %copy-start.6 = (f32[3,4,16]{2,1,0:T(4,128)S(1)}, f32[3,4,16]{2,1,0:T(4,128)}, u32[]{:S(2)}) copy-start(f32[3,4,16]{2,1,0:T(4,128)} %param.36) | copy-start | bytes 2308
  481.8 115.8 %copy-start.7 = (f32[3,4,16]{2,1,0:T(4,128)S(1)}, f32[3,4,16]{2,1,0:T(4,128)}, u32[]{:S(2)}) copy-start(f32[3,4,16]{2,1,0:T(4,128)} %param.42) | copy-start | bytes 2308
  481.9 116.5 %copy-start.2 = (f32[4,2048]{1,0:T(4,128)S(1)}, f32[4,2048]{1,0:T(4,128)}, u32[]{:S(2)}) copy-start(f32[4,2048]{1,0:T(4,128)} %norm_ref.5) | copy-start | bytes 98308
  481.9 116.5 %copy-start.3 = (f32[4,2048]{1,0:T(4,128)S(1)}, f32[4,2048]{1,0:T(4,128)}, u32[]{:S(2)}) copy-start(f32[4,2048]{1,0:T(4,128)} %param.37) | copy-start | bytes 98308
  481.9 116.5 %copy-start.4 = (f32[4,2048]{1,0:T(4,128)S(1)}, f32[4,2048]{1,0:T(4,128)}, u32[]{:S(2)}) copy-start(f32[4,2048]{1,0:T(4,128)} %param.43) | copy-start | bytes 98308
  599.8 17.3 %copy-start.1 = (bf16[256,2048]{1,0:T(8,128)(2,1)S(1)}, bf16[256,2048]{1,0:T(8,128)(2,1)}, u32[]{:S(2)}) copy-start(bf16[256,2048]{1,0:T(8,128)(2,1)} %get-tuple-element.134) | copy-start | bytes 3145732
  617.1 2.0 copy-start

commit v7 on v6

--- a/solution.py
+++ b/solution.py
@@ -120,7 +120,7 @@
     below, above = m, n - 1 - m
     both = jnp.minimum(below, above)
     half = lax.div(j + 1, 2)
-    inside = m + jnp.where(lax.rem(j, 2) == 1, -half, half)
+    inside = m + jnp.where((lax.rem(j, 2) == 1) == (2 * m < n - 1), half, -half)
     outside = m + jnp.where(above > below, j - both, both - j)
     return jnp.where(j <= 2 * both, inside, outside)
 
@@ -149,12 +149,18 @@
     def to_side(self, k, p, src):
         return self.copy(src, k, p, self.core, self.side, self.side_in, self.sibling)
 
-    def start(self, which=None):
+    def start(self, which=None, inward=True, outward=True):
         m = self.m
+        low = 2 * m < self.n - 1
         for p in range(self.pieces) if which is None else which:
-            pl.when(m < self.n - 1)(lambda: self.to_up(m, p, self.own).start())
-            pl.when(m > 0)(lambda: self.to_down(m, p, self.own).start())
-            self.to_side(m, p, self.own).start()
+            if inward and outward:
+                pl.when(m < self.n - 1)(lambda: self.to_up(m, p, self.own).start())
+                pl.when(m > 0)(lambda: self.to_down(m, p, self.own).start())
+            else:
+                pl.when((m < self.n - 1) & (low == inward))(lambda: self.to_up(m, p, self.own).start())
+                pl.when((m > 0) & (low != inward))(lambda: self.to_down(m, p, self.own).start())
+            if outward:
+                self.to_side(m, p, self.own).start()
 
     def arrive(self, d, which=None):
         m = self.m
@@ -221,10 +227,13 @@
 
         lax.fori_loop(0, self.rows // self.step, one, 0)
 
+    def inner(self, k):
+        return ((k > self.m) & (self.m > 0)) | ((k < self.m) & (self.m < self.n - 1))
+
     def pass_on(self, k, own, between=None):
         m, n = self.m, self.n
         self.side(k).wait_recv()
-        inner = ((k > m) & (m > 0)) | ((k < m) & (m < n - 1))
+        inner = self.inner(k)
 
         def one(p, _):
             @pl.when(inner)
@@ -486,6 +495,7 @@
 
     for d in range(1, n - 1):
         first.arrive(d)
+    cots.start(outward=False)
     for kind in range(3):
         for i in range(group_count):
             pl.when(i != group)(lambda: share(kind, kinds[kind], i, i).wait_recv())
@@ -504,7 +514,7 @@
     ]
     for item in kept:
         item.start()
-    cots.start()
+    cots.start(inward=False)
     cots_ref[t] = cot_ref[...]
     pair = 2 * block
 
@@ -645,6 +655,7 @@
     places = [(f, min(256, hidden_units - f)) for f in range(0, hidden_units, 256)]
     early, late = tuple(range(pieces // 2)), tuple(range(pieces // 2, pieces))
     g.start(early)
+    g.start(late, outward=False)
     xs_ref[g.t] = x_ref[...]
     for load in loads:
         load.wait()
@@ -685,7 +696,7 @@
 
     def ring(d, _):
         pl.when(d > 0)(lambda: g.arrive(d, early))
-        pl.when(d == n - 2)(lambda: g.start(late))
+        pl.when(d == n - 2)(lambda: g.start(late, inward=False))
         work_at(d, 0, early)
         return 0
 
@@ -714,9 +725,13 @@
     def one(j, _):
         k = near(n - 1 - j, m, n)
         partials(k, 0)
-        pl.when(j < n - 1)(
-            lambda: halves[0].pass_on(k, acc_ref.at[0, core], lambda p: g.arrive(j + 1, (late[0] + p,))))
+
+        def send():
+            halves[0].pass_on(k, acc_ref.at[0, core], lambda p: g.arrive(j + 1, (late[0] + p,)))
+
+        pl.when((j < n - 1) & jnp.logical_not(halves[0].inner(k)))(send)
         work_at(j, 1, late)
+        pl.when((j < n - 1) & halves[0].inner(k))(send)
         return 0
 
     lax.fori_loop(0, n, one, 0)
@@ -756,14 +771,17 @@
     def two(j, _):
         k = near(n - 1 - j, m, n)
         partials(k, 1)
-        pl.when(j < n - 1)(lambda: halves[1].pass_on(k, acc_ref.at[1, core]))
+
+        def send():
+            halves[1].pass_on(k, acc_ref.at[1, core])
+
+        pl.when((j < n - 1) & jnp.logical_not(halves[1].inner(k)))(send)
         for u in range(per):
             wide_gradient(u, j)
         for index in range(len(places)):
             pl.when(j == index)(functools.partial(down_gradient, index))
+        pl.when((j < n - 1) & halves[1].inner(k))(send)
         return 0
-
-    own = acc_ref.at[0, core]
 
     def settle(h):
         def consume(at, total):
@@ -793,7 +811,7 @@
     lax.fori_loop(0, n, sent, 0)
 
 
-def mlp(x, cots, gate_up, down, middle, norms, n, number, pieces=4):
+def mlp(x, cots, gate_up, down, middle, norms, n, number, pieces=8):
     rows, width = x.shape
     group_count, hidden, depth = down.shape
     half, part = rows // 2, pieces // 2
@@ -848,8 +866,6 @@
     def consume(at, total):
         block_ref[at, :] = (middle_ref[at, :] + total).astype(jnp.bfloat16)
 
-    s.settle(acc_ref, consume)
-
     def last(k, _):
         g.side_wait(k)
         for c in range(2):
@@ -861,12 +877,14 @@
     for a in range(0, width, cut):
         grad_out_ref[a // depth, :, a % depth:a % depth + cut] = dot_nn(
             flipped, xs_ref[:, :, a:a + cut].reshape(mixed_ref.shape[0], cut)).astype(jnp.bfloat16)
+    s.settle(acc_ref, consume)
+
     g.finish()
     s.finish()
     grads.finish()
 
 
-def down_branch(hidden, down, middle, x, out, mixed, wide, narrow, n, number, pieces=4):
+def down_branch(hidden, down, middle, x, out, mixed, wide, narrow, n, number, pieces=8):
     rows, width = x.shape
     f32, low = jnp.float32, jnp.bfloat16
     return pl.pallas_call(functools.partial(down_kernel, n, pieces),

time: 628 us -> 611 us (0.973)
  Pallas kernels: 607 us -> 590 us
    pallas_call x1, Pallas kernels: 167 us -> 154 us  [mlp(): pl.pallas_call(functools.partial(mlp_kernel, n, pieces), out_shape=(shape...]
    pallas_call x1, Pallas kernels: 194 us -> 185 us  [forward(): pl.pallas_call(functools.partial(forward_kernel, n, group_count, pieces),...]
where the time goes in v7:
time: 611 us; the launch traced here: 604 us
  Pallas kernels  590 us (97%)
  other arithmetic  6.5 us (1%)
    pallas_call x1, Pallas kernels, forward(): pl.pallas_call(functools.partial(forward_kernel, n, group_count, pieces),...  185 us
    pallas_call x1, Pallas kernels, mlp(): pl.pallas_call(functools.partial(mlp_kernel, n, pieces), out_shape=(shape...  154 us
    pallas_call x1, Pallas kernels, down_branch(): pl.pallas_call(functools.partial(down_kernel, n, pieces), out_shape=(jax....  120 us
    pallas_call x1, Pallas kernels, backward(): pl.pallas_call(functools.partial(backward_kernel, n, pieces), out_shape=(...  113 us
    pallas_call x1, Pallas kernels, update(): pl.pallas_call(functools.partial(update_kernel, rates), out_shape=tuple((...  17.3 us

profile of v7, /device:TPU:0, one launch (start us, length us, event | category | flops | bytes accessed | tf_op | source)
XLA Modules:
  0.0 603.6 jit_solution(3878983559918985172)
XLA Ops:
  1.4 0.1 broadcast_in_dim.40
  1.5 0.6 reshape_tile.3.frequency_ref
  2.1 1.3 convert_element_type.3
  3.4 0.7 tile.7
  4.1 0.1 tile.8
  4.2 0.6 concatenate.3.bias_ref
  4.8 2.3 broadcast_select_fusion.cot_ref
  7.1 185.1 %forward.1 = (bf16[8,256,2048]{2,1,0:T(8,128)(2,1)}, bf16[3,2048,256]{2,1,0:T(8,128)(2,1)}, bf16[256,2048]{1,0:T(8,128)(2,1)}, bf16[4,2048,64]{2,1,0:T(8,128)(2,...) custom-call(s32[1]{0:T(128)} %copy.44.length_ref, ...), custom_call_target="tpu_custom_call" | custom-call | flops 219999993856 | tf_op jit(solution)/shard_map/forward/pallas_call | solution.py:609
  192.3 153.9 %mlp.1 = (bf16[8,256,704]{2,1,0:T(8,128)(2,1)}, f32[256,2048]{1,0:T(8,128)}, f32[2,2048]{1,0:T(2,128)}, bf16[4,2,704,512]{3,2,1,0:T(8,128)(2,1)}, bf16[4,704,512]{2,1,0:T(8,128)(2,1)}) custom-call(bf16[256,2048]{1,0:T(8,128)(2,1)} %get-tuple-element.64.x_ref, bf16[8,256,2048]{2,1,0:T(8,128)(2,1)} %get-tuple-element.65.cots_hbm, ...), custom_call_target="tpu_custom_call" | custom-call | flops 153999998976 | tf_op jit(solution)/shard_map/mlp/pallas_call | solution.py:824
  346.1 120.0 %down_branch.1 = (bf16[256,2048]{1,0:T(8,128)(2,1)}, bf16[8,256,256]{2,1,0:T(8,128)(2,1)}, bf16[4,256,512]{2,1,0:T(8,128)(2,1)}, bf16[4,2,704,512]{3,2,1,0:T(8,128)(2,1)}, bf16[4,704,512]{2,1,0:T(8,128)(2,1)}) custom-call(bf16[8,256,704]{2,1,0:T(8,128)(2,1)} %get-tuple-element.69.hidden_ref, bf16[4,704,512]{2,1,0:T(8,128)(2,1)} %get-tuple-element.67.down_hbm.down_ref, ...), custom_call_target="tpu_custom_call" | custom-call | flops 126500003840 | tf_op jit(solution)/shard_map/down_branch/pallas_call | solution.py:890
  466.2 0.0 copy-start.5
  466.2 0.0 copy-start.6
  466.2 0.0 copy-start.7
  466.2 0.0 copy-start.2
  466.2 0.0 copy-start.3
  466.2 0.0 copy-start.4
  466.2 113.4 %backward.1 = (f32[256,2048]{1,0:T(8,128)}, f32[4,2048]{1,0:T(4,128)}, f32[1,768]{1,0:T(1,128)}, bf16[4,3,512,256]{3,2,1,0:T(8,128)(2,1)}, bf16[4,256,512]{2,1,0:T(8,128)(2,1)}) custom-call(s32[1]{0:T(128)} %copy.44.length_ref, bf16[4,2048,64]{2,1,0:T(8,128)(2,1)} %get-tuple-element.76.q_ref, bf16[4,2048,64]{2,1,0:T(8,128)(2,1)} %get-tuple-element.77.k_ref, ...), custom_call_target="tpu_custom_call" | custom-call | flops 137500000256 | tf_op jit(solution)/shard_map/backward/pallas_call | solution.py:1161
  579.6 0.7 reduce
  580.3 0.1 reshape.161
  580.4 0.0 copy-done.5
  580.4 0.0 copy-done.6
  580.4 0.0 copy-done.7
  580.4 0.7 multiply_subtract_fusion.1
  581.1 0.0 copy-done.2
  581.1 0.0 copy-done.3
  581.1 0.0 copy-done.4
  581.1 1.4 multiply_subtract_fusion
  582.6 0.0 copy-start.1
  582.6 17.3 %update.1 = (f32[1408,512]{1,0:T(8,128)}, f32[1408,512]{1,0:T(8,128)}, f32[1408,512]{1,0:T(8,128)}, f32[704,512]{1,0:T(8,128)}, f32[704,512]{1,0:T(8,128)}, /*in...) custom-call(f32[1408,512]{1,0:T(8,128)} %bitcast.32, ...), custom_call_target="tpu_custom_call" | custom-call | flops 22000001024 | tf_op jit(solution)/shard_map/update/pallas_call | solution.py:1229
  599.8 0.0 copy-start
  599.9 0.0 copy-done.1
  599.9 1.0 copy.45
  600.8 1.0 copy-done
  601.8 1.3 copy.46
  (6 shorter events, 0.1 us)
Async XLA Ops:
  466.2 114.2 %copy-start.5 = (f32[3,4,16]{2,1,0:T(4,128)S(1)}, f32[3,4,16]{2,1,0:T(4,128)}, u32[]{:S(2)}) copy-start(f32[3,4,16]{2,1,0:T(4,128)} %param.30) | copy-start | bytes 2308
  466.2 114.2 %copy-start.6 = (f32[3,4,16]{2,1,0:T(4,128)S(1)}, f32[3,4,16]{2,1,0:T(4,128)}, u32[]{:S(2)}) copy-start(f32[3,4,16]{2,1,0:T(4,128)} %param.36) | copy-start | bytes 2308
  466.2 114.2 %copy-start.7 = (f32[3,4,16]{2,1,0:T(4,128)S(1)}, f32[3,4,16]{2,1,0:T(4,128)}, u32[]{:S(2)}) copy-start(f32[3,4,16]{2,1,0:T(4,128)} %param.42) | copy-start | bytes 2308
  466.2 114.9 %copy-start.2 = (f32[4,2048]{1,0:T(4,128)S(1)}, f32[4,2048]{1,0:T(4,128)}, u32[]{:S(2)}) copy-start(f32[4,2048]{1,0:T(4,128)} %norm_ref.5) | copy-start | bytes 98308
  466.2 114.9 %copy-start.3 = (f32[4,2048]{1,0:T(4,128)S(1)}, f32[4,2048]{1,0:T(4,128)}, u32[]{:S(2)}) copy-start(f32[4,2048]{1,0:T(4,128)} %param.37) | copy-start | bytes 98308
  466.2 114.9 %copy-start.4 = (f32[4,2048]{1,0:T(4,128)S(1)}, f32[4,2048]{1,0:T(4,128)}, u32[]{:S(2)}) copy-start(f32[4,2048]{1,0:T(4,128)} %param.43) | copy-start | bytes 98308
  582.6 17.3 %copy-start.1 = (bf16[256,2048]{1,0:T(8,128)(2,1)S(1)}, bf16[256,2048]{1,0:T(8,128)(2,1)}, u32[]{:S(2)}) copy-start(bf16[256,2048]{1,0:T(8,128)(2,1)} %get-tuple-element.134) | copy-start | bytes 3145732
  599.8 2.0 copy-start

commit v8 on v7

--- a/solution.py
+++ b/solution.py
@@ -3,6 +3,7 @@
 
 import jax
 import jax.numpy as jnp
+import numpy as np
 from jax import lax
 from jax.experimental import pallas as pl
 from jax.experimental.pallas import tpu as pltpu
@@ -364,8 +365,8 @@
 
 def forward_kernel(n, group_count, pieces, length_ref, place_ref, frequency_ref, x_ref, norm_ref, qkv_ref, out_ref, bias_ref, cot_ref, wide_hbm, down_hbm,
                    xs_out, wq_out, wo_ref, q_out, k_out, v_out, kt_out, mixed_ref, lse_ref, keep_out, ahead_out, behind_out,
-                   middle_ref, normed_ref, cots_ref, wide_copy, down_copy,
-                   xs_ref, wq_ref, q_ref, k_ref, v_ref, kt_ref, keep_ref, ahead_ref, behind_ref, keep_sems,
+                   middle_ref, normed_ref, cots_out, wide_copy, down_copy,
+                   cots_ref, xs_ref, wq_ref, q_ref, k_ref, v_ref, kt_ref, keep_ref, ahead_ref, behind_ref, keep_sems,
                    wide_stage, low_stage, stage_sems, weight_send, weight_recv,
                    vt_ref, biases_ref, acc_ref, side_out, side_in, line_in, side_sems, line_send, line_recv,
                    first_sems, cot_sems, share_send, share_recv):
@@ -380,7 +381,7 @@
     group = lax.axis_index("dp")
     t, core, m = place()
     first = Gather(n, xs_ref.at[t], xs_ref, first_sems, pieces)
-    cots = Gather(n, cot_ref, cots_ref, cot_sems, pieces)
+    cots = Gather(n, cots_ref.at[t], cots_ref, cot_sems, pieces)
     s = Scatter(n, pieces, side_out, side_in, line_in, side_sems, line_send, line_recv)
     step = 32
 
@@ -391,6 +392,15 @@
 
     lax.fori_loop(0, rows // step, first_norm, 0)
     first.start()
+
+    def mask(i, _):
+        start = pl.multiple_of(i * step, step)
+        at = pl.ds(start, step)
+        slots = t * rows + start + lax.broadcasted_iota(jnp.int32, (step, features), 0)
+        cots_ref[t, at, :] = jnp.where(slots < length, cot_ref[at, :].astype(jnp.float32), 0.0).astype(jnp.bfloat16)
+        return 0
+
+    lax.fori_loop(0, rows // step, mask, 0)
     depth = features // group_count
     mine = pl.ds(pl.multiple_of(group * depth, depth), depth)
     for c in range(3):
@@ -449,7 +459,7 @@
 
     def tables(i, _):
         at = pl.ds(pl.multiple_of(i * block, block), block)
-        angles = jnp.broadcast_to(place_ref[:, at], (LANES, block)).T * frequency_ref[...]
+        angles = jnp.broadcast_to(place_ref[:, at].astype(jnp.float32), (LANES, block)).T * frequency_ref[...]
         cosine, sine = jnp.cos(angles), jnp.sin(angles)
         dim = lax.rem(lax.broadcasted_iota(jnp.int32, (block, LANES), 1), HEAD_DIM)
         none = jnp.zeros((block, LANES), jnp.float32)
@@ -515,7 +525,6 @@
     for item in kept:
         item.start()
     cots.start(inward=False)
-    cots_ref[t] = cot_ref[...]
     pair = 2 * block
 
     def attend(i):
@@ -579,9 +588,11 @@
         middle_ref[at, :] = middle
         normed_ref[at, :] = norm_forward(middle, norm_ref[2:3, :], norm_ref[3:4, :]).astype(jnp.bfloat16)
 
-    s.settle(acc_ref, consume)
     for k in range(n):
         cots.side_wait(k)
+    kept.append(pltpu.make_async_copy(cots_ref, cots_out, keep_sems.at[len(kept)]))
+    kept[-1].start()
+    s.settle(acc_ref, consume)
     first.finish()
     cots.finish()
     s.finish()
@@ -602,7 +613,7 @@
     f32, low = jnp.float32, jnp.bfloat16
     shape = jax.ShapeDtypeStruct
     half_rot = ROTARY // 2
-    frequency = rope_base ** (-(2.0 * jnp.arange(half_rot, dtype=jnp.float32)) / ROTARY)
+    frequency = np.tile(rope_base ** (-(2.0 * np.arange(half_rot)) / ROTARY), LANES // half_rot)
     split = shape((heads, total_rows, HEAD_DIM), low)
     table = shape((total_rows, LANES), f32)
     gathered = shape((2 * n, rows, features), low)
@@ -613,12 +624,12 @@
                    table, table, table, shape((rows, features), f32), shape((rows, features), low), gathered,
                    shape((group_count,) + wide.shape, low), shape((group_count,) + down.shape, low)),
         in_specs=[pl.BlockSpec(memory_space=pltpu.SMEM)] + [VM] * 8 + [ANYWHERE] * 2,
-        out_specs=(ANYWHERE, ANYWHERE, VM) + (ANYWHERE,) * 4 + (VM, VM) + (ANYWHERE,) * 3 + (VM,) * 3 + (ANYWHERE,) * 2,
+        out_specs=(ANYWHERE, ANYWHERE, VM) + (ANYWHERE,) * 4 + (VM, VM) + (ANYWHERE,) * 3 + (VM,) * 2 + (ANYWHERE,) * 3,
         scratch_shapes=[
             pltpu.VMEM(item.shape, item.dtype)
-            for item in (gathered, shape((3, features, width), low), split, split, split, shape((width, total_rows), low), table, table, table)
+            for item in (gathered, gathered, shape((3, features, width), low), split, split, split, shape((width, total_rows), low), table, table, table)
         ] + [
-            pltpu.SemaphoreType.DMA((9,)), pltpu.VMEM((down.shape[0] // 2, down.shape[1]), f32), pltpu.VMEM((down.shape[0] // 2, down.shape[1]), low),
+            pltpu.SemaphoreType.DMA((10,)), pltpu.VMEM((down.shape[0] // 2, down.shape[1]), f32), pltpu.VMEM((down.shape[0] // 2, down.shape[1]), low),
             pltpu.SemaphoreType.DMA((2,)), pltpu.SemaphoreType.DMA((2, group_count)), pltpu.SemaphoreType.DMA((2, group_count)),
             pltpu.VMEM((width, total_rows), low), pltpu.VMEM((group_count + 1, 8, width), f32), pltpu.VMEM((rows, features), f32),
         ] + scatter_scratch(n, pieces, rows, features) + [
@@ -626,7 +637,7 @@
             pltpu.SemaphoreType.DMA((3, group_count)), pltpu.SemaphoreType.DMA((3, group_count)),
         ],
         compiler_params=params(number), cost_estimate=lasting(200), name="forward",
-    )(lengths, positions.astype(f32).reshape(1, total_rows), jnp.tile(frequency, LANES // half_rot).reshape(1, LANES),
+    )(lengths, positions.reshape(1, total_rows), jnp.asarray(frequency.reshape(1, LANES), f32),
       x, norms, qkv, out, bias, cot, wide, down)
 
 
@@ -836,8 +847,8 @@
         compiler_params=params(number), cost_estimate=lasting(140), name="mlp")(x, cots, gate_up, down, middle, norms)
 
 
-def down_kernel(n, pieces, hidden_ref, down_ref, middle_ref, grad_ref, out_ref, mixed_ref, wide_ref, low_ref, block_ref, back_ref, grad_out_ref, wide_parts, low_parts,
-                local_sems, share_send, share_recv, xs_ref, x_ref, acc_ref, side_out, side_in, line_in, side_sems, line_send, line_recv, gather_sems):
+def down_kernel(n, pieces, hidden_ref, down_ref, middle_hbm, grad_ref, out_hbm, mixed_hbm, wide_ref, low_ref, block_ref, back_ref, grad_out_ref, wide_parts, low_parts,
+                middle_ref, out_ref, mixed_ref, late_sems, local_sems, share_send, share_recv, xs_ref, x_ref, acc_ref, side_out, side_in, line_in, side_sems, line_send, line_recv, gather_sems):
     group_count, _, depth = down_ref.shape
     greet_all(n, group_count)
     grads = Exchange(group_count, ((wide_ref, wide_parts), (low_ref, low_parts)), local_sems, share_send, share_recv)
@@ -846,6 +857,12 @@
     x_ref[...] = grad_ref[...].astype(jnp.bfloat16)
     g.start()
     grads.start()
+    late = [
+        pltpu.make_async_copy(src, dst, late_sems.at[index])
+        for index, (src, dst) in enumerate(((middle_hbm, middle_ref), (out_hbm, out_ref), (mixed_hbm, mixed_ref)))
+    ]
+    for item in late:
+        item.start()
     xs_ref[g.t] = x_ref[...]
     m, core = s.m, s.core
     width = group_count * depth
@@ -866,6 +883,9 @@
     def consume(at, total):
         block_ref[at, :] = (middle_ref[at, :] + total).astype(jnp.bfloat16)
 
+    for item in late:
+        item.wait()
+
     def last(k, _):
         g.side_wait(k)
         for c in range(2):
@@ -891,8 +911,8 @@
         out_shape=(jax.ShapeDtypeStruct((rows, width), low), jax.ShapeDtypeStruct((2 * n, rows, out.shape[0]), low),
                    jax.ShapeDtypeStruct((down.shape[0], out.shape[0], down.shape[2]), low),
                    jax.ShapeDtypeStruct(wide.shape, low), jax.ShapeDtypeStruct(narrow.shape, low)),
-        in_specs=[VM] * 6 + [ANYWHERE] * 2, out_specs=(VM,) * 3 + (ANYWHERE,) * 2,
-        scratch_shapes=exchange_scratch(2, down.shape[0]) + [pltpu.VMEM((2 * n, rows, width), low), pltpu.VMEM((rows, width), low), pltpu.VMEM((rows, width), f32)] + scatter_scratch(n, pieces, rows, width) + [pltpu.SemaphoreType.DMA((5, n * pieces))],
+        in_specs=[VM, VM, ANYWHERE, VM] + [ANYWHERE] * 4, out_specs=(VM,) * 3 + (ANYWHERE,) * 2,
+        scratch_shapes=[pltpu.VMEM(item.shape, item.dtype) for item in (middle, out, mixed)] + [pltpu.SemaphoreType.DMA((3,))] + exchange_scratch(2, down.shape[0]) + [pltpu.VMEM((2 * n, rows, width), low), pltpu.VMEM((rows, width), low), pltpu.VMEM((rows, width), f32)] + scatter_scratch(n, pieces, rows, width) + [pltpu.SemaphoreType.DMA((5, n * pieces))],
         compiler_params=params(number), cost_estimate=lasting(115), name="down_branch")(hidden, down, middle, x, out, mixed, wide, narrow)
 
 
@@ -1269,17 +1289,9 @@
     row_length = group_tokens // row_count
     heads_here = bias_master.shape[1]
     width_here = heads_here * HEAD_DIM
-    own_start = lax.axis_index("tensor") * local_tokens
     chips = tensor_count // 2
     group = lax.axis_index("dp")
     group_count = lax.axis_size("dp")
-    group_index = own_start + jnp.arange(local_tokens, dtype=jnp.int32)
-    row_of = group_index // row_length
-    slot_of = group_index % row_length
-    row_match = row_of[:, None] == jnp.arange(row_count, dtype=jnp.int32)[None, :]
-    length_of = jnp.sum(jnp.where(row_match, lengths[None, :], 0), axis=1)
-    valid = slot_of < length_of
-    grad_low = jnp.where(valid[:, None], cotangent, jnp.zeros_like(cotangent))
     own_dims = jnp.arange(HEAD_DIM) // (HEAD_DIM // group_count) == group
     bias_row = jnp.where(own_dims, jnp.tile(bias_master, (1, 1, group_count)), 0.0).reshape(3, width_here)
     bias_row = jnp.concatenate([bias_row, jnp.zeros((5, width_here), jnp.float32)], axis=0)
@@ -1287,7 +1299,7 @@
         gathered_one, qkv_copy, out_copy, queries, keys, values, keys_flipped, mixed_low, log_totals,
         keep, ahead, behind, middle, normed_two, gathered_grad, gate_up_copy, down_copy,
     ) = forward(
-        lengths, positions, inputs, norm_master, qkv_master, out_master, bias_row, grad_low,
+        lengths, positions, inputs, norm_master, qkv_master, out_master, bias_row, cotangent,
         jnp.swapaxes(gate_up_master, 1, 2), down_master, chips, group_count, 0
     )
     hidden, grad_middle, sums_two, grad_gate_up_w, grad_down = mlp(

time: 611 us -> 603 us (0.987)
  no operation moved by 1% of the time
where the time goes in v8:
time: 603 us; the launch traced here: 596 us
  Pallas kernels  586 us (97%)
    pallas_call x1, Pallas kernels, forward(): pl.pallas_call(functools.partial(forward_kernel, n, group_count, pieces),...  183 us
    pallas_call x1, Pallas kernels, mlp(): pl.pallas_call(functools.partial(mlp_kernel, n, pieces), out_shape=(shape...  154 us
    pallas_call x1, Pallas kernels, down_branch(): pl.pallas_call(functools.partial(down_kernel, n, pieces), out_shape=(jax....  119 us
    pallas_call x1, Pallas kernels, backward(): pl.pallas_call(functools.partial(backward_kernel, n, pieces), out_shape=(...  113 us
    pallas_call x1, Pallas kernels, update(): pl.pallas_call(functools.partial(update_kernel, rates), out_shape=tuple((...  17.3 us

profile of v8, /device:TPU:0, one launch (start us, length us, event | category | flops | bytes accessed | tf_op | source)
XLA Modules:
  0.0 595.8 jit_solution(2540262154576511869)
XLA Ops:
  1.3 0.1 broadcast_in_dim.14
  1.4 0.7 tile.4
  2.1 0.1 tile.10
  2.2 0.6 concatenate.3.bias_ref
  2.8 182.6 %forward.1 = (bf16[8,256,2048]{2,1,0:T(8,128)(2,1)}, bf16[3,2048,256]{2,1,0:T(8,128)(2,1)}, bf16[256,2048]{1,0:T(8,128)(2,1)}, bf16[4,2048,64]{2,1,0:T(8,128)(2,...) custom-call(s32[1]{0:T(128)S(6)} %copy.45.length_ref, ...), custom_call_target="tpu_custom_call" | custom-call | flops 219999993856 | tf_op jit(solution)/shard_map/forward/pallas_call | solution.py:620
  185.4 154.0 %mlp.1 = (bf16[8,256,704]{2,1,0:T(8,128)(2,1)}, f32[256,2048]{1,0:T(8,128)}, f32[2,2048]{1,0:T(2,128)}, bf16[4,2,704,512]{3,2,1,0:T(8,128)(2,1)}, bf16[4,704,512]{2,1,0:T(8,128)(2,1)}) custom-call(bf16[256,2048]{1,0:T(8,128)(2,1)} %get-tuple-element.64.x_ref, bf16[8,256,2048]{2,1,0:T(8,128)(2,1)} %get-tuple-element.65.cots_hbm, ...), custom_call_target="tpu_custom_call" | custom-call | flops 153999998976 | tf_op jit(solution)/shard_map/mlp/pallas_call | solution.py:835
  339.5 119.2 %down_branch.1 = (bf16[256,2048]{1,0:T(8,128)(2,1)}, bf16[8,256,256]{2,1,0:T(8,128)(2,1)}, bf16[4,256,512]{2,1,0:T(8,128)(2,1)}, bf16[4,2,704,512]{3,2,1,0:T(8,128)(2,1)}, bf16[4,704,512]{2,1,0:T(8,128)(2,1)}) custom-call(bf16[8,256,704]{2,1,0:T(8,128)(2,1)} %get-tuple-element.69.hidden_ref, bf16[4,704,512]{2,1,0:T(8,128)(2,1)} %get-tuple-element.67.down_hbm.down_ref, ...), custom_call_target="tpu_custom_call" | custom-call | flops 126500003840 | tf_op jit(solution)/shard_map/down_branch/pallas_call | solution.py:910
  458.7 0.0 copy-start.5
  458.7 0.0 copy-start.6
  458.7 0.0 copy-start.7
  458.7 0.0 copy-start.2
  458.7 0.0 copy-start.3
  458.7 0.0 copy-start.4
  458.7 113.1 %backward.1 = (f32[256,2048]{1,0:T(8,128)}, f32[4,2048]{1,0:T(4,128)}, f32[1,768]{1,0:T(1,128)}, bf16[4,3,512,256]{3,2,1,0:T(8,128)(2,1)}, bf16[4,256,512]{2,1,0:T(8,128)(2,1)}) custom-call(s32[1]{0:T(128)S(6)} %copy.45.length_ref, bf16[4,2048,64]{2,1,0:T(8,128)(2,1)} %get-tuple-element.76.q_ref, bf16[4,2048,64]{2,1,0:T(8,128)(2,1)} %get-tuple-element.77.k_ref, ...), custom_call_target="tpu_custom_call" | custom-call | flops 137500000256 | tf_op jit(solution)/shard_map/backward/pallas_call | solution.py:1181
  571.9 0.7 reduce
  572.5 0.1 reshape.114
  572.6 0.0 copy-done.5
  572.6 0.0 copy-done.6
  572.6 0.0 copy-done.7
  572.6 0.7 multiply_subtract_fusion.1
  573.3 0.0 copy-done.2
  573.3 0.0 copy-done.3
  573.3 0.0 copy-done.4
  573.3 1.4 multiply_subtract_fusion
  574.8 0.0 copy-start.1
  574.8 17.3 %update.1 = (f32[1408,512]{1,0:T(8,128)}, f32[1408,512]{1,0:T(8,128)}, f32[1408,512]{1,0:T(8,128)}, f32[704,512]{1,0:T(8,128)}, f32[704,512]{1,0:T(8,128)}, /*in...) custom-call(f32[1408,512]{1,0:T(8,128)} %bitcast.29, ...), custom_call_target="tpu_custom_call" | custom-call | flops 22000001024 | tf_op jit(solution)/shard_map/update/pallas_call | solution.py:1249
  592.1 0.0 copy-start
  592.1 0.0 copy-done.1
  592.1 1.0 copy.46
  593.1 1.0 copy-done
  594.0 1.3 copy.47
  (3 shorter events, 0.0 us)
Async XLA Ops:
  458.7 114.0 %copy-start.5 = (f32[3,4,16]{2,1,0:T(4,128)S(1)}, f32[3,4,16]{2,1,0:T(4,128)}, u32[]{:S(2)}) copy-start(f32[3,4,16]{2,1,0:T(4,128)} %param.31) | copy-start | bytes 2308
  458.7 114.0 %copy-start.6 = (f32[3,4,16]{2,1,0:T(4,128)S(1)}, f32[3,4,16]{2,1,0:T(4,128)}, u32[]{:S(2)}) copy-start(f32[3,4,16]{2,1,0:T(4,128)} %param.37) | copy-start | bytes 2308
  458.7 113.9 %copy-start.7 = (f32[3,4,16]{2,1,0:T(4,128)S(1)}, f32[3,4,16]{2,1,0:T(4,128)}, u32[]{:S(2)}) copy-start(f32[3,4,16]{2,1,0:T(4,128)} %param.43) | copy-start | bytes 2308
  458.7 114.6 %copy-start.2 = (f32[4,2048]{1,0:T(4,128)S(1)}, f32[4,2048]{1,0:T(4,128)}, u32[]{:S(2)}) copy-start(f32[4,2048]{1,0:T(4,128)} %norm_ref.5) | copy-start | bytes 98308
  458.7 114.6 %copy-start.3 = (f32[4,2048]{1,0:T(4,128)S(1)}, f32[4,2048]{1,0:T(4,128)}, u32[]{:S(2)}) copy-start(f32[4,2048]{1,0:T(4,128)} %param.38) | copy-start | bytes 98308
  458.7 114.6 %copy-start.4 = (f32[4,2048]{1,0:T(4,128)S(1)}, f32[4,2048]{1,0:T(4,128)}, u32[]{:S(2)}) copy-start(f32[4,2048]{1,0:T(4,128)} %param.44) | copy-start | bytes 98308
  574.8 17.3 %copy-start.1 = (bf16[256,2048]{1,0:T(8,128)(2,1)S(1)}, bf16[256,2048]{1,0:T(8,128)(2,1)}, u32[]{:S(2)}) copy-start(bf16[256,2048]{1,0:T(8,128)(2,1)} %get-tuple-element.134) | copy-start | bytes 3145732
  592.1 2.0 copy-start

commit v9 on v8

--- a/solution.py
+++ b/solution.py
@@ -1323,17 +1323,17 @@
     def turned(array):
         return level(jnp.swapaxes(array, 1, 2))
 
-    gate_up_new, down_new, out_new, qkv_new = update(
+    out_new, down_new, gate_up_new, qkv_new = update(
         (
+            (out_master, out_first, out_second, out_parts),
+            (down_master, down_first, down_second, down_parts),
             (turned(gate_up_master), turned(gate_up_first), turned(gate_up_second), level_parts(gate_up_parts)),
-            (down_master, down_first, down_second, down_parts),
-            (out_master, out_first, out_second, out_parts),
             (level(qkv_master), level(qkv_first), level(qkv_second), level_parts(qkv_parts)),
         ),
         (
+            (16.0 / math.sqrt(HEADS * HEAD_DIM), decay_rate),
+            (6.0 / math.sqrt(FF), decay_rate),
             (2.0 / math.sqrt(D), decay_rate),
-            (6.0 / math.sqrt(FF), decay_rate),
-            (16.0 / math.sqrt(HEADS * HEAD_DIM), decay_rate),
             (2.0 / math.sqrt(D), decay_rate),
         ),
     )

time: 603 us -> 603 us (level)
  no operation moved by 1% of the time
where the time goes in v9:
time: 603 us; the launch traced here: 596 us
  Pallas kernels  587 us (97%)
    pallas_call x1, Pallas kernels, forward(): pl.pallas_call(functools.partial(forward_kernel, n, group_count, pieces),...  183 us
    pallas_call x1, Pallas kernels, mlp(): pl.pallas_call(functools.partial(mlp_kernel, n, pieces), out_shape=(shape...  154 us
    pallas_call x1, Pallas kernels, down_branch(): pl.pallas_call(functools.partial(down_kernel, n, pieces), out_shape=(jax....  119 us
    pallas_call x1, Pallas kernels, backward(): pl.pallas_call(functools.partial(backward_kernel, n, pieces), out_shape=(...  113 us
    pallas_call x1, Pallas kernels, update(): pl.pallas_call(functools.partial(update_kernel, rates), out_shape=tuple((...  17.6 us

profile of v9, /device:TPU:0, one launch (start us, length us, event | category | flops | bytes accessed | tf_op | source)
XLA Modules:
  0.0 596.2 jit_solution(10534205897175358372)
XLA Ops:
  1.3 0.1 broadcast_in_dim.14
  1.4 0.7 tile.4
  2.1 0.1 tile.10
  2.2 0.6 concatenate.3.bias_ref
  2.8 182.6 %forward.1 = (bf16[8,256,2048]{2,1,0:T(8,128)(2,1)}, bf16[3,2048,256]{2,1,0:T(8,128)(2,1)}, bf16[256,2048]{1,0:T(8,128)(2,1)}, bf16[4,2048,64]{2,1,0:T(8,128)(2,...) custom-call(s32[1]{0:T(128)S(6)} %copy.45.length_ref, ...), custom_call_target="tpu_custom_call" | custom-call | flops 219999993856 | tf_op jit(solution)/shard_map/forward/pallas_call | solution.py:620
  185.4 154.0 %mlp.1 = (bf16[8,256,704]{2,1,0:T(8,128)(2,1)}, f32[256,2048]{1,0:T(8,128)}, f32[2,2048]{1,0:T(2,128)}, bf16[4,2,704,512]{3,2,1,0:T(8,128)(2,1)}, bf16[4,704,512]{2,1,0:T(8,128)(2,1)}) custom-call(bf16[256,2048]{1,0:T(8,128)(2,1)} %get-tuple-element.64.x_ref, bf16[8,256,2048]{2,1,0:T(8,128)(2,1)} %get-tuple-element.65.cots_hbm, ...), custom_call_target="tpu_custom_call" | custom-call | flops 153999998976 | tf_op jit(solution)/shard_map/mlp/pallas_call | solution.py:835
  339.5 119.2 %down_branch.1 = (bf16[256,2048]{1,0:T(8,128)(2,1)}, bf16[8,256,256]{2,1,0:T(8,128)(2,1)}, bf16[4,256,512]{2,1,0:T(8,128)(2,1)}, bf16[4,2,704,512]{3,2,1,0:T(8,128)(2,1)}, bf16[4,704,512]{2,1,0:T(8,128)(2,1)}) custom-call(bf16[8,256,704]{2,1,0:T(8,128)(2,1)} %get-tuple-element.69.hidden_ref, bf16[4,704,512]{2,1,0:T(8,128)(2,1)} %get-tuple-element.67.down_hbm.down_ref, ...), custom_call_target="tpu_custom_call" | custom-call | flops 126500003840 | tf_op jit(solution)/shard_map/down_branch/pallas_call | solution.py:910
  458.7 0.0 copy-start.5
  458.7 0.0 copy-start.6
  458.7 0.0 copy-start.7
  458.7 0.0 copy-start.2
  458.7 0.0 copy-start.3
  458.7 0.0 copy-start.4
  458.7 113.1 %backward.1 = (f32[256,2048]{1,0:T(8,128)}, f32[4,2048]{1,0:T(4,128)}, f32[1,768]{1,0:T(1,128)}, bf16[4,3,512,256]{3,2,1,0:T(8,128)(2,1)}, bf16[4,256,512]{2,1,0:T(8,128)(2,1)}) custom-call(s32[1]{0:T(128)S(6)} %copy.45.length_ref, bf16[4,2048,64]{2,1,0:T(8,128)(2,1)} %get-tuple-element.76.q_ref, bf16[4,2048,64]{2,1,0:T(8,128)(2,1)} %get-tuple-element.77.k_ref, ...), custom_call_target="tpu_custom_call" | custom-call | flops 137500000256 | tf_op jit(solution)/shard_map/backward/pallas_call | solution.py:1181
  571.9 0.7 reduce
  572.5 0.1 reshape.114
  572.6 0.0 copy-done.5
  572.6 0.0 copy-done.6
  572.6 0.0 copy-done.7
  572.6 0.7 multiply_subtract_fusion.1
  573.3 0.0 copy-done.2
  573.3 0.0 copy-done.3
  573.3 0.0 copy-done.4
  573.3 1.4 multiply_subtract_fusion
  574.8 0.0 copy-start.1
  574.8 17.6 %update.1 = (f32[256,512]{1,0:T(8,128)}, f32[256,512]{1,0:T(8,128)}, f32[256,512]{1,0:T(8,128)}, f32[704,512]{1,0:T(8,128)}, f32[704,512]{1,0:T(8,128)}, /*index...) custom-call(f32[256,512]{1,0:T(8,128)} %refs_0_.1, ...), custom_call_target="tpu_custom_call" | custom-call | flops 22000001024 | tf_op jit(solution)/shard_map/update/pallas_call | solution.py:1249
  592.4 0.0 copy-start
  592.4 0.0 copy-done.1
  592.4 1.0 copy.46
  593.4 1.0 copy-done
  594.4 1.3 copy.47
  (3 shorter events, 0.0 us)
Async XLA Ops:
  458.7 114.0 %copy-start.5 = (f32[3,4,16]{2,1,0:T(4,128)S(1)}, f32[3,4,16]{2,1,0:T(4,128)}, u32[]{:S(2)}) copy-start(f32[3,4,16]{2,1,0:T(4,128)} %param.31) | copy-start | bytes 2308
  458.7 114.0 %copy-start.6 = (f32[3,4,16]{2,1,0:T(4,128)S(1)}, f32[3,4,16]{2,1,0:T(4,128)}, u32[]{:S(2)}) copy-start(f32[3,4,16]{2,1,0:T(4,128)} %param.37) | copy-start | bytes 2308
  458.7 113.9 %copy-start.7 = (f32[3,4,16]{2,1,0:T(4,128)S(1)}, f32[3,4,16]{2,1,0:T(4,128)}, u32[]{:S(2)}) copy-start(f32[3,4,16]{2,1,0:T(4,128)} %param.43) | copy-start | bytes 2308
  458.7 114.6 %copy-start.2 = (f32[4,2048]{1,0:T(4,128)S(1)}, f32[4,2048]{1,0:T(4,128)}, u32[]{:S(2)}) copy-start(f32[4,2048]{1,0:T(4,128)} %norm_ref.5) | copy-start | bytes 98308
  458.7 114.6 %copy-start.3 = (f32[4,2048]{1,0:T(4,128)S(1)}, f32[4,2048]{1,0:T(4,128)}, u32[]{:S(2)}) copy-start(f32[4,2048]{1,0:T(4,128)} %param.38) | copy-start | bytes 98308
  458.7 114.6 %copy-start.4 = (f32[4,2048]{1,0:T(4,128)S(1)}, f32[4,2048]{1,0:T(4,128)}, u32[]{:S(2)}) copy-start(f32[4,2048]{1,0:T(4,128)} %param.44) | copy-start | bytes 98308
  574.8 17.7 %copy-start.1 = (bf16[256,2048]{1,0:T(8,128)(2,1)S(1)}, bf16[256,2048]{1,0:T(8,128)(2,1)}, u32[]{:S(2)}) copy-start(bf16[256,2048]{1,0:T(8,128)(2,1)} %get-tuple-element.134) | copy-start | bytes 3145732
  592.4 2.0 copy-start
